TPU v7x, 256 devices: a whole 4x4x8 slice. The times are simulated.
256 devices in a mesh: freq: 8 (over y_hi, x), chan: 32 (over z, y_lo, core).
Axes of the slice: x: 4, y: 4 (y_hi: 2, y_lo: 2; y = y_hi * 2 + y_lo), z: 8, core: 2. Of those that a mesh axis runs over, the one named last changes fastest.
Arguments:
- spectra: bfloat16 [2, 128, 2048, 256], P(None, 'freq', 'chan'), may hold values from -500 to 500
Outputs:
- correlation: float32 [128, 2048, 2048], P(None, 'chan', 'freq')
All inputs are finite; a program needn't handle non-finite values.
Results may differ from a plain program's by a relative error of at most 0.0052.
Values may be sent and summed in bfloat16 or wider, within the bound.
No kernel may reach another device: no remote copies, remote signals or barrier semaphores. Data moves between devices by JAX's collectives and lax.ppermute only.
A program may use at most 128 MiB of HBM per device.

v0:
```python
import math

import jax
import jax.numpy as jnp
from jax import lax
from jax.sharding import PartitionSpec as P

LAGS = 128


def lag_table(count_f, lags):
    freqs = jnp.arange(count_f, dtype=jnp.int32)
    shifts = jnp.arange(lags, dtype=jnp.int32)
    turns = shifts[:, None] * freqs[None, :] % lags
    angle = 2.0 * math.pi / lags * turns.astype(jnp.float32)
    return jnp.stack([jnp.cos(angle), -jnp.sin(angle)], axis=1).astype(jnp.bfloat16)


def shards(spectra):
    values = spectra.astype(jnp.float32)
    power = jnp.mean(values[0] * values[0] + values[1] * values[1], axis=-1, keepdims=True)
    white = (values * lax.rsqrt(power + 1e-06)[None]).astype(jnp.bfloat16)
    rows_local = jnp.stack([white, jnp.stack([white[1], -white[0]])])
    windows = spectra.shape[3]
    gathered = lax.all_gather(white, "chan", axis=2, tiled=True)
    products = jnp.einsum(
        "qpfiw,pfjw->qfij", rows_local, gathered, preferred_element_type=jnp.float32
    )
    cross = (products * (1.0 / windows)).astype(jnp.bfloat16)
    total_freq = cross.shape[1] * lax.axis_size("freq")
    table = lag_table(total_freq, LAGS)
    factor = math.sqrt(windows / total_freq)
    moved = lax.all_to_all(cross, "freq", split_axis=3, concat_axis=1, tiled=True)
    return jnp.einsum("lpf,pfij->lij", table, moved, preferred_element_type=jnp.float32) * factor


def solution(mesh):
    return jax.shard_map(
        shards,
        mesh=mesh,
        in_specs=(P(None, "freq", "chan", None),),
        out_specs=P(None, "chan", "freq"),
        check_vma=False,
    )
```

profile of v0, /device:TPU:102, one launch (start us, length us, event | category | flops | bytes accessed | tf_op | source)
XLA Modules:
  0.0 472.8 jit_solution(4115304766162185864)
XLA Ops:
  6.5 0.0 copy-start
  6.5 0.0 all-gather.2.cloned.1.call-start
  6.5 1.5 copy_convert_fusion
  8.1 0.2 fusion.10
  8.3 2.5 multiply_convert_fusion
  10.8 0.0 all-gather.2.cloned.1.call-update
  10.9 1.3 fusion.21
  12.1 0.1 maximum_bitcast_fusion
  12.2 0.0 copy-done
  12.3 0.3 fusion.23
  12.6 185.6 %all-gather.2.cloned.1.call-done = bf16[2,16,2048,256]{3,2,0,1:T(8,128)(2,1)} async-done(((bf16[2,16,64,256]{3,2,0,1:T(8,128)(2,1)}), bf16[2,16,2048,256]{3,2,0,1:T(8,128)(2,1)}) %all-gather.2.cloned.1.call-update) | async-done | bytes 33554448 | tf_op jit(solution)/shard_map/all_gather | solution.py:25
  198.2 20.1 %fusion.3 = bf16[2,16,64,2048]{3,2,0,1:T(8,128)(2,1)} fusion(bf16[2,16,2048,256]{3,2,0,1:T(8,128)(2,1)} %all-gather.2.cloned.1.call-done, bf16[1,2,16,64,256]{4,3,1,0,2:T(8,128)(2,1)S(1)} %maximum_bitcast_fusion, bf16[1,2,16,64,256]{4,3,1,0,2:T(8,128)(2,1)S(1)} %fusion.23), kind=kOutput, calls=%fused_computation.4 | convolution fusion | flops 4307550208 | bytes 44040192 | tf_op jit(solution)/shard_map/qpfiw,pfjw->qfij/dot_general | solution.py:26
  218.3 40.1 %copy.8 = bf16[2,16,64,2048]{2,0,1,3:T(2,128)(2,1)} copy(bf16[2,16,64,2048]{3,2,0,1:T(8,128)(2,1)} %fusion.3) | data formatting | bytes 16777216 | tf_op jit(solution)/shard_map/convert_element_type | solution.py:29
  258.3 16.8 %reshape.85 = bf16[8,2,262144]{2,1,0:T(2,128)(2,1)} reshape(bf16[2048,16,2,64]{3,2,1,0:T(2,128)(2,1)} %bitcast.35) | data formatting | bytes 16777216
  275.2 7.2 %all-to-all-start = ((bf16[8,2,262144]{2,1,0:T(2,128)(2,1)}), bf16[8,2,262144]{2,1,0:T(2,128)(2,1)}, u32[]{:S(2)}, u32[]{:S(2)}) async-start(bf16[8,2,262144]{2,1,0:T(2,128)(2,1)} %reshape.85), calls=%async_computation | async-start | bytes 16777216 | tf_op jit(solution)/shard_map/all_to_all | solution.py:33
  282.4 0.3 negate_convert_fusion
  282.7 124.7 %all-to-all-done = bf16[8,2,262144]{2,1,0:T(2,128)(2,1)} async-done(((bf16[8,2,262144]{2,1,0:T(2,128)(2,1)}), bf16[8,2,262144]{2,1,0:T(2,128)(2,1)}, u32[]{:S(2)}, u32[]{:S(2)}) %all-to-all-start) | async-done | bytes 8388640 | tf_op jit(solution)/shard_map/all_to_all | solution.py:33
  407.4 16.5 %reshape.86 = bf16[2048,16,2,64]{3,2,1,0:T(2,128)(2,1)} reshape(bf16[8,2,262144]{2,1,0:T(2,128)(2,1)} %all-to-all-done) | data formatting | bytes 16777216
  423.9 29.0 %copy.9 = bf16[2,16,64,8,256]{4,1,3,0,2:T(8,128)(2,1)} copy(bf16[2,16,64,8,256]{2,0,1,4,3:T(2,128)(2,1)} %bitcast.36) | data formatting | bytes 16777216 | tf_op jit(solution)/shard_map/all_to_all | solution.py:33
  452.9 4.8 %bitcast_multiply_fusion.1 = f32[128,64,256]{2,0,1:T(8,128)S(1)} fusion(bf16[2,128,64,256]{3,1,0,2:T(8,128)(2,1)} %bitcast.37, bf16[128,1,128]{2,0,1:T(8,128)(2,1)S(1)} %get-tuple-element.7, bf16[128,1,128]{2,0,1:T(8,128)(2,1)S(1)} %get-tuple-element.8), kind=kOutput, calls=%fused_computation.5 | convolution fusion | flops 1075970048 | bytes 16842752 | tf_op jit(solution)/shard_map/lpf,pfij->lij/dot_general | solution.py:34
  457.7 8.3 %copy.10 = f32[128,64,256]{2,1,0:T(8,128)} copy(f32[128,64,256]{2,0,1:T(8,128)S(1)} %bitcast_multiply_fusion.1) | data formatting | bytes 16777216 | tf_op jit(solution)/shard_map/mul | solution.py:34
  (1 shorter events, 0.0 us)
Async XLA Ops:
  6.5 5.7 %copy-start = (bf16[2,16,64,256]{3,2,1,0:T(8,128)(2,1)S(1)}, bf16[2,16,64,256]{3,2,1,0:T(8,128)(2,1)}, u32[]{:S(2)}) copy-start(bf16[2,16,64,256]{3,2,1,0:T(8,128)(2,1)} %param.1) | copy-start | bytes 3145732
  6.5 191.6 %all-gather.2.cloned.1.call-start = ((), (), s32[]{:S(2)}) async-start(), calls=%async_computation.1 | async-start | bytes 34603008 | tf_op jit(solution)/shard_map/all_gather | solution.py:25
  275.2 132.2 %all-to-all-start = ((bf16[8,2,262144]{2,1,0:T(2,128)(2,1)}), bf16[8,2,262144]{2,1,0:T(2,128)(2,1)}, u32[]{:S(2)}, u32[]{:S(2)}) async-start(bf16[8,2,262144]{2,1,0:T(2,128)(2,1)} %reshape.85), calls=%async_computation | async-start | bytes 16777216 | tf_op jit(solution)/shard_map/all_to_all | solution.py:33
Sparse Core Ops, SparseCore 0:
  11.0 187.1 all-gather.1
where the time goes:
time: 475 us; the launch traced here: 473 us
  waiting for transfers between devices  310 us (65%)
  local copies, waits for them, and re-layouts  111 us (23%)
  matrix products  24.9 us (5%)
  between operations  13.4 us (3%)
  starting transfers between devices  7.24 us (2%)
  other arithmetic  6.22 us (1%)
    all_gather x1, waiting for transfers between devices, shards(): gathered = lax.all_gather(white, 'chan', axis=2, tiled=True)  186 us
    all_to_all x1, waiting for transfers between devices, shards(): lax.all_to_all(cross, 'freq', split_axis=3, concat_axis=1, tiled=True)  125 us
    convert_element_type x1, local copies, waits for them, and re-layouts, shards(): cross = (products * (1.0 / windows)).astype(jnp.bfloat16)  40.1 us
    unnamed x4, local copies, waits for them, and re-layouts  33.3 us
    all_to_all x1, local copies, waits for them, and re-layouts, shards(): lax.all_to_all(cross, 'freq', split_axis=3, concat_axis=1, tiled=True)  29 us
    dot_general x1, matrix products, shards(): jnp.einsum('qpfiw,pfjw->qfij', rows_local, gathered, preferred_element_ty...  20.1 us
  transfers between devices with their start and end apart: 2, of which 2 were waited for; matrix products, arithmetic and copies ran while one was open for 0% of the time, Pallas kernels for 0%

commit v1 on v0

v1 whole, which is shorter than its diff:
```python
import functools
import math

import jax
import jax.numpy as jnp
import ml_dtypes
import numpy as np
from jax import lax
from jax.experimental import pallas as pl
from jax.experimental.pallas import tpu as pltpu
from jax.sharding import Mesh, PartitionSpec as P

LAGS = 128
NF = 128
W = 256
CH = 64
X, YH, Z, YL, CO = 4, 2, 8, 2, 2
NK = YH * X
NQ = YL * CO
PLANE = ("yh", "x", "yl", "co")
VMEM = 56 * 1024 * 1024


def lag_matrix():
    out = np.zeros((LAGS, NK, NQ, 2, 2), np.float32)
    lags = np.arange(LAGS)
    step = np.float32(2.0 * math.pi / LAGS)

    def angle(f):
        return step * (lags * f % LAGS).astype(np.float32)

    for k in range(NK):
        group, side = min(k, 7 - k), int(k > 3)
        for q in range(NQ):
            for t in range(2):
                m = 2 * (side * NQ + q) + t
                if m == 0 and group == 3:
                    out[:, k, q, t, 0] = np.cos(angle(0))
                    out[:, k, q, t, 1] = np.cos(angle(64))
                else:
                    f = 16 * group + m if m else 16 * (group + 1)
                    out[:, k, q, t, 0] = np.cos(angle(f))
                    out[:, k, q, t, 1] = -np.sin(angle(f))
    return out.reshape(LAGS, NK * NQ * 4).astype(ml_dtypes.bfloat16)


def whiten_kernel(hi_ref, x_ref, sp_ref, o_ref, *, t):
    x = x_ref[:, 0].astype(jnp.float32)
    if t == 0:
        take = jnp.logical_and(hi_ref[0] == 0, pl.program_id(0) == 0)
        x = jnp.where(take, sp_ref[...].astype(jnp.float32), x)
    power = jnp.sum(x[0] * x[0] + x[1] * x[1], axis=-1, keepdims=True) * (1.0 / W)
    o_ref[0] = (x * lax.rsqrt(power + 1e-06)[None]).astype(jnp.bfloat16)


def whiten(spectra, special, hi, t):
    def source(r, hi_ref):
        m = 2 * r + t
        return (0, jnp.where(hi_ref[0] == 0, m, lax.rem(16 - m, 16)), 0, 0)

    return pl.pallas_call(
        functools.partial(whiten_kernel, t=t),
        grid_spec=pltpu.PrefetchScalarGridSpec(
            num_scalar_prefetch=1,
            grid=(8,),
            in_specs=[
                pl.BlockSpec((2, 1, CH, W), source),
                pl.BlockSpec((2, CH, W), lambda r, hi_ref: (0, 0, 0)),
            ],
            out_specs=pl.BlockSpec((1, 2, CH, W), lambda r, hi_ref: (r, 0, 0, 0)),
        ),
        out_shape=jax.ShapeDtypeStruct((8, 2, CH, W), jnp.bfloat16),
        compiler_params=pltpu.CompilerParams(vmem_limit_bytes=VMEM),
        cost_estimate=pl.CostEstimate(flops=2000000, bytes_accessed=1 << 20, transcendentals=0),
        name="whiten",
    )(hi, spectra, special)


def cross_kernel(h, has_prev, z_ref, coef_ref, y_ref, *refs):
    if has_prev:
        refs = refs[1:]
    ups, dns, out_ref, left = refs[0:4], refs[4:8], refs[8], refs[9]
    step = pl.program_id(0)

    @pl.when(step == 0)
    def _():
        for side in range(2):
            re = y_ref[side, :, 0].reshape(4 * CH, W).astype(jnp.float32)
            im = y_ref[side, :, 1].reshape(4 * CH, W).astype(jnp.float32)
            for o in range(2):
                alpha = coef_ref[o * 4 + side * 2]
                beta = coef_ref[o * 4 + side * 2 + 1]
                left[o, side, 0] = (alpha * re + beta * im).astype(jnp.bfloat16)
                left[o, side, 1] = (alpha * im - beta * re).astype(jnp.bfloat16)

    def emit(pieces):
        for o in range(2):
            acc = None
            for side in range(2):
                for p in range(2):
                    part = lax.dot_general(
                        left[o, side, p],
                        pieces(side, p),
                        (((1,), (1,)), ((), ())),
                        preferred_element_type=jnp.float32,
                    )
                    acc = part if acc is None else acc + part
            acc = (acc * (1.0 / W)).astype(jnp.bfloat16)
            out_ref[0, :, 0, o] = acc.reshape(4, CH, 128)

    def block(ref):
        return lambda side, p: ref[side, :, p].reshape(2 * CH, W)

    @pl.when(step == 0)
    def _():
        emit(lambda side, p: y_ref[side, 2 * h:2 * h + 2, p].reshape(2 * CH, W))

    for s in range(3):
        @pl.when(step == 2 * s + 1)
        def _(s=s):
            emit(block(ups[s]))

        @pl.when(step == 2 * s + 2)
        def _(s=s):
            emit(block(dns[s]))

    @pl.when(step == 7)
    def _():
        emit(lambda side, p: (ups, dns)[side][3][0, :, p].reshape(2 * CH, W))


def cross(zpos, coef, y, ups, dns, prev, h, slot, slots):

    def whole(shape):
        return pl.BlockSpec(shape, lambda s, *_: (0,) * len(shape))

    def target(s, z_ref, coef_ref):
        dist = lax.div(s + 1, 2)
        g = lax.rem(z_ref[0] + 8 + jnp.where(lax.rem(s, 2) == 1, -dist, dist), 8)
        return (g, 0, slot, 0, 0, 0)

    has_prev = prev is not None
    ins = [y] + ([prev] if has_prev else []) + list(ups) + list(dns)
    specs = [whole(y.shape)]
    if has_prev:
        specs.append(pl.BlockSpec(memory_space=pl.ANY))
    specs += [whole(b.shape) for b in list(ups) + list(dns)]
    return pl.pallas_call(
        functools.partial(cross_kernel, h, has_prev),
        grid_spec=pltpu.PrefetchScalarGridSpec(
            num_scalar_prefetch=2,
            grid=(8,),
            in_specs=specs,
            out_specs=pl.BlockSpec((1, 4, 1, 2, CH, 128), target),
            scratch_shapes=[pltpu.VMEM((2, 2, 2, 4 * CH, W), jnp.bfloat16)],
        ),
        out_shape=jax.ShapeDtypeStruct((8, 4, slots, 2, CH, 128), jnp.bfloat16),
        input_output_aliases={3: 0} if has_prev else {},
        compiler_params=pltpu.CompilerParams(vmem_limit_bytes=VMEM),
        cost_estimate=pl.CostEstimate(flops=1 << 30, bytes_accessed=7 << 19, transcendentals=0),
        name="cross",
    )(zpos, coef, *ins)


def lags_kernel(has_prev, t_ref, x_ref, *refs):
    out_ref, wide = refs[-2:]
    rows = 16
    n = NK * NQ * 4
    wide[...] = x_ref[...].reshape(n, rows, 128).astype(jnp.float32).reshape(n * rows, 128)
    out = out_ref.reshape(LAGS * rows, 128)
    for i in range(rows):
        x = wide[pl.ds(i, n, stride=rows), :].astype(jnp.bfloat16)
        y = jnp.dot(t_ref[...], x, preferred_element_type=jnp.float32)
        out[pl.ds(i, LAGS, stride=rows), :] = y * math.sqrt(W / NF)


def lags(table, moved, prev, h):
    has_prev = prev is not None
    n = NK * NQ * 4
    ins = [table, moved] + ([prev] if has_prev else [])
    specs = [
        pl.BlockSpec((LAGS, n), lambda i: (0, 0)),
        pl.BlockSpec((NK * NQ, 2, 2, 16, 128), lambda i: (0, 0, 0, i, 0)),
    ]
    if has_prev:
        specs.append(pl.BlockSpec(memory_space=pl.ANY))
    return pl.pallas_call(
        functools.partial(lags_kernel, has_prev),
        grid=(CH // 16,),
        in_specs=specs,
        out_specs=pl.BlockSpec((LAGS, 16, 128), lambda i: (0, i, h)),
        out_shape=jax.ShapeDtypeStruct((LAGS, CH, 256), jnp.float32),
        scratch_shapes=[pltpu.VMEM((n * 16, 128), jnp.float32)],
        input_output_aliases={2: 0} if has_prev else {},
        compiler_params=pltpu.CompilerParams(vmem_limit_bytes=VMEM),
        cost_estimate=pl.CostEstimate(flops=1 << 28, bytes_accessed=6 << 20, transcendentals=0),
        name="lags",
    )(*ins)


def shards(spectra):
    k = lax.axis_index("yh") * X + lax.axis_index("x")
    q = lax.axis_index("yl") * CO + lax.axis_index("co")
    hi = (k > 3).astype(jnp.int32)
    zpos = lax.axis_index("z").astype(jnp.int32).reshape(1)

    special = lax.ppermute(spectra[:, 0], ("yh", "x"), [(1, 0), (2, 1), (3, 2), (0, 3)])
    groups = [[j * NQ + i for j in (g, 7 - g) for i in range(NQ)] for g in range(4)]

    def regroup(t):
        sent = whiten(spectra, special, hi.reshape(1), t)
        got = lax.all_to_all(
            sent, PLANE, split_axis=0, concat_axis=0, tiled=True, axis_index_groups=groups
        )
        return got.reshape(2, NQ, 2, CH, W)

    sin0 = -math.sin(0.0)
    sin64 = -math.sin(math.pi)
    regular = np.array([1, 0, 1, 0, 0, 1, 0, -1], np.float32)
    selfs = np.array([1, sin0, 0, 0, 0, 0, 1, sin64], np.float32)
    is_self = jnp.logical_and(k == 3, q == 0)
    coefs = {0: jnp.where(is_self, selfs, regular), 1: jnp.asarray(regular)}

    up = [(i, (i + 1) % Z) for i in range(Z)]
    dn = [((i + 1) % Z, i) for i in range(Z)]

    def ring(chunk):
        a = b = chunk
        ups, dns = [], []
        for _ in range(3):
            a = lax.ppermute(a, "z", up)
            b = lax.ppermute(b, "z", dn)
            ups.append(a)
            dns.append(b)
        ups.append(lax.ppermute(a[0:1], "z", up))
        dns.append(lax.ppermute(b[1:2], "z", dn))
        return ups, dns

    table = jnp.asarray(lag_matrix())
    ys = {1: regroup(1), 0: regroup(0)}
    out = None
    for h in range(2):
        parts = None
        for t in (1, 0):
            ups, dns = ring(ys[t][:, 2 * h:2 * h + 2])
            parts = cross(zpos, coefs[t], ys[t], ups, dns, parts, h, t, 2)
        parts = parts.reshape(NK * NQ, 2, 2, CH, 128)
        moved = lax.all_to_all(parts, PLANE, split_axis=0, concat_axis=0, tiled=True)
        out = lags(table, moved, out, h)
    return out


def solution(mesh):
    fine = Mesh(mesh.devices.reshape(YH, X, Z, YL, CO), ("yh", "x", "z", "yl", "co"))
    return jax.shard_map(
        shards,
        mesh=fine,
        in_specs=(P(None, ("yh", "x"), ("z", "yl", "co"), None),),
        out_specs=P(None, ("z", "yl", "co"), ("yh", "x")),
        check_vma=False,
    )
```

time: 475 us -> 219 us (0.46)
  the two profiles are of different devices: /device:TPU:102 before, /device:TPU:1 now
where the time goes in v1:
time: 219 us; the launch traced here: 218 us
  waiting for transfers between devices  80.7 us (37%)
  starting transfers between devices  74.5 us (34%)
  Pallas kernels  51.7 us (24%)
  local copies, waits for them, and re-layouts  9.86 us (5%)
    ppermute x12, waiting for transfers between devices, ring(): b = lax.ppermute(b, 'z', dn)  34.3 us
    pallas_call x4, Pallas kernels, cross(): pl.pallas_call(functools.partial(cross_kernel, h, has_prev), grid_spec=pl...  29.3 us
    ppermute x12, starting transfers between devices, ring(): b = lax.ppermute(b, 'z', dn)  29.1 us
    all_to_all x2, waiting for transfers between devices, shards(): lax.all_to_all(parts, PLANE, split_axis=0, concat_axis=0, tiled=True)  24.3 us
    all_to_all x2, starting transfers between devices, shards(): lax.all_to_all(parts, PLANE, split_axis=0, concat_axis=0, tiled=True)  17.9 us
    all_to_all x2, waiting for transfers between devices, regroup(): lax.all_to_all(sent, PLANE, split_axis=0, concat_axis=0, tiled=True, axis...  13.6 us
    pallas_call x2, Pallas kernels, lags(): pl.pallas_call(functools.partial(lags_kernel, has_prev), grid=(CH // 16,)...  12.1 us
    all_to_all x2, starting transfers between devices, regroup(): lax.all_to_all(sent, PLANE, split_axis=0, concat_axis=0, tiled=True, axis...  10.5 us
  transfers between devices with their start and end apart: 37, of which 19 were waited for; matrix products, arithmetic and copies ran while one was open for 2% of the time, Pallas kernels for 15%

profile of v1, /device:TPU:1, one launch (start us, length us, event | category | flops | bytes accessed | tf_op | source)
XLA Modules:
  0.0 217.6 jit_solution(12911674138455119860)
XLA Ops:
  0.8 5.2 %collective-permute-start = (bf16[2,64,256]{2,1,0:T(8,128)(2,1)S(1)}, bf16[2,64,256]{2,1,0:T(8,128)(2,1)S(1)}, u32[]{:S(2)}, u32[]{:S(2)}) collective-permute-start(bf16[2,64,256]{2,1,0:T(8,128)(2,1)S(1)} %slice_bitcast_fusion), channel_id=1, source_target_pairs={{32,0},{64,32},{96,64},{0,96},{33,1},{65,33},{97,65},{1,97},{34,2}... | collective-permute-start | bytes 196616 | tf_op jit(solution)/shard_map/ppermute | solution.py:207
  6.1 1.3 collective-permute-done.sp_ref
  8.0 5.2 %whiten.2 = bf16[8,2,64,256]{3,2,1,0:T(8,128)(2,1)} custom-call(s32[1]{0:T(128)} %bitcast.1.hi_ref, bf16[2,16,64,256]{3,2,1,0:T(8,128)(2,1)} %x_ref.3, bf16[2,64,256]{2,1,0:T(8,128)(2,1)} %copy-done.25), custom_call_target="tpu_custom_call" | custom-call | flops 2000000 | bytes 1048576 | tf_op jit(solution)/shard_map/whiten/pallas_call | solution.py:61
  13.2 6.3 %all-to-all-start = ((bf16[8,2,64,256]{3,2,1,0:T(8,128)(2,1)}), bf16[8,2,64,256]{3,2,1,0:T(8,128)(2,1)S(1)}, u32[]{:S(2)}, u32[]{:S(2)}) async-start(bf16[8,2,64,256]{3,2,1,0:T(8,128)(2,1)} %whiten.2), calls=%async_computation | async-start | bytes 1048576 | tf_op jit(solution)/shard_map/all_to_all | solution.py:212
  19.4 5.1 %whiten.3 = bf16[8,2,64,256]{3,2,1,0:T(8,128)(2,1)} custom-call(s32[1]{0:T(128)} %bitcast.1.hi_ref, bf16[2,16,64,256]{3,2,1,0:T(8,128)(2,1)} %x_ref.3, bf16[2,64,256]{2,1,0:T(8,128)(2,1)} %copy-done.25), custom_call_target="tpu_custom_call" | custom-call | flops 2000000 | bytes 1048576 | tf_op jit(solution)/shard_map/whiten/pallas_call | solution.py:61
  24.6 6.7 %all-to-all-done = bf16[8,2,64,256]{3,2,1,0:T(8,128)(2,1)S(1)} async-done(((bf16[8,2,64,256]{3,2,1,0:T(8,128)(2,1)}), bf16[8,2,64,256]{3,2,1,0:T(8,128)(2,1)S(1)}, u32[]{:S(2)}, u32[]{:S(2)}) %all-to-all-start) | async-done | bytes 524320 | tf_op jit(solution)/shard_map/all_to_all | solution.py:212
  31.3 4.3 %all-to-all-start.1 = ((bf16[8,2,64,256]{3,2,1,0:T(8,128)(2,1)}), bf16[8,2,64,256]{3,2,1,0:T(8,128)(2,1)S(1)}, u32[]{:S(2)}, u32[]{:S(2)}) async-start(bf16[8,2,64,256]{3,2,1,0:T(8,128)(2,1)} %whiten.3), calls=%async_computation.1 | async-start | bytes 1048576 | tf_op jit(solution)/shard_map/all_to_all | solution.py:212
  36.4 4.3 %collective-permute-start.29 = (bf16[2,2,2,64,256]{4,3,2,1,0:T(8,128)(2,1)S(1)}, bf16[2,2,2,64,256]{4,3,2,1,0:T(8,128)(2,1)S(1)}, u32[]{:S(2)}, u32[]{:S(2)}) collective-permute-start(bf16[2,2,2,64,256]{4,3,2,1,0:T(8,128)(2,1)S(1)} %get-tuple-element.5), channel_id=1, source_target_pairs={{4,0},{8,4},{12,8},{16,12},{20,16},{24,20},{28,24},{0,28},{5,1},{9... | collective-permute-start | bytes 786440 | tf_op jit(solution)/shard_map/ppermute | solution.py:232
  40.6 6.9 %all-to-all-done.1 = bf16[8,2,64,256]{3,2,1,0:T(8,128)(2,1)S(1)} async-done(((bf16[8,2,64,256]{3,2,1,0:T(8,128)(2,1)}), bf16[8,2,64,256]{3,2,1,0:T(8,128)(2,1)S(1)}, u32[]{:S(2)}, u32[]{:S(2)}) %all-to-all-start.1) | async-done | bytes 524320 | tf_op jit(solution)/shard_map/all_to_all | solution.py:212
  48.3 4.3 %collective-permute-start.21 = (bf16[2,2,2,64,256]{4,3,2,1,0:T(8,128)(2,1)S(1)}, bf16[2,2,2,64,256]{4,3,2,1,0:T(8,128)(2,1)S(1)}, u32[]{:S(2)}, u32[]{:S(2)}) collective-permute-start(bf16[2,2,2,64,256]{4,3,2,1,0:T(8,128)(2,1)S(1)} %get-tuple-element.7), channel_id=1, source_target_pairs={{4,0},{8,4},{12,8},{16,12},{20,16},{24,20},{28,24},{0,28},{5,1},{9... | collective-permute-start | bytes 786440 | tf_op jit(solution)/shard_map/ppermute | solution.py:232
  52.6 2.7 %collective-permute-start.30 = (bf16[2,2,2,64,256]{4,3,2,1,0:T(8,128)(2,1)S(1)}, bf16[2,2,2,64,256]{4,3,2,1,0:T(8,128)(2,1)S(1)}, u32[]{:S(2)}, u32[]{:S(2)}) collective-permute-start(bf16[2,2,2,64,256]{4,3,2,1,0:T(8,128)(2,1)S(1)} %collective-permute-done.29.refs_5_), channel_id=1, source_target_pairs={{4,0},{8,4},{12,8},{16,12},{20,16},{24,20},{28,24},{0,28},{5,1},{9... | collective-permute-start | bytes 786440 | tf_op jit(solution)/shard_map/ppermute | solution.py:232
  55.3 2.1 collective-permute-done.21.refs_4_
  57.4 3.4 %collective-permute-start.22 = (bf16[2,2,2,64,256]{4,3,2,1,0:T(8,128)(2,1)S(1)}, bf16[2,2,2,64,256]{4,3,2,1,0:T(8,128)(2,1)}, u32[]{:S(2)}, u32[]{:S(2)}) collective-permute-start(bf16[2,2,2,64,256]{4,3,2,1,0:T(8,128)(2,1)S(1)} %collective-permute-done.21.refs_4_), channel_id=1, source_target_pairs={{4,0},{8,4},{12,8},{16,12},{20,16},{24,20},{28,24},{0,28},{5,1},{9... | collective-permute-start | bytes 786440 | tf_op jit(solution)/shard_map/ppermute | solution.py:232
  60.8 2.2 %collective-permute-done.30.refs_6_ = bf16[2,2,2,64,256]{4,3,2,1,0:T(8,128)(2,1)S(1)} collective-permute-done((bf16[2,2,2,64,256]{4,3,2,1,0:T(8,128)(2,1)S(1)}, bf16[2,2,2,64,256]{4,3,2,1,0:T(8,128)(2,1)S(1)}, u32[]{:S(2)}, u32[]{:S(2)}) %collective-permute-start.30) | collective-permute-done | bytes 262176 | tf_op jit(solution)/shard_map/ppermute | solution.py:232
  63.0 3.4 %collective-permute-start.31 = (bf16[2,2,2,64,256]{4,3,2,1,0:T(8,128)(2,1)S(1)}, bf16[2,2,2,64,256]{4,3,2,1,0:T(8,128)(2,1)S(1)}, u32[]{:S(2)}, u32[]{:S(2)}) collective-permute-start(bf16[2,2,2,64,256]{4,3,2,1,0:T(8,128)(2,1)S(1)} %collective-permute-done.30.refs_6_), channel_id=1, source_target_pairs={{4,0},{8,4},{12,8},{16,12},{20,16},{24,20},{28,24},{0,28},{5,1},{9... | collective-permute-start | bytes 786440 | tf_op jit(solution)/shard_map/ppermute | solution.py:232
  66.4 2.2 %collective-permute-done.22.refs_5_ = bf16[2,2,2,64,256]{4,3,2,1,0:T(8,128)(2,1)} collective-permute-done((bf16[2,2,2,64,256]{4,3,2,1,0:T(8,128)(2,1)S(1)}, bf16[2,2,2,64,256]{4,3,2,1,0:T(8,128)(2,1)}, u32[]{:S(2)}, u32[]{:S(2)}) %collective-permute-start.22) | collective-permute-done | bytes 262176 | tf_op jit(solution)/shard_map/ppermute | solution.py:232
  68.6 3.5 %collective-permute-start.23 = (bf16[2,2,2,64,256]{4,3,2,1,0:T(8,128)(2,1)}, bf16[2,2,2,64,256]{4,3,2,1,0:T(8,128)(2,1)S(1)}, u32[]{:S(2)}, u32[]{:S(2)}) collective-permute-start(bf16[2,2,2,64,256]{4,3,2,1,0:T(8,128)(2,1)} %collective-permute-done.22.refs_5_), channel_id=1, source_target_pairs={{4,0},{8,4},{12,8},{16,12},{20,16},{24,20},{28,24},{0,28},{5,1},{9... | collective-permute-start | bytes 786440 | tf_op jit(solution)/shard_map/ppermute | solution.py:232
  72.1 2.1 collective-permute-done.31.refs_7_
  74.9 3.4 %collective-permute-start.32 = (bf16[1,2,2,64,256]{4,3,2,1,0:T(8,128)(2,1)}, bf16[1,2,2,64,256]{4,3,2,1,0:T(8,128)(2,1)S(1)}, u32[]{:S(2)}, u32[]{:S(2)}) collective-permute-start(bf16[1,2,2,64,256]{4,3,2,1,0:T(8,128)(2,1)} %slice.63), channel_id=1, source_target_pairs={{4,0},{8,4},{12,8},{16,12},{20,16},{24,20},{28,24},{0,28},{5,1},{9... | collective-permute-start | bytes 393224 | tf_op jit(solution)/shard_map/ppermute | solution.py:236
  80.6 3.3 %collective-permute-start.24 = (bf16[1,2,2,64,256]{4,3,2,1,0:T(8,128)(2,1)}, bf16[1,2,2,64,256]{4,3,2,1,0:T(8,128)(2,1)}, u32[]{:S(2)}, u32[]{:S(2)}) collective-permute-start(bf16[1,2,2,64,256]{4,3,2,1,0:T(8,128)(2,1)} %slice.60), channel_id=1, source_target_pairs={{4,0},{8,4},{12,8},{16,12},{20,16},{24,20},{28,24},{0,28},{5,1},{9... | collective-permute-start | bytes 393224 | tf_op jit(solution)/shard_map/ppermute | solution.py:236
  85.2 1.0 collective-permute-done.24.refs_7_
  86.2 3.8 %collective-permute-done.20.refs_3_ = bf16[1,2,2,64,256]{4,3,2,1,0:T(8,128)(2,1)} collective-permute-done((bf16[1,2,2,64,256]{4,3,2,1,0:T(8,128)(2,1)}, bf16[1,2,2,64,256]{4,3,2,1,0:T(8,128)(2,1)}, u32[]{:S(2)}, u32[]{:S(2)}) %collective-permute-start.20) | collective-permute-done | bytes 131104 | tf_op jit(solution)/shard_map/ppermute | solution.py:235
  90.0 7.4 %cross.6.refs_0_ = bf16[8,4,2,2,64,128]{5,4,3,2,1,0:T(8,128)(2,1)} custom-call(s32[1]{0:T(128)} %bitcast.z_ref, f32[8]{0:T(128)} %constant.35.clone.coef_ref, bf16[2,4,2,64,256]{4,3,2,1,0:T(8,128)(2,1)} %bitcast.13, bf16[2,2,2,64,256]{4,3,2,1,0:T(8,128)(2,1)} %copy-done.16, bf16[2,2,2,64,256]{4,3,2,1,0:T(8,128)(2,1)} %collective-permute-done.18.refs_1_, ...), custom_call_target="tpu_custom_call" | custom-call | flops 1073741824 | bytes 3670016 | tf_op jit(solution)/shard_map/cross/pallas_call | solution.py:148
  98.0 7.3 %cross.7 = bf16[8,4,2,2,64,128]{5,4,3,2,1,0:T(8,128)(2,1)} custom-call(s32[1]{0:T(128)} %bitcast.z_ref, f32[8]{0:T(128)} %broadcast_select_fusion.coef_ref, bf16[2,4,2,64,256]{4,3,2,1,0:T(8,128)(2,1)} %bitcast.16, bf16[8,4,2,2,64,128]{5,4,3,2,1,0:T(8,128)(2,1)} %cross.6.refs_0_, ...), custom_call_target="tpu_custom_call", output_to_operand_aliasing={{}: (3, {})} | custom-call | flops 1073741824 | bytes 3670016 | tf_op jit(solution)/shard_map/cross/pallas_call | solution.py:148
  105.4 9.7 %all-to-all-start.3 = ((bf16[32,2,2,64,128]{4,3,2,1,0:T(8,128)(2,1)}), bf16[32,2,2,64,128]{4,3,2,1,0:T(8,128)(2,1)S(1)}, u32[]{:S(2)}, u32[]{:S(2)}) async-start(bf16[32,2,2,64,128]{4,3,2,1,0:T(8,128)(2,1)} %bitcast.11), calls=%async_computation.3 | async-start | bytes 4194304 | tf_op jit(solution)/shard_map/all_to_all | solution.py:248
  115.2 1.5 collective-permute-start.1
  116.6 1.3 collective-permute-start.13
  118.1 4.7 %collective-permute-done.5.refs_4_ = bf16[2,2,2,64,256]{4,3,2,1,0:T(8,128)(2,1)S(1)} collective-permute-done((bf16[2,2,2,64,256]{4,3,2,1,0:T(8,128)(2,1)S(1)}, bf16[2,2,2,64,256]{4,3,2,1,0:T(8,128)(2,1)S(1)}, u32[]{:S(2)}, u32[]{:S(2)}) %collective-permute-start.5) | collective-permute-done | bytes 262176 | tf_op jit(solution)/shard_map/ppermute | solution.py:232
  122.9 1.5 collective-permute-start.6
  124.4 4.1 %collective-permute-done.13.refs_5_ = bf16[2,2,2,64,256]{4,3,2,1,0:T(8,128)(2,1)S(1)} collective-permute-done((bf16[2,2,2,64,256]{4,3,2,1,0:T(8,128)(2,1)S(1)}, bf16[2,2,2,64,256]{4,3,2,1,0:T(8,128)(2,1)S(1)}, u32[]{:S(2)}, u32[]{:S(2)}) %collective-permute-start.13) | collective-permute-done | bytes 262176 | tf_op jit(solution)/shard_map/ppermute | solution.py:232
  128.5 1.5 collective-permute-start.14
  130.0 4.1 %collective-permute-done.6.refs_5_ = bf16[2,2,2,64,256]{4,3,2,1,0:T(8,128)(2,1)S(1)} collective-permute-done((bf16[2,2,2,64,256]{4,3,2,1,0:T(8,128)(2,1)S(1)}, bf16[2,2,2,64,256]{4,3,2,1,0:T(8,128)(2,1)S(1)}, u32[]{:S(2)}, u32[]{:S(2)}) %collective-permute-start.6) | collective-permute-done | bytes 262176 | tf_op jit(solution)/shard_map/ppermute | solution.py:232
  134.1 1.5 collective-permute-start.7
  135.6 4.1 %collective-permute-done.14.refs_6_ = bf16[2,2,2,64,256]{4,3,2,1,0:T(8,128)(2,1)S(1)} collective-permute-done((bf16[2,2,2,64,256]{4,3,2,1,0:T(8,128)(2,1)S(1)}, bf16[2,2,2,64,256]{4,3,2,1,0:T(8,128)(2,1)S(1)}, u32[]{:S(2)}, u32[]{:S(2)}) %collective-permute-start.14) | collective-permute-done | bytes 262176 | tf_op jit(solution)/shard_map/ppermute | solution.py:232
  139.7 1.5 collective-permute-start.15
  141.3 4.1 %collective-permute-done.7.refs_6_ = bf16[2,2,2,64,256]{4,3,2,1,0:T(8,128)(2,1)S(1)} collective-permute-done((bf16[2,2,2,64,256]{4,3,2,1,0:T(8,128)(2,1)S(1)}, bf16[2,2,2,64,256]{4,3,2,1,0:T(8,128)(2,1)S(1)}, u32[]{:S(2)}, u32[]{:S(2)}) %collective-permute-start.7) | collective-permute-done | bytes 262176 | tf_op jit(solution)/shard_map/ppermute | solution.py:232
  145.3 1.6 collective-permute-start.8
  147.1 3.9 %collective-permute-done.15.refs_7_ = bf16[2,2,2,64,256]{4,3,2,1,0:T(8,128)(2,1)S(1)} collective-permute-done((bf16[2,2,2,64,256]{4,3,2,1,0:T(8,128)(2,1)S(1)}, bf16[2,2,2,64,256]{4,3,2,1,0:T(8,128)(2,1)S(1)}, u32[]{:S(2)}, u32[]{:S(2)}) %collective-permute-start.15) | collective-permute-done | bytes 262176 | tf_op jit(solution)/shard_map/ppermute | solution.py:232
  151.0 1.6 collective-permute-start.16
  152.7 1.1 collective-permute-done.8.refs_7_
  153.8 1.3 collective-permute-done.4.refs_3_
  155.8 7.3 %cross.4.refs_0_ = bf16[8,4,2,2,64,128]{5,4,3,2,1,0:T(8,128)(2,1)} custom-call(s32[1]{0:T(128)} %bitcast.z_ref, f32[8]{0:T(128)} %constant.35.clone.coef_ref, bf16[2,4,2,64,256]{4,3,2,1,0:T(8,128)(2,1)} %bitcast.14, bf16[2,2,2,64,256]{4,3,2,1,0:T(8,128)(2,1)} %copy-done.20, bf16[2,2,2,64,256]{4,3,2,1,0:T(8,128)(2,1)} %copy-done.24, ...), custom_call_target="tpu_custom_call" | custom-call | flops 1073741824 | bytes 3670016 | tf_op jit(solution)/shard_map/cross/pallas_call | solution.py:148
  164.4 7.3 %cross.5 = bf16[8,4,2,2,64,128]{5,4,3,2,1,0:T(8,128)(2,1)} custom-call(s32[1]{0:T(128)} %bitcast.z_ref, f32[8]{0:T(128)} %broadcast_select_fusion.coef_ref, bf16[2,4,2,64,256]{4,3,2,1,0:T(8,128)(2,1)} %bitcast.17, bf16[8,4,2,2,64,128]{5,4,3,2,1,0:T(8,128)(2,1)} %cross.4.refs_0_, ...), custom_call_target="tpu_custom_call", output_to_operand_aliasing={{}: (3, {})} | custom-call | flops 1073741824 | bytes 3670016 | tf_op jit(solution)/shard_map/cross/pallas_call | solution.py:148
  171.7 1.4 copy-done
  173.1 8.2 %all-to-all-start.2 = ((bf16[32,2,2,64,128]{4,3,2,1,0:T(8,128)(2,1)}), bf16[32,2,2,64,128]{4,3,2,1,0:T(8,128)(2,1)}, u32[]{:S(2)}, u32[]{:S(2)}) async-start(bf16[32,2,2,64,128]{4,3,2,1,0:T(8,128)(2,1)} %bitcast.10), calls=%async_computation.2 | async-start | bytes 4194304 | tf_op jit(solution)/shard_map/all_to_all | solution.py:248
  181.3 6.0 %lags.2.refs_0_ = f32[128,64,256]{2,1,0:T(8,128)} custom-call(bf16[128,128]{1,0:T(8,128)(2,1)} %constant.36.clone.t_ref, bf16[32,2,2,64,128]{4,3,2,1,0:T(8,128)(2,1)} %copy-done), custom_call_target="tpu_custom_call" | custom-call | flops 268435456 | bytes 6291456 | tf_op jit(solution)/shard_map/lags/pallas_call | solution.py:187
  187.3 24.3 %all-to-all-done.2.x_ref = bf16[32,2,2,64,128]{4,3,2,1,0:T(8,128)(2,1)} async-done(((bf16[32,2,2,64,128]{4,3,2,1,0:T(8,128)(2,1)}), bf16[32,2,2,64,128]{4,3,2,1,0:T(8,128)(2,1)}, u32[]{:S(2)}, u32[]{:S(2)}) %all-to-all-start.2) | async-done | bytes 2097184 | tf_op jit(solution)/shard_map/all_to_all | solution.py:248
  211.6 6.0 %lags.3 = f32[128,64,256]{2,1,0:T(8,128)} custom-call(bf16[128,128]{1,0:T(8,128)(2,1)} %constant.36.clone.t_ref, bf16[32,2,2,64,128]{4,3,2,1,0:T(8,128)(2,1)} %all-to-all-done.2.x_ref, f32[128,64,256]{2,1,0:T(8,128)} %lags.2.refs_0_), custom_call_target="tpu_custom_call", output_to_operand_aliasing={{}: (2, {})} | custom-call | flops 268435456 | bytes 6291456 | tf_op jit(solution)/shard_map/lags/pallas_call | solution.py:187
  (116 shorter events, 10.5 us)
Async XLA Ops:
  0.8 6.5 %collective-permute-start = (bf16[2,64,256]{2,1,0:T(8,128)(2,1)S(1)}, bf16[2,64,256]{2,1,0:T(8,128)(2,1)S(1)}, u32[]{:S(2)}, u32[]{:S(2)}) collective-permute-start(bf16[2,64,256]{2,1,0:T(8,128)(2,1)S(1)} %slice_bitcast_fusion), channel_id=1, source_target_pairs={{32,0},{64,32},{96,64},{0,96},{33,1},{65,33},{97,65},{1,97},{34,2}... | collective-permute-start | bytes 196616 | tf_op jit(solution)/shard_map/ppermute | solution.py:207
  13.2 18.1 %all-to-all-start = ((bf16[8,2,64,256]{3,2,1,0:T(8,128)(2,1)}), bf16[8,2,64,256]{3,2,1,0:T(8,128)(2,1)S(1)}, u32[]{:S(2)}, u32[]{:S(2)}) async-start(bf16[8,2,64,256]{3,2,1,0:T(8,128)(2,1)} %whiten.2), calls=%async_computation | async-start | bytes 1048576 | tf_op jit(solution)/shard_map/all_to_all | solution.py:212
  24.6 60.1 %copy-start.33 = (f32[8]{0:T(128)S(1)}, f32[8]{0:T(128)}, u32[]{:S(2)}) copy-start(f32[8]{0:T(128)} %constant.35.clone.coef_ref) | copy-start | bytes 100
  24.6 60.1 %copy-start.34 = (f32[8]{0:T(128)S(1)}, f32[8]{0:T(128)}, u32[]{:S(2)}) copy-start(f32[8]{0:T(128)} %constant.34.clone) | copy-start | bytes 100
  31.3 53.3 %copy-start.2 = (bf16[8,2,64,256]{3,2,1,0:T(8,128)(2,1)}, bf16[8,2,64,256]{3,2,1,0:T(8,128)(2,1)S(1)}, u32[]{:S(2)}) copy-start(bf16[8,2,64,256]{3,2,1,0:T(8,128)(2,1)S(1)} %all-to-all-done) | copy-start | bytes 1572868
  31.3 16.2 %all-to-all-start.1 = ((bf16[8,2,64,256]{3,2,1,0:T(8,128)(2,1)}), bf16[8,2,64,256]{3,2,1,0:T(8,128)(2,1)S(1)}, u32[]{:S(2)}, u32[]{:S(2)}) async-start(bf16[8,2,64,256]{3,2,1,0:T(8,128)(2,1)} %whiten.3), calls=%async_computation.1 | async-start | bytes 1048576 | tf_op jit(solution)/shard_map/all_to_all | solution.py:212
  36.4 16.3 %collective-permute-start.29 = (bf16[2,2,2,64,256]{4,3,2,1,0:T(8,128)(2,1)S(1)}, bf16[2,2,2,64,256]{4,3,2,1,0:T(8,128)(2,1)S(1)}, u32[]{:S(2)}, u32[]{:S(2)}) collective-permute-start(bf16[2,2,2,64,256]{4,3,2,1,0:T(8,128)(2,1)S(1)} %get-tuple-element.5), channel_id=1, source_target_pairs={{4,0},{8,4},{12,8},{16,12},{20,16},{24,20},{28,24},{0,28},{5,1},{9... | collective-permute-start | bytes 786440 | tf_op jit(solution)/shard_map/ppermute | solution.py:232
  40.6 14.7 %collective-permute-start.25 = (bf16[2,2,2,64,256]{4,3,2,1,0:T(8,128)(2,1)S(1)}, bf16[2,2,2,64,256]{4,3,2,1,0:T(8,128)(2,1)S(1)}, u32[]{:S(2)}, u32[]{:S(2)}) collective-permute-start(bf16[2,2,2,64,256]{4,3,2,1,0:T(8,128)(2,1)S(1)} %get-tuple-element.5), channel_id=1, source_target_pairs={{0,4},{4,8},{8,12},{12,16},{16,20},{20,24},{24,28},{28,0},{1,5},{5... | collective-permute-start | bytes 786440 | tf_op jit(solution)/shard_map/ppermute | solution.py:231
  47.5 42.5 %copy-start.1 = (bf16[8,2,64,256]{3,2,1,0:T(8,128)(2,1)}, bf16[8,2,64,256]{3,2,1,0:T(8,128)(2,1)S(1)}, u32[]{:S(2)}) copy-start(bf16[8,2,64,256]{3,2,1,0:T(8,128)(2,1)S(1)} %all-to-all-done.1) | copy-start | bytes 1572868
  48.3 9.0 %collective-permute-start.21 = (bf16[2,2,2,64,256]{4,3,2,1,0:T(8,128)(2,1)S(1)}, bf16[2,2,2,64,256]{4,3,2,1,0:T(8,128)(2,1)S(1)}, u32[]{:S(2)}, u32[]{:S(2)}) collective-permute-start(bf16[2,2,2,64,256]{4,3,2,1,0:T(8,128)(2,1)S(1)} %get-tuple-element.7), channel_id=1, source_target_pairs={{4,0},{8,4},{12,8},{16,12},{20,16},{24,20},{28,24},{0,28},{5,1},{9... | collective-permute-start | bytes 786440 | tf_op jit(solution)/shard_map/ppermute | solution.py:232
  52.6 8.2 %collective-permute-start.17 = (bf16[2,2,2,64,256]{4,3,2,1,0:T(8,128)(2,1)S(1)}, bf16[2,2,2,64,256]{4,3,2,1,0:T(8,128)(2,1)S(1)}, u32[]{:S(2)}, u32[]{:S(2)}) collective-permute-start(bf16[2,2,2,64,256]{4,3,2,1,0:T(8,128)(2,1)S(1)} %get-tuple-element.7), channel_id=1, source_target_pairs={{0,4},{4,8},{8,12},{12,16},{16,20},{20,24},{24,28},{28,0},{1,5},{5... | collective-permute-start | bytes 786440 | tf_op jit(solution)/shard_map/ppermute | solution.py:231
  52.6 44.8 %copy-start.11 = (bf16[2,2,2,64,256]{4,3,2,1,0:T(8,128)(2,1)}, bf16[2,2,2,64,256]{4,3,2,1,0:T(8,128)(2,1)S(1)}, u32[]{:S(2)}) copy-start(bf16[2,2,2,64,256]{4,3,2,1,0:T(8,128)(2,1)S(1)} %collective-permute-done.29.refs_5_) | copy-start | bytes 786436
  52.6 10.4 %collective-permute-start.30 = (bf16[2,2,2,64,256]{4,3,2,1,0:T(8,128)(2,1)S(1)}, bf16[2,2,2,64,256]{4,3,2,1,0:T(8,128)(2,1)S(1)}, u32[]{:S(2)}, u32[]{:S(2)}) collective-permute-start(bf16[2,2,2,64,256]{4,3,2,1,0:T(8,128)(2,1)S(1)} %collective-permute-done.29.refs_5_), channel_id=1, source_target_pairs={{4,0},{8,4},{12,8},{16,12},{20,16},{24,20},{28,24},{0,28},{5,1},{9... | collective-permute-start | bytes 786440 | tf_op jit(solution)/shard_map/ppermute | solution.py:232
  55.3 42.1 %copy-start.12 = (bf16[2,2,2,64,256]{4,3,2,1,0:T(8,128)(2,1)}, bf16[2,2,2,64,256]{4,3,2,1,0:T(8,128)(2,1)S(1)}, u32[]{:S(2)}) copy-start(bf16[2,2,2,64,256]{4,3,2,1,0:T(8,128)(2,1)S(1)} %collective-permute-done.25.refs_1_) | copy-start | bytes 786436
  55.3 11.1 %collective-permute-start.26 = (bf16[2,2,2,64,256]{4,3,2,1,0:T(8,128)(2,1)S(1)}, bf16[2,2,2,64,256]{4,3,2,1,0:T(8,128)(2,1)S(1)}, u32[]{:S(2)}, u32[]{:S(2)}) collective-permute-start(bf16[2,2,2,64,256]{4,3,2,1,0:T(8,128)(2,1)S(1)} %collective-permute-done.25.refs_1_), channel_id=1, source_target_pairs={{0,4},{4,8},{8,12},{12,16},{16,20},{20,24},{24,28},{28,0},{1,5},{5... | collective-permute-start | bytes 786440 | tf_op jit(solution)/shard_map/ppermute | solution.py:231
  57.4 32.7 %copy-start.15 = (bf16[2,2,2,64,256]{4,3,2,1,0:T(8,128)(2,1)}, bf16[2,2,2,64,256]{4,3,2,1,0:T(8,128)(2,1)S(1)}, u32[]{:S(2)}) copy-start(bf16[2,2,2,64,256]{4,3,2,1,0:T(8,128)(2,1)S(1)} %collective-permute-done.21.refs_4_) | copy-start | bytes 786436
  57.4 11.2 %collective-permute-start.22 = (bf16[2,2,2,64,256]{4,3,2,1,0:T(8,128)(2,1)S(1)}, bf16[2,2,2,64,256]{4,3,2,1,0:T(8,128)(2,1)}, u32[]{:S(2)}, u32[]{:S(2)}) collective-permute-start(bf16[2,2,2,64,256]{4,3,2,1,0:T(8,128)(2,1)S(1)} %collective-permute-done.21.refs_4_), channel_id=1, source_target_pairs={{4,0},{8,4},{12,8},{16,12},{20,16},{24,20},{28,24},{0,28},{5,1},{9... | collective-permute-start | bytes 786440 | tf_op jit(solution)/shard_map/ppermute | solution.py:232
  60.8 11.3 %collective-permute-start.18 = (bf16[2,2,2,64,256]{4,3,2,1,0:T(8,128)(2,1)S(1)}, bf16[2,2,2,64,256]{4,3,2,1,0:T(8,128)(2,1)}, u32[]{:S(2)}, u32[]{:S(2)}) collective-permute-start(bf16[2,2,2,64,256]{4,3,2,1,0:T(8,128)(2,1)S(1)} %collective-permute-done.17.refs_0_), channel_id=1, source_target_pairs={{0,4},{4,8},{8,12},{12,16},{16,20},{20,24},{24,28},{28,0},{1,5},{5... | collective-permute-start | bytes 786440 | tf_op jit(solution)/shard_map/ppermute | solution.py:231
  63.0 34.5 %copy-start.13 = (bf16[2,2,2,64,256]{4,3,2,1,0:T(8,128)(2,1)}, bf16[2,2,2,64,256]{4,3,2,1,0:T(8,128)(2,1)S(1)}, u32[]{:S(2)}) copy-start(bf16[2,2,2,64,256]{4,3,2,1,0:T(8,128)(2,1)S(1)} %collective-permute-done.30.refs_6_) | copy-start | bytes 786436
  63.0 11.2 %collective-permute-start.31 = (bf16[2,2,2,64,256]{4,3,2,1,0:T(8,128)(2,1)S(1)}, bf16[2,2,2,64,256]{4,3,2,1,0:T(8,128)(2,1)S(1)}, u32[]{:S(2)}, u32[]{:S(2)}) collective-permute-start(bf16[2,2,2,64,256]{4,3,2,1,0:T(8,128)(2,1)S(1)} %collective-permute-done.30.refs_6_), channel_id=1, source_target_pairs={{4,0},{8,4},{12,8},{16,12},{20,16},{24,20},{28,24},{0,28},{5,1},{9... | collective-permute-start | bytes 786440 | tf_op jit(solution)/shard_map/ppermute | solution.py:232
  66.4 11.9 %collective-permute-start.27 = (bf16[2,2,2,64,256]{4,3,2,1,0:T(8,128)(2,1)S(1)}, bf16[2,2,2,64,256]{4,3,2,1,0:T(8,128)(2,1)S(1)}, u32[]{:S(2)}, u32[]{:S(2)}) collective-permute-start(bf16[2,2,2,64,256]{4,3,2,1,0:T(8,128)(2,1)S(1)} %collective-permute-done.26.refs_2_), channel_id=1, source_target_pairs={{0,4},{4,8},{8,12},{12,16},{16,20},{20,24},{24,28},{28,0},{1,5},{5... | collective-permute-start | bytes 786440 | tf_op jit(solution)/shard_map/ppermute | solution.py:231
  68.6 11.3 %collective-permute-start.23 = (bf16[2,2,2,64,256]{4,3,2,1,0:T(8,128)(2,1)}, bf16[2,2,2,64,256]{4,3,2,1,0:T(8,128)(2,1)S(1)}, u32[]{:S(2)}, u32[]{:S(2)}) collective-permute-start(bf16[2,2,2,64,256]{4,3,2,1,0:T(8,128)(2,1)} %collective-permute-done.22.refs_5_), channel_id=1, source_target_pairs={{4,0},{8,4},{12,8},{16,12},{20,16},{24,20},{28,24},{0,28},{5,1},{9... | collective-permute-start | bytes 786440 | tf_op jit(solution)/shard_map/ppermute | solution.py:232
  72.1 11.8 %collective-permute-start.19 = (bf16[2,2,2,64,256]{4,3,2,1,0:T(8,128)(2,1)}, bf16[2,2,2,64,256]{4,3,2,1,0:T(8,128)(2,1)S(1)}, u32[]{:S(2)}, u32[]{:S(2)}) collective-permute-start(bf16[2,2,2,64,256]{4,3,2,1,0:T(8,128)(2,1)} %collective-permute-done.18.refs_1_), channel_id=1, source_target_pairs={{0,4},{4,8},{8,12},{12,16},{16,20},{20,24},{24,28},{28,0},{1,5},{5... | collective-permute-start | bytes 786440 | tf_op jit(solution)/shard_map/ppermute | solution.py:231
  74.9 22.5 %collective-permute-start.32 = (bf16[1,2,2,64,256]{4,3,2,1,0:T(8,128)(2,1)}, bf16[1,2,2,64,256]{4,3,2,1,0:T(8,128)(2,1)S(1)}, u32[]{:S(2)}, u32[]{:S(2)}) collective-permute-start(bf16[1,2,2,64,256]{4,3,2,1,0:T(8,128)(2,1)} %slice.63), channel_id=1, source_target_pairs={{4,0},{8,4},{12,8},{16,12},{20,16},{24,20},{28,24},{0,28},{5,1},{9... | collective-permute-start | bytes 393224 | tf_op jit(solution)/shard_map/ppermute | solution.py:236
  79.0 18.4 %collective-permute-start.28 = (bf16[1,2,2,64,256]{4,3,2,1,0:T(8,128)(2,1)}, bf16[1,2,2,64,256]{4,3,2,1,0:T(8,128)(2,1)}, u32[]{:S(2)}, u32[]{:S(2)}) collective-permute-start(bf16[1,2,2,64,256]{4,3,2,1,0:T(8,128)(2,1)} %slice.62), channel_id=1, source_target_pairs={{0,4},{4,8},{8,12},{12,16},{16,20},{20,24},{24,28},{28,0},{1,5},{5... | collective-permute-start | bytes 393224 | tf_op jit(solution)/shard_map/ppermute | solution.py:235
  80.6 5.6 %collective-permute-start.24 = (bf16[1,2,2,64,256]{4,3,2,1,0:T(8,128)(2,1)}, bf16[1,2,2,64,256]{4,3,2,1,0:T(8,128)(2,1)}, u32[]{:S(2)}, u32[]{:S(2)}) collective-permute-start(bf16[1,2,2,64,256]{4,3,2,1,0:T(8,128)(2,1)} %slice.60), channel_id=1, source_target_pairs={{4,0},{8,4},{12,8},{16,12},{20,16},{24,20},{28,24},{0,28},{5,1},{9... | collective-permute-start | bytes 393224 | tf_op jit(solution)/shard_map/ppermute | solution.py:236
  84.7 5.3 %collective-permute-start.20 = (bf16[1,2,2,64,256]{4,3,2,1,0:T(8,128)(2,1)}, bf16[1,2,2,64,256]{4,3,2,1,0:T(8,128)(2,1)}, u32[]{:S(2)}, u32[]{:S(2)}) collective-permute-start(bf16[1,2,2,64,256]{4,3,2,1,0:T(8,128)(2,1)} %slice.59), channel_id=1, source_target_pairs={{0,4},{4,8},{8,12},{12,16},{16,20},{20,24},{24,28},{28,0},{1,5},{5... | collective-permute-start | bytes 393224 | tf_op jit(solution)/shard_map/ppermute | solution.py:235
  105.4 66.3 %all-to-all-start.3 = ((bf16[32,2,2,64,128]{4,3,2,1,0:T(8,128)(2,1)}), bf16[32,2,2,64,128]{4,3,2,1,0:T(8,128)(2,1)S(1)}, u32[]{:S(2)}, u32[]{:S(2)}) async-start(bf16[32,2,2,64,128]{4,3,2,1,0:T(8,128)(2,1)} %bitcast.11), calls=%async_computation.3 | async-start | bytes 4194304 | tf_op jit(solution)/shard_map/all_to_all | solution.py:248
  115.1 7.8 %collective-permute-start.5 = (bf16[2,2,2,64,256]{4,3,2,1,0:T(8,128)(2,1)S(1)}, bf16[2,2,2,64,256]{4,3,2,1,0:T(8,128)(2,1)S(1)}, u32[]{:S(2)}, u32[]{:S(2)}) collective-permute-start(bf16[2,2,2,64,256]{4,3,2,1,0:T(8,128)(2,1)S(1)} %copy-done.27), channel_id=1, source_target_pairs={{4,0},{8,4},{12,8},{16,12},{20,16},{24,20},{28,24},{0,28},{5,1},{9... | collective-permute-start | bytes 786440 | tf_op jit(solution)/shard_map/ppermute | solution.py:232
  115.2 9.2 %collective-permute-start.1 = (bf16[2,2,2,64,256]{4,3,2,1,0:T(8,128)(2,1)S(1)}, bf16[2,2,2,64,256]{4,3,2,1,0:T(8,128)(2,1)S(1)}, u32[]{:S(2)}, u32[]{:S(2)}) collective-permute-start(bf16[2,2,2,64,256]{4,3,2,1,0:T(8,128)(2,1)S(1)} %copy-done.27), channel_id=1, source_target_pairs={{0,4},{4,8},{8,12},{12,16},{16,20},{20,24},{24,28},{28,0},{1,5},{5... | collective-permute-start | bytes 786440 | tf_op jit(solution)/shard_map/ppermute | solution.py:231
  116.6 11.8 %collective-permute-start.13 = (bf16[2,2,2,64,256]{4,3,2,1,0:T(8,128)(2,1)S(1)}, bf16[2,2,2,64,256]{4,3,2,1,0:T(8,128)(2,1)S(1)}, u32[]{:S(2)}, u32[]{:S(2)}) collective-permute-start(bf16[2,2,2,64,256]{4,3,2,1,0:T(8,128)(2,1)S(1)} %copy-done.26), channel_id=1, source_target_pairs={{4,0},{8,4},{12,8},{16,12},{20,16},{24,20},{28,24},{0,28},{5,1},{9... | collective-permute-start | bytes 786440 | tf_op jit(solution)/shard_map/ppermute | solution.py:232
  118.0 12.1 %collective-permute-start.9 = (bf16[2,2,2,64,256]{4,3,2,1,0:T(8,128)(2,1)S(1)}, bf16[2,2,2,64,256]{4,3,2,1,0:T(8,128)(2,1)S(1)}, u32[]{:S(2)}, u32[]{:S(2)}) collective-permute-start(bf16[2,2,2,64,256]{4,3,2,1,0:T(8,128)(2,1)S(1)} %copy-done.26), channel_id=1, source_target_pairs={{0,4},{4,8},{8,12},{12,16},{16,20},{20,24},{24,28},{28,0},{1,5},{5... | collective-permute-start | bytes 786440 | tf_op jit(solution)/shard_map/ppermute | solution.py:231
  122.9 32.2 %copy-start.19 = (bf16[2,2,2,64,256]{4,3,2,1,0:T(8,128)(2,1)}, bf16[2,2,2,64,256]{4,3,2,1,0:T(8,128)(2,1)S(1)}, u32[]{:S(2)}) copy-start(bf16[2,2,2,64,256]{4,3,2,1,0:T(8,128)(2,1)S(1)} %collective-permute-done.5.refs_4_) | copy-start | bytes 786436
  122.9 11.2 %collective-permute-start.6 = (bf16[2,2,2,64,256]{4,3,2,1,0:T(8,128)(2,1)S(1)}, bf16[2,2,2,64,256]{4,3,2,1,0:T(8,128)(2,1)S(1)}, u32[]{:S(2)}, u32[]{:S(2)}) collective-permute-start(bf16[2,2,2,64,256]{4,3,2,1,0:T(8,128)(2,1)S(1)} %collective-permute-done.5.refs_4_), channel_id=1, source_target_pairs={{4,0},{8,4},{12,8},{16,12},{20,16},{24,20},{28,24},{0,28},{5,1},{9... | collective-permute-start | bytes 786440 | tf_op jit(solution)/shard_map/ppermute | solution.py:232
  124.4 11.2 %collective-permute-start.2 = (bf16[2,2,2,64,256]{4,3,2,1,0:T(8,128)(2,1)S(1)}, bf16[2,2,2,64,256]{4,3,2,1,0:T(8,128)(2,1)S(1)}, u32[]{:S(2)}, u32[]{:S(2)}) collective-permute-start(bf16[2,2,2,64,256]{4,3,2,1,0:T(8,128)(2,1)S(1)} %collective-permute-done.1.refs_0_), channel_id=1, source_target_pairs={{0,4},{4,8},{8,12},{12,16},{16,20},{20,24},{24,28},{28,0},{1,5},{5... | collective-permute-start | bytes 786440 | tf_op jit(solution)/shard_map/ppermute | solution.py:231
  128.5 34.6 %copy-start.17 = (bf16[2,2,2,64,256]{4,3,2,1,0:T(8,128)(2,1)}, bf16[2,2,2,64,256]{4,3,2,1,0:T(8,128)(2,1)S(1)}, u32[]{:S(2)}) copy-start(bf16[2,2,2,64,256]{4,3,2,1,0:T(8,128)(2,1)S(1)} %collective-permute-done.13.refs_5_) | copy-start | bytes 786436
  128.5 11.2 %collective-permute-start.14 = (bf16[2,2,2,64,256]{4,3,2,1,0:T(8,128)(2,1)S(1)}, bf16[2,2,2,64,256]{4,3,2,1,0:T(8,128)(2,1)S(1)}, u32[]{:S(2)}, u32[]{:S(2)}) collective-permute-start(bf16[2,2,2,64,256]{4,3,2,1,0:T(8,128)(2,1)S(1)} %collective-permute-done.13.refs_5_), channel_id=1, source_target_pairs={{4,0},{8,4},{12,8},{16,12},{20,16},{24,20},{28,24},{0,28},{5,1},{9... | collective-permute-start | bytes 786440 | tf_op jit(solution)/shard_map/ppermute | solution.py:232
  130.0 33.0 %copy-start.18 = (bf16[2,2,2,64,256]{4,3,2,1,0:T(8,128)(2,1)}, bf16[2,2,2,64,256]{4,3,2,1,0:T(8,128)(2,1)S(1)}, u32[]{:S(2)}) copy-start(bf16[2,2,2,64,256]{4,3,2,1,0:T(8,128)(2,1)S(1)} %collective-permute-done.9.refs_1_) | copy-start | bytes 786436
  130.0 11.2 %collective-permute-start.10 = (bf16[2,2,2,64,256]{4,3,2,1,0:T(8,128)(2,1)S(1)}, bf16[2,2,2,64,256]{4,3,2,1,0:T(8,128)(2,1)S(1)}, u32[]{:S(2)}, u32[]{:S(2)}) collective-permute-start(bf16[2,2,2,64,256]{4,3,2,1,0:T(8,128)(2,1)S(1)} %collective-permute-done.9.refs_1_), channel_id=1, source_target_pairs={{0,4},{4,8},{8,12},{12,16},{16,20},{20,24},{24,28},{28,0},{1,5},{5... | collective-permute-start | bytes 786440 | tf_op jit(solution)/shard_map/ppermute | solution.py:231
  134.1 11.2 %collective-permute-start.7 = (bf16[2,2,2,64,256]{4,3,2,1,0:T(8,128)(2,1)S(1)}, bf16[2,2,2,64,256]{4,3,2,1,0:T(8,128)(2,1)S(1)}, u32[]{:S(2)}, u32[]{:S(2)}) collective-permute-start(bf16[2,2,2,64,256]{4,3,2,1,0:T(8,128)(2,1)S(1)} %collective-permute-done.6.refs_5_), channel_id=1, source_target_pairs={{4,0},{8,4},{12,8},{16,12},{20,16},{24,20},{28,24},{0,28},{5,1},{9... | collective-permute-start | bytes 786440 | tf_op jit(solution)/shard_map/ppermute | solution.py:232
  135.6 11.3 %collective-permute-start.3 = (bf16[2,2,2,64,256]{4,3,2,1,0:T(8,128)(2,1)S(1)}, bf16[2,2,2,64,256]{4,3,2,1,0:T(8,128)(2,1)S(1)}, u32[]{:S(2)}, u32[]{:S(2)}) collective-permute-start(bf16[2,2,2,64,256]{4,3,2,1,0:T(8,128)(2,1)S(1)} %collective-permute-done.2.refs_1_), channel_id=1, source_target_pairs={{0,4},{4,8},{8,12},{12,16},{16,20},{20,24},{24,28},{28,0},{1,5},{5... | collective-permute-start | bytes 786440 | tf_op jit(solution)/shard_map/ppermute | solution.py:231
  139.7 11.2 %collective-permute-start.15 = (bf16[2,2,2,64,256]{4,3,2,1,0:T(8,128)(2,1)S(1)}, bf16[2,2,2,64,256]{4,3,2,1,0:T(8,128)(2,1)S(1)}, u32[]{:S(2)}, u32[]{:S(2)}) collective-permute-start(bf16[2,2,2,64,256]{4,3,2,1,0:T(8,128)(2,1)S(1)} %collective-permute-done.14.refs_6_), channel_id=1, source_target_pairs={{4,0},{8,4},{12,8},{16,12},{20,16},{24,20},{28,24},{0,28},{5,1},{9... | collective-permute-start | bytes 786440 | tf_op jit(solution)/shard_map/ppermute | solution.py:232
  141.2 11.3 %collective-permute-start.11 = (bf16[2,2,2,64,256]{4,3,2,1,0:T(8,128)(2,1)S(1)}, bf16[2,2,2,64,256]{4,3,2,1,0:T(8,128)(2,1)S(1)}, u32[]{:S(2)}, u32[]{:S(2)}) collective-permute-start(bf16[2,2,2,64,256]{4,3,2,1,0:T(8,128)(2,1)S(1)} %collective-permute-done.10.refs_2_), channel_id=1, source_target_pairs={{0,4},{4,8},{8,12},{12,16},{16,20},{20,24},{24,28},{28,0},{1,5},{5... | collective-permute-start | bytes 786440 | tf_op jit(solution)/shard_map/ppermute | solution.py:231
  145.3 8.4 %collective-permute-start.8 = (bf16[1,2,2,64,256]{4,3,2,1,0:T(8,128)(2,1)S(1)}, bf16[1,2,2,64,256]{4,3,2,1,0:T(8,128)(2,1)S(1)}, u32[]{:S(2)}, u32[]{:S(2)}) collective-permute-start(bf16[1,2,2,64,256]{4,3,2,1,0:T(8,128)(2,1)S(1)} %slice.54), channel_id=1, source_target_pairs={{4,0},{8,4},{12,8},{16,12},{20,16},{24,20},{28,24},{0,28},{5,1},{9... | collective-permute-start | bytes 393224 | tf_op jit(solution)/shard_map/ppermute | solution.py:236
  147.0 8.1 %collective-permute-start.4 = (bf16[1,2,2,64,256]{4,3,2,1,0:T(8,128)(2,1)S(1)}, bf16[1,2,2,64,256]{4,3,2,1,0:T(8,128)(2,1)S(1)}, u32[]{:S(2)}, u32[]{:S(2)}) collective-permute-start(bf16[1,2,2,64,256]{4,3,2,1,0:T(8,128)(2,1)S(1)} %slice.53), channel_id=1, source_target_pairs={{0,4},{4,8},{8,12},{12,16},{16,20},{20,24},{24,28},{28,0},{1,5},{5... | collective-permute-start | bytes 393224 | tf_op jit(solution)/shard_map/ppermute | solution.py:235
  151.0 12.1 %collective-permute-start.16 = (bf16[1,2,2,64,256]{4,3,2,1,0:T(8,128)(2,1)S(1)}, bf16[1,2,2,64,256]{4,3,2,1,0:T(8,128)(2,1)S(1)}, u32[]{:S(2)}, u32[]{:S(2)}) collective-permute-start(bf16[1,2,2,64,256]{4,3,2,1,0:T(8,128)(2,1)S(1)} %slice.57), channel_id=1, source_target_pairs={{4,0},{8,4},{12,8},{16,12},{20,16},{24,20},{28,24},{0,28},{5,1},{9... | collective-permute-start | bytes 393224 | tf_op jit(solution)/shard_map/ppermute | solution.py:236
  152.6 10.5 %collective-permute-start.12 = (bf16[1,2,2,64,256]{4,3,2,1,0:T(8,128)(2,1)S(1)}, bf16[1,2,2,64,256]{4,3,2,1,0:T(8,128)(2,1)S(1)}, u32[]{:S(2)}, u32[]{:S(2)}) collective-permute-start(bf16[1,2,2,64,256]{4,3,2,1,0:T(8,128)(2,1)S(1)} %slice.56), channel_id=1, source_target_pairs={{0,4},{4,8},{8,12},{12,16},{16,20},{20,24},{24,28},{28,0},{1,5},{5... | collective-permute-start | bytes 393224 | tf_op jit(solution)/shard_map/ppermute | solution.py:235
  173.1 38.6 %all-to-all-start.2 = ((bf16[32,2,2,64,128]{4,3,2,1,0:T(8,128)(2,1)}), bf16[32,2,2,64,128]{4,3,2,1,0:T(8,128)(2,1)}, u32[]{:S(2)}, u32[]{:S(2)}) async-start(bf16[32,2,2,64,128]{4,3,2,1,0:T(8,128)(2,1)} %bitcast.10), calls=%async_computation.2 | async-start | bytes 4194304 | tf_op jit(solution)/shard_map/all_to_all | solution.py:248
  (24 other events, 284.6 us)

commit v2 on v0

v2 whole, which is shorter than its diff:
```python
import functools
import math

import jax
import jax.numpy as jnp
import ml_dtypes
import numpy as np
from jax import lax
from jax.experimental import pallas as pl
from jax.experimental.pallas import tpu as pltpu
from jax.sharding import Mesh, PartitionSpec as P

LAGS = 128
NF = 128
W = 256
CH = 64
COLS = 256
X, YH, Z, YL, CO = 4, 2, 8, 2, 2
NK = YH * X
NQ = YL * CO
PLANE = ("yh", "x", "yl", "co")
VMEM = 56 * 1024 * 1024
ROWS = 32
FLOPS = 3 << 32


def lag_matrix():
    out = np.zeros((LAGS, 2, NK, NQ, 2), np.float32)
    lags = np.arange(LAGS)
    step = np.float32(2.0 * math.pi / LAGS)

    def angle(f):
        return step * (lags * f % LAGS).astype(np.float32)

    for k in range(NK):
        group, side = min(k, 7 - k), int(k > 3)
        for q in range(NQ):
            for t in range(2):
                m = 2 * (side * NQ + q) + t
                if m == 0 and group == 3:
                    out[:, t, k, q, 0] = np.cos(angle(0))
                    out[:, t, k, q, 1] = np.cos(angle(64))
                else:
                    f = 16 * group + m if m else 16 * (group + 1)
                    out[:, t, k, q, 0] = np.cos(angle(f))
                    out[:, t, k, q, 1] = -np.sin(angle(f))
    return out[:, ::-1].reshape(LAGS, NK * NQ * 4).astype(ml_dtypes.bfloat16)


def whiten_kernel(t, hi_ref, x_ref, *refs):
    o_ref = refs[-1]
    hi = hi_ref[0] == 1
    for j in range(4):
        u = pl.program_id(0) * 4 + j
        x = x_ref[:, j, 0].astype(jnp.float32)
        if t == 0 and j == 0:
            take = jnp.logical_and(jnp.logical_not(hi), pl.program_id(0) == 0)
            x = jnp.where(take, refs[0][...].astype(jnp.float32), x)
        power = jnp.sum(x[0] * x[0] + x[1] * x[1], axis=-1, keepdims=True) * (1.0 / W)
        r = jnp.where(hi, 7 - u if t else lax.rem(8 - u, 8), u)
        o_ref[r] = (x * lax.rsqrt(power + 1e-06)[None]).astype(jnp.bfloat16)


def whiten(spectra, special, hi, t):
    ins = [spectra] + ([special] if t == 0 else [])
    specs = [pl.BlockSpec((2, 4, 1, CH, W), lambda i, hi_ref: (0, i, t, 0, 0))]
    if t == 0:
        specs.append(pl.BlockSpec((2, CH, W), lambda i, hi_ref: (0, 0, 0)))
    return pl.pallas_call(
        functools.partial(whiten_kernel, t),
        grid_spec=pltpu.PrefetchScalarGridSpec(
            num_scalar_prefetch=1,
            grid=(2,),
            in_specs=specs,
            out_specs=pl.BlockSpec((8, 2, CH, W), lambda i, hi_ref: (0, 0, 0, 0)),
        ),
        out_shape=jax.ShapeDtypeStruct((8, 2, CH, W), jnp.bfloat16),
        compiler_params=pltpu.CompilerParams(vmem_limit_bytes=VMEM),
        cost_estimate=pl.CostEstimate(flops=2000000, bytes_accessed=1 << 20, transcendentals=0),
        name="whiten",
    )(hi, *ins)


def plane(s, zpos):
    dist = lax.div(s + 1, 2)
    return lax.rem(zpos + 8 + jnp.where(lax.rem(s, 2) == 1, -dist, dist), 8)


def cross_kernel(first, count, z_ref, coef_ref, *refs):
    has_own = first == 0
    own, rest = refs[0:2], refs[2:]
    lows, highs = rest[:count - has_own], rest[count - has_own:2 * (count - has_own)]
    out_ref, left, base, bufs, outs, base_sem, in_sem, out_sem = refs[-8:]

    def load(j, side):
        src = (lows, highs)[side][j]
        return pltpu.make_async_copy(src, bufs.at[j, side], in_sem.at[j, side])

    def load_own(side):
        return pltpu.make_async_copy(own[side], base.at[side], base_sem.at[side])

    for side in range(2):
        load_own(side).start()
    for j in range(count - has_own):
        for side in range(2):
            load(j, side).start()
    for side in range(2):
        load_own(side).wait()
        re = base[side, :, 0].reshape(COLS, W).astype(jnp.float32)
        im = base[side, :, 1].reshape(COLS, W).astype(jnp.float32)
        for o in range(2):
            alpha = coef_ref[o * 4 + side * 2]
            beta = coef_ref[o * 4 + side * 2 + 1]
            rows = pl.ds(o * COLS, COLS)
            left[rows, side * 2 * W:side * 2 * W + W] = (alpha * re + beta * im).astype(jnp.bfloat16)
            left[rows, side * 2 * W + W:side * 2 * W + 2 * W] = (
                alpha * im - beta * re
            ).astype(jnp.bfloat16)

    def store(j):
        g = plane(j + first, z_ref[0])
        return pltpu.make_async_copy(outs.at[j], out_ref.at[g], out_sem.at[j])

    def emit(block, j):
        right = jnp.concatenate(
            [block[side, :, p].reshape(COLS, W) for side in range(2) for p in range(2)], axis=1
        )
        acc = lax.dot_general(
            left[...], right, (((1,), (1,)), ((), ())), preferred_element_type=jnp.float32
        )
        acc = (acc * (1.0 / W)).astype(jnp.bfloat16)
        for o in range(2):
            outs[j, :, o] = acc[o * COLS:(o + 1) * COLS].reshape(NQ, CH, COLS)
        store(j).start()

    if has_own:
        emit(base, 0)

    def body(j, carry):
        for side in range(2):
            pltpu.make_async_copy(own[0], bufs.at[j, side], in_sem.at[j, side]).wait()
        emit(bufs.at[j], j + has_own)
        return carry

    lax.fori_loop(0, count - has_own, body, 0)
    for j in range(count):
        store(j).wait()


def cross(zpos, coef, own, lows, highs, first, prev=None, flops=1 << 30):
    count = len(lows) + (first == 0)
    ins = [*own, *lows, *highs] + ([prev] if prev is not None else [])
    block = (NQ, 2, CH, W)
    return pl.pallas_call(
        functools.partial(cross_kernel, first, count),
        grid_spec=pltpu.PrefetchScalarGridSpec(
            num_scalar_prefetch=2,
            grid=(1,),
            in_specs=[pl.BlockSpec(memory_space=pl.ANY) for b in ins],
            out_specs=pl.BlockSpec(memory_space=pl.ANY),
            scratch_shapes=[
                pltpu.VMEM((2 * COLS, 4 * W), jnp.bfloat16),
                pltpu.VMEM((2, *block), jnp.bfloat16),
                pltpu.VMEM((len(lows), 2, *block), jnp.bfloat16),
                pltpu.VMEM((count, NQ, 2, CH, COLS), jnp.bfloat16),
                pltpu.SemaphoreType.DMA((2,)),
                pltpu.SemaphoreType.DMA((len(lows), 2)),
                pltpu.SemaphoreType.DMA((count,)),
            ],
        ),
        out_shape=jax.ShapeDtypeStruct((NK, NQ, 2, CH, COLS), jnp.bfloat16),
        input_output_aliases={} if prev is None else {len(ins) + 1: 0},
        compiler_params=pltpu.CompilerParams(vmem_limit_bytes=VMEM),
        cost_estimate=pl.CostEstimate(flops=flops, bytes_accessed=4 << 20, transcendentals=0),
        name="cross",
    )(zpos, coef, *ins)


def lags_kernel(t_ref, x1_ref, x0_ref, out_ref):
    x = jnp.concatenate([r[...].reshape(NK * NQ * 2, ROWS, COLS) for r in (x1_ref, x0_ref)])
    x = x.reshape(NK * NQ * 4, ROWS * COLS)
    y = jnp.dot(t_ref[...], x, preferred_element_type=jnp.float32) * math.sqrt(W / NF)
    out_ref[...] = y.reshape(LAGS, ROWS, COLS)


def lags(table, moved):
    n = NK * NQ * 4
    part = pl.BlockSpec((NK * NQ, 2, ROWS, COLS), lambda i: (0, 0, i, 0))
    return pl.pallas_call(
        lags_kernel,
        grid=(CH // ROWS,),
        in_specs=[pl.BlockSpec((LAGS, n), lambda i: (0, 0)), part, part],
        out_specs=pl.BlockSpec((LAGS, ROWS, COLS), lambda i: (0, i, 0)),
        out_shape=jax.ShapeDtypeStruct((LAGS, CH, COLS), jnp.float32),
        compiler_params=pltpu.CompilerParams(vmem_limit_bytes=VMEM),
        cost_estimate=pl.CostEstimate(flops=1 << 29, bytes_accessed=12 << 20, transcendentals=0),
        name="lags",
    )(table, *moved)


def shards(spectra):
    k = lax.axis_index("yh") * X + lax.axis_index("x")
    q = lax.axis_index("yl") * CO + lax.axis_index("co")
    hi = (k > 3).astype(jnp.int32).reshape(1)
    zpos = lax.axis_index("z").astype(jnp.int32).reshape(1)

    special = lax.ppermute(spectra[:, 0], ("yh", "x"), [(1, 0), (2, 1), (3, 2), (0, 3)])
    groups = [[j * NQ + i for j in (g, 7 - g) for i in range(NQ)] for g in range(4)]
    split = spectra.reshape(2, 8, 2, CH, W)

    white = {t: whiten(split, special, hi, t) for t in (1, 0)}

    def regroup(t):
        got = lax.all_to_all(
            white[t],
            PLANE, split_axis=0, concat_axis=0, tiled=True, axis_index_groups=groups,
        )
        return got[:NQ], got[NQ:]

    sin0 = -math.sin(0.0)
    sin64 = -math.sin(math.pi)
    regular = np.array([1, 0, 1, 0, 0, 1, 0, -1], np.float32)
    selfs = np.array([1, sin0, 0, 0, 0, 0, 1, sin64], np.float32)
    is_self = jnp.logical_and(k == 3, q == 0)
    coefs = {0: jnp.where(is_self, selfs, regular), 1: jnp.asarray(regular)}

    up = [(i, (i + 1) % Z) for i in range(Z)]
    dn = [((i + 1) % Z, i) for i in range(Z)]

    def ring(own):
        ups, dns = ([], []), ([], [])
        for s in range(4):
            for side in range(2):
                if s < 3 or side == 0:
                    ups[side].append(lax.ppermute(ups[side][-1] if s else own[side], "z", up))
                if s < 3 or side == 1:
                    dns[side].append(lax.ppermute(dns[side][-1] if s else own[side], "z", dn))
        return ups, dns

    table = jnp.asarray(lag_matrix())
    owns = {t: regroup(t) for t in (1, 0)}
    moved = []
    for t in (1, 0):
        own = owns[t]
        if t == 1:
            own, _ = lax.optimization_barrier((own, white[0]))
        else:
            own, _ = lax.optimization_barrier((own, (ups[1][2], near_parts)))
        ups, dns = ring(own)
        near = [(ups[i][s] if d == 0 else dns[i][s]) for i in range(2) for s in range(2) for d in range(2)]
        near_parts = parts = cross(zpos, coefs[t], own, near[:4], near[4:], 0)
        far = ([ups[0][2], dns[0][2], ups[0][3]], [ups[1][2], dns[1][2], dns[1][3]])
        parts = cross(zpos, coefs[t], own, *far, 5, parts, FLOPS if t == 0 else 1 << 29)
        parts = parts.reshape(NK * NQ, 2, CH, COLS)
        moved.append(lax.all_to_all(parts, PLANE, split_axis=0, concat_axis=0, tiled=True))
    return lags(table, moved)


def solution(mesh):
    fine = Mesh(mesh.devices.reshape(YH, X, Z, YL, CO), ("yh", "x", "z", "yl", "co"))
    return jax.shard_map(
        shards,
        mesh=fine,
        in_specs=(P(None, ("yh", "x"), ("z", "yl", "co"), None),),
        out_specs=P(None, ("z", "yl", "co"), ("yh", "x")),
        check_vma=False,
    )
```

time: 475 us -> 172 us (0.36)
  the two profiles are of different devices: /device:TPU:102 before, /device:TPU:1 now
where the time goes in v2:
time: 172 us
  starting transfers between devices  63.6 us (37%)
  blocking collectives  37.3 us (22%)
  waiting for transfers between devices  34.7 us (20%)
  Pallas kernels  31.3 us (18%)
  local copies, waits for them, and re-layouts  3.74 us (2%)
    all_to_all x1, blocking collectives, shards(): lax.all_to_all(parts, PLANE, split_axis=0, concat_axis=0, tiled=True)  37.3 us
    ppermute x14, starting transfers between devices, ring(): dns[side].append(lax.ppermute(dns[side][-1] if s else own[side], 'z', dn))  34.1 us
    ppermute x14, waiting for transfers between devices, ring(): ups[side].append(lax.ppermute(ups[side][-1] if s else own[side], 'z', up))  20.3 us
    pallas_call x4, Pallas kernels, cross(): pl.pallas_call(functools.partial(cross_kernel, first, count), grid_spec=p...  19.9 us
    all_to_all x2, starting transfers between devices, regroup(): lax.all_to_all(white[t], PLANE, split_axis=0, concat_axis=0, tiled=True,...  12.7 us
    all_to_all x1, starting transfers between devices, shards(): lax.all_to_all(parts, PLANE, split_axis=0, concat_axis=0, tiled=True)  11.4 us
    ppermute x14, waiting for transfers between devices, ring(): dns[side].append(lax.ppermute(dns[side][-1] if s else own[side], 'z', dn))  8.14 us
    pallas_call x1, Pallas kernels, lags(): pl.pallas_call(lags_kernel, grid=(CH // ROWS,), in_specs=[pl.BlockSpec((L...  7.37 us
  transfers between devices with their start and end apart: 32, of which 15 were waited for; matrix products, arithmetic and copies ran while one was open for 1% of the time, Pallas kernels for 13%

profile of v2, /device:TPU:1, one launch (start us, length us, event | category | flops | bytes accessed | tf_op | source)
XLA Modules:
  0.0 171.5 jit_solution(12701042582890701571)
XLA Ops:
  0.0 2.0 %whiten.2 = bf16[8,2,64,256]{3,2,1,0:T(8,128)(2,1)} custom-call(s32[1]{0:T(128)} %bitcast.1.hi_ref, bf16[2,8,2,64,256]{4,3,2,1,0:T(8,128)(2,1)} %bitcast.11), custom_call_target="tpu_custom_call" | custom-call | flops 2000000 | bytes 1048576 | tf_op jit(solution)/shard_map/whiten/pallas_call | solution.py:69
  2.0 8.2 %all-to-all-start = ((bf16[8,2,64,256]{3,2,1,0:T(8,128)(2,1)}), bf16[8,2,64,256]{3,2,1,0:T(8,128)(2,1)S(1)}, u32[]{:S(2)}, u32[]{:S(2)}) async-start(bf16[8,2,64,256]{3,2,1,0:T(8,128)(2,1)} %whiten.2), calls=%async_computation | async-start | bytes 1048576 | tf_op jit(solution)/shard_map/all_to_all | solution.py:214
  10.2 0.8 slice_bitcast_fusion
  11.0 2.1 %collective-permute-start = (bf16[2,64,256]{2,1,0:T(8,128)(2,1)S(1)}, bf16[2,64,256]{2,1,0:T(8,128)(2,1)S(1)}, u32[]{:S(2)}, u32[]{:S(2)}) collective-permute-start(bf16[2,64,256]{2,1,0:T(8,128)(2,1)S(1)} %slice_bitcast_fusion), channel_id=1, source_target_pairs={{32,0},{64,32},{96,64},{0,96},{33,1},{65,33},{97,65},{1,97},{34,2}... | collective-permute-start | bytes 196616 | tf_op jit(solution)/shard_map/ppermute | solution.py:207
  13.1 4.6 %collective-permute-done.refs_0_ = bf16[2,64,256]{2,1,0:T(8,128)(2,1)S(1)} collective-permute-done((bf16[2,64,256]{2,1,0:T(8,128)(2,1)S(1)}, bf16[2,64,256]{2,1,0:T(8,128)(2,1)S(1)}, u32[]{:S(2)}, u32[]{:S(2)}) %collective-permute-start) | collective-permute-done | bytes 65568 | tf_op jit(solution)/shard_map/ppermute | solution.py:207
  17.8 0.6 copy-done.20
  18.4 2.1 %whiten.3 = bf16[8,2,64,256]{3,2,1,0:T(8,128)(2,1)} custom-call(s32[1]{0:T(128)} %bitcast.1.hi_ref, bf16[2,8,2,64,256]{4,3,2,1,0:T(8,128)(2,1)} %bitcast.12, bf16[2,64,256]{2,1,0:T(8,128)(2,1)} %copy-done.20), custom_call_target="tpu_custom_call" | custom-call | flops 2000000 | bytes 1048576 | tf_op jit(solution)/shard_map/whiten/pallas_call | solution.py:69
  20.4 1.6 all-to-all-done
  22.1 1.7 collective-permute-start.1
  23.9 4.0 %collective-permute-start.11 = (bf16[4,2,64,256]{3,2,1,0:T(8,128)(2,1)S(1)}, bf16[4,2,64,256]{3,2,1,0:T(8,128)(2,1)S(1)}, u32[]{:S(2)}, u32[]{:S(2)}) collective-permute-start(bf16[4,2,64,256]{3,2,1,0:T(8,128)(2,1)S(1)} %get-tuple-element.10.refs_1_), channel_id=1, source_target_pairs={{4,0},{8,4},{12,8},{16,12},{20,16},{24,20},{28,24},{0,28},{5,1},{9... | collective-permute-start | bytes 786440 | tf_op jit(solution)/shard_map/ppermute | solution.py:237
  27.9 4.5 %all-to-all-start.2 = ((bf16[8,2,64,256]{3,2,1,0:T(8,128)(2,1)}), bf16[8,2,64,256]{3,2,1,0:T(8,128)(2,1)S(1)}, u32[]{:S(2)}, u32[]{:S(2)}) async-start(bf16[8,2,64,256]{3,2,1,0:T(8,128)(2,1)} %whiten.3), calls=%async_computation.2 | async-start | bytes 1048576 | tf_op jit(solution)/shard_map/all_to_all | solution.py:214
  32.4 3.0 %collective-permute-start.4 = (bf16[4,2,64,256]{3,2,1,0:T(8,128)(2,1)S(1)}, bf16[4,2,64,256]{3,2,1,0:T(8,128)(2,1)S(1)}, u32[]{:S(2)}, u32[]{:S(2)}) collective-permute-start(bf16[4,2,64,256]{3,2,1,0:T(8,128)(2,1)S(1)} %get-tuple-element.9.refs_0_), channel_id=1, source_target_pairs={{4,0},{8,4},{12,8},{16,12},{20,16},{24,20},{28,24},{0,28},{5,1},{9... | collective-permute-start | bytes 786440 | tf_op jit(solution)/shard_map/ppermute | solution.py:237
  35.4 2.7 %collective-permute-start.12 = (bf16[4,2,64,256]{3,2,1,0:T(8,128)(2,1)S(1)}, bf16[4,2,64,256]{3,2,1,0:T(8,128)(2,1)S(1)}, u32[]{:S(2)}, u32[]{:S(2)}) collective-permute-start(bf16[4,2,64,256]{3,2,1,0:T(8,128)(2,1)S(1)} %collective-permute-done.11.refs_7_), channel_id=1, source_target_pairs={{4,0},{8,4},{12,8},{16,12},{20,16},{24,20},{28,24},{0,28},{5,1},{9... | collective-permute-start | bytes 786440 | tf_op jit(solution)/shard_map/ppermute | solution.py:237
  38.1 1.1 collective-permute-done.8.refs_6_
  39.2 1.7 collective-permute-done.4.refs_3_
  40.9 3.4 %collective-permute-start.5 = (bf16[4,2,64,256]{3,2,1,0:T(8,128)(2,1)S(1)}, bf16[4,2,64,256]{3,2,1,0:T(8,128)(2,1)S(1)}, u32[]{:S(2)}, u32[]{:S(2)}) collective-permute-start(bf16[4,2,64,256]{3,2,1,0:T(8,128)(2,1)S(1)} %collective-permute-done.4.refs_3_), channel_id=1, source_target_pairs={{4,0},{8,4},{12,8},{16,12},{20,16},{24,20},{28,24},{0,28},{5,1},{9... | collective-permute-start | bytes 786440 | tf_op jit(solution)/shard_map/ppermute | solution.py:237
  44.3 0.7 collective-permute-done.2.refs_4_
  45.0 1.5 collective-permute-done.12.refs_9_
  46.5 3.4 %collective-permute-start.13 = (bf16[4,2,64,256]{3,2,1,0:T(8,128)(2,1)S(1)}, bf16[4,2,64,256]{3,2,1,0:T(8,128)(2,1)}, u32[]{:S(2)}, u32[]{:S(2)}) collective-permute-start(bf16[4,2,64,256]{3,2,1,0:T(8,128)(2,1)S(1)} %collective-permute-done.12.refs_9_), channel_id=1, source_target_pairs={{4,0},{8,4},{12,8},{16,12},{20,16},{24,20},{28,24},{0,28},{5,1},{9... | collective-permute-start | bytes 786440 | tf_op jit(solution)/shard_map/ppermute | solution.py:237
  50.0 0.8 collective-permute-done.9.refs_8_
  50.8 1.4 collective-permute-done.5.refs_5_
  52.2 3.4 %collective-permute-start.6 = (bf16[4,2,64,256]{3,2,1,0:T(8,128)(2,1)S(1)}, bf16[4,2,64,256]{3,2,1,0:T(8,128)(2,1)S(1)}, u32[]{:S(2)}, u32[]{:S(2)}) collective-permute-start(bf16[4,2,64,256]{3,2,1,0:T(8,128)(2,1)S(1)} %collective-permute-done.5.refs_5_), channel_id=1, source_target_pairs={{4,0},{8,4},{12,8},{16,12},{20,16},{24,20},{28,24},{0,28},{5,1},{9... | collective-permute-start | bytes 786440 | tf_op jit(solution)/shard_map/ppermute | solution.py:237
  55.6 5.5 %cross.4.refs_8_ = bf16[8,4,2,64,256]{4,3,2,1,0:T(8,128)(2,1)} custom-call(s32[1]{0:T(128)} %bitcast.z_ref, f32[8]{0:T(128)} %constant.35.clone.coef_ref, bf16[4,2,64,256]{3,2,1,0:T(8,128)(2,1)} %copy-done.2, bf16[4,2,64,256]{3,2,1,0:T(8,128)(2,1)} %copy-done.1, bf16[4,2,64,256]{3,2,1,0:T(8,128)(2,1)} %copy-done.8, bf16[4,2,64,256]{3,2,1,0:T(8,128)(2,1)} %copy-done.15, ...), custom_call_target="tpu_custom_call" | custom-call | flops 1073741824 | bytes 4194304 | tf_op jit(solution)/shard_map/cross/pallas_call | solution.py:154
  61.1 0.8 collective-permute-done.10.refs_5_
  62.0 2.7 %collective-permute-start.25 = (bf16[4,2,64,256]{3,2,1,0:T(8,128)(2,1)S(1)}, bf16[4,2,64,256]{3,2,1,0:T(8,128)(2,1)S(1)}, u32[]{:S(2)}, u32[]{:S(2)}) collective-permute-start(bf16[4,2,64,256]{3,2,1,0:T(8,128)(2,1)S(1)} %get-tuple-element.12.refs_1_), channel_id=1, source_target_pairs={{4,0},{8,4},{12,8},{16,12},{20,16},{24,20},{28,24},{0,28},{5,1},{9... | collective-permute-start | bytes 786440 | tf_op jit(solution)/shard_map/ppermute | solution.py:237
  64.7 1.4 collective-permute-start.14
  66.1 0.7 collective-permute-start.18
  66.8 3.1 %collective-permute-done.7.refs_4_ = bf16[4,2,64,256]{3,2,1,0:T(8,128)(2,1)S(1)} collective-permute-done((bf16[4,2,64,256]{3,2,1,0:T(8,128)(2,1)}, bf16[4,2,64,256]{3,2,1,0:T(8,128)(2,1)S(1)}, u32[]{:S(2)}, u32[]{:S(2)}) %collective-permute-start.7) | collective-permute-done | bytes 262176 | tf_op jit(solution)/shard_map/ppermute | solution.py:235
  69.9 5.6 %collective-permute-done.15.refs_2_ = bf16[4,2,64,256]{3,2,1,0:T(8,128)(2,1)S(1)} collective-permute-done((bf16[4,2,64,256]{3,2,1,0:T(8,128)(2,1)S(1)}, bf16[4,2,64,256]{3,2,1,0:T(8,128)(2,1)S(1)}, u32[]{:S(2)}, u32[]{:S(2)}) %collective-permute-start.15) | collective-permute-done | bytes 262176 | tf_op jit(solution)/shard_map/ppermute | solution.py:235
  75.5 2.7 %collective-permute-start.26 = (bf16[4,2,64,256]{3,2,1,0:T(8,128)(2,1)S(1)}, bf16[4,2,64,256]{3,2,1,0:T(8,128)(2,1)}, u32[]{:S(2)}, u32[]{:S(2)}) collective-permute-start(bf16[4,2,64,256]{3,2,1,0:T(8,128)(2,1)S(1)} %collective-permute-done.25.refs_7_), channel_id=1, source_target_pairs={{4,0},{8,4},{12,8},{16,12},{20,16},{24,20},{28,24},{0,28},{5,1},{9... | collective-permute-start | bytes 786440 | tf_op jit(solution)/shard_map/ppermute | solution.py:237
  78.2 0.7 copy-done.19
  78.9 4.4 %cross.5 = bf16[8,4,2,64,256]{4,3,2,1,0:T(8,128)(2,1)} custom-call(s32[1]{0:T(128)} %bitcast.z_ref, f32[8]{0:T(128)} %constant.35.clone.coef_ref, bf16[4,2,64,256]{3,2,1,0:T(8,128)(2,1)} %copy-done.2, bf16[4,2,64,256]{3,2,1,0:T(8,128)(2,1)} %copy-done.1, bf16[4,2,64,256]{3,2,1,0:T(8,128)(2,1)} %collective-permute-done.3.refs_2_, ...), custom_call_target="tpu_custom_call", output_to_operand_aliasing={{}: (10, {})} | custom-call | flops 536870912 | bytes 4194304 | tf_op jit(solution)/shard_map/cross/pallas_call | solution.py:154
  83.4 11.4 %all-to-all-start.1 = ((bf16[32,2,64,256]{3,2,1,0:T(8,128)(2,1)}), bf16[32,2,64,256]{3,2,1,0:T(8,128)(2,1)S(1)}, u32[]{:S(2)}, u32[]{:S(2)}) async-start(bf16[32,2,64,256]{3,2,1,0:T(8,128)(2,1)} %bitcast.9), calls=%async_computation.1 | async-start | bytes 4194304 | tf_op jit(solution)/shard_map/all_to_all | solution.py:255
  94.9 1.4 collective-permute-start.23
  96.4 2.6 %collective-permute-start.27 = (bf16[4,2,64,256]{3,2,1,0:T(8,128)(2,1)}, bf16[4,2,64,256]{3,2,1,0:T(8,128)(2,1)S(1)}, u32[]{:S(2)}, u32[]{:S(2)}) collective-permute-start(bf16[4,2,64,256]{3,2,1,0:T(8,128)(2,1)} %collective-permute-done.26.refs_9_), channel_id=1, source_target_pairs={{4,0},{8,4},{12,8},{16,12},{20,16},{24,20},{28,24},{0,28},{5,1},{9... | collective-permute-start | bytes 786440 | tf_op jit(solution)/shard_map/ppermute | solution.py:237
  99.0 3.5 %collective-permute-done.19.refs_5_ = bf16[4,2,64,256]{3,2,1,0:T(8,128)(2,1)S(1)} collective-permute-done((bf16[4,2,64,256]{3,2,1,0:T(8,128)(2,1)S(1)}, bf16[4,2,64,256]{3,2,1,0:T(8,128)(2,1)S(1)}, u32[]{:S(2)}, u32[]{:S(2)}) %collective-permute-start.19) | collective-permute-done | bytes 262176 | tf_op jit(solution)/shard_map/ppermute | solution.py:237
  102.6 1.4 collective-permute-start.20
  104.0 0.1 collective-permute-done.23.refs_8_
  104.1 5.6 %collective-permute-done.17.refs_2_ = bf16[4,2,64,256]{3,2,1,0:T(8,128)(2,1)S(1)} collective-permute-done((bf16[4,2,64,256]{3,2,1,0:T(8,128)(2,1)}, bf16[4,2,64,256]{3,2,1,0:T(8,128)(2,1)S(1)}, u32[]{:S(2)}, u32[]{:S(2)}) %collective-permute-start.17) | collective-permute-done | bytes 262176 | tf_op jit(solution)/shard_map/ppermute | solution.py:235
  109.7 2.7 %collective-permute-start.28 = (bf16[4,2,64,256]{3,2,1,0:T(8,128)(2,1)S(1)}, bf16[4,2,64,256]{3,2,1,0:T(8,128)(2,1)S(1)}, u32[]{:S(2)}, u32[]{:S(2)}) collective-permute-start(bf16[4,2,64,256]{3,2,1,0:T(8,128)(2,1)S(1)} %collective-permute-done.27.refs_6_), channel_id=1, source_target_pairs={{4,0},{8,4},{12,8},{16,12},{20,16},{24,20},{28,24},{0,28},{5,1},{9... | collective-permute-start | bytes 786440 | tf_op jit(solution)/shard_map/ppermute | solution.py:237
  112.4 0.5 broadcast_select_fusion.coef_ref
  112.9 5.5 %cross.6.refs_8_ = bf16[8,4,2,64,256]{4,3,2,1,0:T(8,128)(2,1)} custom-call(s32[1]{0:T(128)} %bitcast.z_ref, f32[8]{0:T(128)} %broadcast_select_fusion.coef_ref, bf16[4,2,64,256]{3,2,1,0:T(8,128)(2,1)} %copy-done.4, bf16[4,2,64,256]{3,2,1,0:T(8,128)(2,1)} %copy-done.3, bf16[4,2,64,256]{3,2,1,0:T(8,128)(2,1)} %copy-done.5, bf16[4,2,64,256]{3,2,1,0:T(8,128)(2,1)} %copy-done.7, ...), custom_call_target="tpu_custom_call" | custom-call | flops 1073741824 | bytes 4194304 | tf_op jit(solution)/shard_map/cross/pallas_call | solution.py:154
  118.4 2.5 %collective-permute-done.21.refs_4_ = bf16[4,2,64,256]{3,2,1,0:T(8,128)(2,1)S(1)} collective-permute-done((bf16[4,2,64,256]{3,2,1,0:T(8,128)(2,1)S(1)}, bf16[4,2,64,256]{3,2,1,0:T(8,128)(2,1)S(1)}, u32[]{:S(2)}, u32[]{:S(2)}) %collective-permute-start.21) | collective-permute-done | bytes 262176 | tf_op jit(solution)/shard_map/ppermute | solution.py:235
  120.9 0.7 copy-done.27
  121.6 0.7 copy-done.28
  122.3 4.5 %cross.7 = bf16[8,4,2,64,256]{4,3,2,1,0:T(8,128)(2,1)} custom-call(s32[1]{0:T(128)} %bitcast.z_ref, f32[8]{0:T(128)} %broadcast_select_fusion.coef_ref, bf16[4,2,64,256]{3,2,1,0:T(8,128)(2,1)} %copy-done.4, bf16[4,2,64,256]{3,2,1,0:T(8,128)(2,1)} %copy-done.3, bf16[4,2,64,256]{3,2,1,0:T(8,128)(2,1)} %copy-done.23, ...), custom_call_target="tpu_custom_call", output_to_operand_aliasing={{}: (10, {})} | custom-call | flops 12884901888 | bytes 4194304 | tf_op jit(solution)/shard_map/cross/pallas_call | solution.py:154
  126.8 37.3 %all_to_all.20.x0_ref = bf16[32,2,64,256]{3,2,1,0:T(8,128)(2,1)} all-to-all(bf16[32,2,64,256]{3,2,1,0:T(8,128)(2,1)} %bitcast.10), channel_id=1, replica_groups=mesh['yh'=2,'x'=4,'z'=8,'yl'=2,'co'=2] {'yh','x','yl','co'}, dimensions={0} | all-to-all | bytes 4194304 | tf_op jit(solution)/shard_map/all_to_all | solution.py:255
  164.1 7.4 %lags.1 = f32[128,64,256]{2,1,0:T(8,128)} custom-call(bf16[128,128]{1,0:T(8,128)(2,1)} %constant.36.clone.t_ref, bf16[32,2,64,256]{3,2,1,0:T(8,128)(2,1)} %copy-done, bf16[32,2,64,256]{3,2,1,0:T(8,128)(2,1)} %all_to_all.20.x0_ref), custom_call_target="tpu_custom_call" | custom-call | flops 536870912 | bytes 12582912 | tf_op jit(solution)/shard_map/lags/pallas_call | solution.py:189
  (86 shorter events, 0.4 us)
Async XLA Ops:
  2.0 20.0 %all-to-all-start = ((bf16[8,2,64,256]{3,2,1,0:T(8,128)(2,1)}), bf16[8,2,64,256]{3,2,1,0:T(8,128)(2,1)S(1)}, u32[]{:S(2)}, u32[]{:S(2)}) async-start(bf16[8,2,64,256]{3,2,1,0:T(8,128)(2,1)} %whiten.2), calls=%async_computation | async-start | bytes 1048576 | tf_op jit(solution)/shard_map/all_to_all | solution.py:214
  11.0 6.7 %collective-permute-start = (bf16[2,64,256]{2,1,0:T(8,128)(2,1)S(1)}, bf16[2,64,256]{2,1,0:T(8,128)(2,1)S(1)}, u32[]{:S(2)}, u32[]{:S(2)}) collective-permute-start(bf16[2,64,256]{2,1,0:T(8,128)(2,1)S(1)} %slice_bitcast_fusion), channel_id=1, source_target_pairs={{32,0},{64,32},{96,64},{0,96},{33,1},{65,33},{97,65},{1,97},{34,2}... | collective-permute-start | bytes 196616 | tf_op jit(solution)/shard_map/ppermute | solution.py:207
  22.1 33.5 %copy-start.1 = (bf16[4,2,64,256]{3,2,1,0:T(8,128)(2,1)}, bf16[4,2,64,256]{3,2,1,0:T(8,128)(2,1)S(1)}, u32[]{:S(2)}) copy-start(bf16[4,2,64,256]{3,2,1,0:T(8,128)(2,1)S(1)} %get-tuple-element.10.refs_1_) | copy-start | bytes 786436
  22.1 33.4 %copy-start.2 = (bf16[4,2,64,256]{3,2,1,0:T(8,128)(2,1)}, bf16[4,2,64,256]{3,2,1,0:T(8,128)(2,1)S(1)}, u32[]{:S(2)}) copy-start(bf16[4,2,64,256]{3,2,1,0:T(8,128)(2,1)S(1)} %get-tuple-element.9.refs_0_) | copy-start | bytes 786436
  22.1 13.2 %collective-permute-start.1 = (bf16[4,2,64,256]{3,2,1,0:T(8,128)(2,1)S(1)}, bf16[4,2,64,256]{3,2,1,0:T(8,128)(2,1)S(1)}, u32[]{:S(2)}, u32[]{:S(2)}) collective-permute-start(bf16[4,2,64,256]{3,2,1,0:T(8,128)(2,1)S(1)} %get-tuple-element.9.refs_0_), channel_id=1, source_target_pairs={{0,4},{4,8},{8,12},{12,16},{16,20},{20,24},{24,28},{28,0},{1,5},{5... | collective-permute-start | bytes 786440 | tf_op jit(solution)/shard_map/ppermute | solution.py:235
  23.9 11.5 %collective-permute-start.11 = (bf16[4,2,64,256]{3,2,1,0:T(8,128)(2,1)S(1)}, bf16[4,2,64,256]{3,2,1,0:T(8,128)(2,1)S(1)}, u32[]{:S(2)}, u32[]{:S(2)}) collective-permute-start(bf16[4,2,64,256]{3,2,1,0:T(8,128)(2,1)S(1)} %get-tuple-element.10.refs_1_), channel_id=1, source_target_pairs={{4,0},{8,4},{12,8},{16,12},{20,16},{24,20},{28,24},{0,28},{5,1},{9... | collective-permute-start | bytes 786440 | tf_op jit(solution)/shard_map/ppermute | solution.py:237
  27.9 11.3 %collective-permute-start.8 = (bf16[4,2,64,256]{3,2,1,0:T(8,128)(2,1)S(1)}, bf16[4,2,64,256]{3,2,1,0:T(8,128)(2,1)S(1)}, u32[]{:S(2)}, u32[]{:S(2)}) collective-permute-start(bf16[4,2,64,256]{3,2,1,0:T(8,128)(2,1)S(1)} %get-tuple-element.10.refs_1_), channel_id=1, source_target_pairs={{0,4},{4,8},{8,12},{12,16},{16,20},{20,24},{24,28},{28,0},{1,5},{5... | collective-permute-start | bytes 786440 | tf_op jit(solution)/shard_map/ppermute | solution.py:235
  27.9 22.8 %all-to-all-start.2 = ((bf16[8,2,64,256]{3,2,1,0:T(8,128)(2,1)}), bf16[8,2,64,256]{3,2,1,0:T(8,128)(2,1)S(1)}, u32[]{:S(2)}, u32[]{:S(2)}) async-start(bf16[8,2,64,256]{3,2,1,0:T(8,128)(2,1)} %whiten.3), calls=%async_computation.2 | async-start | bytes 1048576 | tf_op jit(solution)/shard_map/all_to_all | solution.py:214
  32.4 8.5 %collective-permute-start.4 = (bf16[4,2,64,256]{3,2,1,0:T(8,128)(2,1)S(1)}, bf16[4,2,64,256]{3,2,1,0:T(8,128)(2,1)S(1)}, u32[]{:S(2)}, u32[]{:S(2)}) collective-permute-start(bf16[4,2,64,256]{3,2,1,0:T(8,128)(2,1)S(1)} %get-tuple-element.9.refs_0_), channel_id=1, source_target_pairs={{4,0},{8,4},{12,8},{16,12},{20,16},{24,20},{28,24},{0,28},{5,1},{9... | collective-permute-start | bytes 786440 | tf_op jit(solution)/shard_map/ppermute | solution.py:237
  35.4 20.2 %copy-start.8 = (bf16[4,2,64,256]{3,2,1,0:T(8,128)(2,1)}, bf16[4,2,64,256]{3,2,1,0:T(8,128)(2,1)S(1)}, u32[]{:S(2)}) copy-start(bf16[4,2,64,256]{3,2,1,0:T(8,128)(2,1)S(1)} %collective-permute-done.1.refs_2_) | copy-start | bytes 786436
  35.4 9.6 %collective-permute-start.2 = (bf16[4,2,64,256]{3,2,1,0:T(8,128)(2,1)S(1)}, bf16[4,2,64,256]{3,2,1,0:T(8,128)(2,1)S(1)}, u32[]{:S(2)}, u32[]{:S(2)}) collective-permute-start(bf16[4,2,64,256]{3,2,1,0:T(8,128)(2,1)S(1)} %collective-permute-done.1.refs_2_), channel_id=1, source_target_pairs={{0,4},{4,8},{8,12},{12,16},{16,20},{20,24},{24,28},{28,0},{1,5},{5... | collective-permute-start | bytes 786440 | tf_op jit(solution)/shard_map/ppermute | solution.py:235
  35.4 20.2 %copy-start.9 = (bf16[4,2,64,256]{3,2,1,0:T(8,128)(2,1)}, bf16[4,2,64,256]{3,2,1,0:T(8,128)(2,1)S(1)}, u32[]{:S(2)}) copy-start(bf16[4,2,64,256]{3,2,1,0:T(8,128)(2,1)S(1)} %collective-permute-done.11.refs_7_) | copy-start | bytes 786436
  35.4 11.1 %collective-permute-start.12 = (bf16[4,2,64,256]{3,2,1,0:T(8,128)(2,1)S(1)}, bf16[4,2,64,256]{3,2,1,0:T(8,128)(2,1)S(1)}, u32[]{:S(2)}, u32[]{:S(2)}) collective-permute-start(bf16[4,2,64,256]{3,2,1,0:T(8,128)(2,1)S(1)} %collective-permute-done.11.refs_7_), channel_id=1, source_target_pairs={{4,0},{8,4},{12,8},{16,12},{20,16},{24,20},{28,24},{0,28},{5,1},{9... | collective-permute-start | bytes 786440 | tf_op jit(solution)/shard_map/ppermute | solution.py:237
  39.2 16.4 %copy-start.11 = (bf16[4,2,64,256]{3,2,1,0:T(8,128)(2,1)}, bf16[4,2,64,256]{3,2,1,0:T(8,128)(2,1)S(1)}, u32[]{:S(2)}) copy-start(bf16[4,2,64,256]{3,2,1,0:T(8,128)(2,1)S(1)} %collective-permute-done.8.refs_6_) | copy-start | bytes 786436
  39.2 11.5 %collective-permute-start.9 = (bf16[4,2,64,256]{3,2,1,0:T(8,128)(2,1)S(1)}, bf16[4,2,64,256]{3,2,1,0:T(8,128)(2,1)}, u32[]{:S(2)}, u32[]{:S(2)}) collective-permute-start(bf16[4,2,64,256]{3,2,1,0:T(8,128)(2,1)S(1)} %collective-permute-done.8.refs_6_), channel_id=1, source_target_pairs={{0,4},{4,8},{8,12},{12,16},{16,20},{20,24},{24,28},{28,0},{1,5},{5... | collective-permute-start | bytes 786440 | tf_op jit(solution)/shard_map/ppermute | solution.py:235
  40.9 14.7 %copy-start.15 = (bf16[4,2,64,256]{3,2,1,0:T(8,128)(2,1)}, bf16[4,2,64,256]{3,2,1,0:T(8,128)(2,1)S(1)}, u32[]{:S(2)}) copy-start(bf16[4,2,64,256]{3,2,1,0:T(8,128)(2,1)S(1)} %collective-permute-done.4.refs_3_) | copy-start | bytes 786436
  40.9 11.2 %collective-permute-start.5 = (bf16[4,2,64,256]{3,2,1,0:T(8,128)(2,1)S(1)}, bf16[4,2,64,256]{3,2,1,0:T(8,128)(2,1)S(1)}, u32[]{:S(2)}, u32[]{:S(2)}) collective-permute-start(bf16[4,2,64,256]{3,2,1,0:T(8,128)(2,1)S(1)} %collective-permute-done.4.refs_3_), channel_id=1, source_target_pairs={{4,0},{8,4},{12,8},{16,12},{20,16},{24,20},{28,24},{0,28},{5,1},{9... | collective-permute-start | bytes 786440 | tf_op jit(solution)/shard_map/ppermute | solution.py:237
  45.0 10.6 %copy-start.16 = (bf16[4,2,64,256]{3,2,1,0:T(8,128)(2,1)}, bf16[4,2,64,256]{3,2,1,0:T(8,128)(2,1)S(1)}, u32[]{:S(2)}) copy-start(bf16[4,2,64,256]{3,2,1,0:T(8,128)(2,1)S(1)} %collective-permute-done.2.refs_4_) | copy-start | bytes 786436
  45.0 17.0 %collective-permute-start.3 = (bf16[4,2,64,256]{3,2,1,0:T(8,128)(2,1)S(1)}, bf16[4,2,64,256]{3,2,1,0:T(8,128)(2,1)}, u32[]{:S(2)}, u32[]{:S(2)}) collective-permute-start(bf16[4,2,64,256]{3,2,1,0:T(8,128)(2,1)S(1)} %collective-permute-done.2.refs_4_), channel_id=1, source_target_pairs={{0,4},{4,8},{8,12},{12,16},{16,20},{20,24},{24,28},{28,0},{1,5},{5... | collective-permute-start | bytes 786440 | tf_op jit(solution)/shard_map/ppermute | solution.py:235
  46.5 9.1 %copy-start.12 = (bf16[4,2,64,256]{3,2,1,0:T(8,128)(2,1)}, bf16[4,2,64,256]{3,2,1,0:T(8,128)(2,1)S(1)}, u32[]{:S(2)}) copy-start(bf16[4,2,64,256]{3,2,1,0:T(8,128)(2,1)S(1)} %collective-permute-done.12.refs_9_) | copy-start | bytes 786436
  46.5 18.1 %collective-permute-start.13 = (bf16[4,2,64,256]{3,2,1,0:T(8,128)(2,1)S(1)}, bf16[4,2,64,256]{3,2,1,0:T(8,128)(2,1)}, u32[]{:S(2)}, u32[]{:S(2)}) collective-permute-start(bf16[4,2,64,256]{3,2,1,0:T(8,128)(2,1)S(1)} %collective-permute-done.12.refs_9_), channel_id=1, source_target_pairs={{4,0},{8,4},{12,8},{16,12},{20,16},{24,20},{28,24},{0,28},{5,1},{9... | collective-permute-start | bytes 786440 | tf_op jit(solution)/shard_map/ppermute | solution.py:237
  50.7 11.2 %collective-permute-start.10 = (bf16[4,2,64,256]{3,2,1,0:T(8,128)(2,1)}, bf16[4,2,64,256]{3,2,1,0:T(8,128)(2,1)}, u32[]{:S(2)}, u32[]{:S(2)}) collective-permute-start(bf16[4,2,64,256]{3,2,1,0:T(8,128)(2,1)} %collective-permute-done.9.refs_8_), channel_id=1, source_target_pairs={{0,4},{4,8},{8,12},{12,16},{16,20},{20,24},{24,28},{28,0},{1,5},{5... | collective-permute-start | bytes 786440 | tf_op jit(solution)/shard_map/ppermute | solution.py:235
  50.8 15.4 %copy-start.4 = (bf16[4,2,64,256]{3,2,1,0:T(8,128)(2,1)}, bf16[4,2,64,256]{3,2,1,0:T(8,128)(2,1)S(1)}, u32[]{:S(2)}) copy-start(bf16[4,2,64,256]{3,2,1,0:T(8,128)(2,1)S(1)} %get-tuple-element.11.refs_0_) | copy-start | bytes 786436
  50.8 19.1 %copy-start.3 = (bf16[4,2,64,256]{3,2,1,0:T(8,128)(2,1)}, bf16[4,2,64,256]{3,2,1,0:T(8,128)(2,1)S(1)}, u32[]{:S(2)}) copy-start(bf16[4,2,64,256]{3,2,1,0:T(8,128)(2,1)S(1)} %get-tuple-element.12.refs_1_) | copy-start | bytes 786436
  52.2 14.0 %collective-permute-start.6 = (bf16[4,2,64,256]{3,2,1,0:T(8,128)(2,1)S(1)}, bf16[4,2,64,256]{3,2,1,0:T(8,128)(2,1)S(1)}, u32[]{:S(2)}, u32[]{:S(2)}) collective-permute-start(bf16[4,2,64,256]{3,2,1,0:T(8,128)(2,1)S(1)} %collective-permute-done.5.refs_5_), channel_id=1, source_target_pairs={{4,0},{8,4},{12,8},{16,12},{20,16},{24,20},{28,24},{0,28},{5,1},{9... | collective-permute-start | bytes 786440 | tf_op jit(solution)/shard_map/ppermute | solution.py:237
  62.0 7.9 %collective-permute-start.7 = (bf16[4,2,64,256]{3,2,1,0:T(8,128)(2,1)}, bf16[4,2,64,256]{3,2,1,0:T(8,128)(2,1)S(1)}, u32[]{:S(2)}, u32[]{:S(2)}) collective-permute-start(bf16[4,2,64,256]{3,2,1,0:T(8,128)(2,1)} %collective-permute-done.3.refs_2_), channel_id=1, source_target_pairs={{0,4},{4,8},{8,12},{12,16},{16,20},{20,24},{24,28},{28,0},{1,5},{5... | collective-permute-start | bytes 786440 | tf_op jit(solution)/shard_map/ppermute | solution.py:235
  62.0 13.5 %collective-permute-start.15 = (bf16[4,2,64,256]{3,2,1,0:T(8,128)(2,1)S(1)}, bf16[4,2,64,256]{3,2,1,0:T(8,128)(2,1)S(1)}, u32[]{:S(2)}, u32[]{:S(2)}) collective-permute-start(bf16[4,2,64,256]{3,2,1,0:T(8,128)(2,1)S(1)} %get-tuple-element.11.refs_0_), channel_id=1, source_target_pairs={{0,4},{4,8},{8,12},{12,16},{16,20},{20,24},{24,28},{28,0},{1,5},{5... | collective-permute-start | bytes 786440 | tf_op jit(solution)/shard_map/ppermute | solution.py:235
  62.0 13.5 %collective-permute-start.25 = (bf16[4,2,64,256]{3,2,1,0:T(8,128)(2,1)S(1)}, bf16[4,2,64,256]{3,2,1,0:T(8,128)(2,1)S(1)}, u32[]{:S(2)}, u32[]{:S(2)}) collective-permute-start(bf16[4,2,64,256]{3,2,1,0:T(8,128)(2,1)S(1)} %get-tuple-element.12.refs_1_), channel_id=1, source_target_pairs={{4,0},{8,4},{12,8},{16,12},{20,16},{24,20},{28,24},{0,28},{5,1},{9... | collective-permute-start | bytes 786440 | tf_op jit(solution)/shard_map/ppermute | solution.py:237
  64.7 13.5 %collective-permute-start.14 = (bf16[4,2,64,256]{3,2,1,0:T(8,128)(2,1)}, bf16[4,2,64,256]{3,2,1,0:T(8,128)(2,1)S(1)}, u32[]{:S(2)}, u32[]{:S(2)}) collective-permute-start(bf16[4,2,64,256]{3,2,1,0:T(8,128)(2,1)} %collective-permute-done.13.refs_6_), channel_id=1, source_target_pairs={{4,0},{8,4},{12,8},{16,12},{20,16},{24,20},{28,24},{0,28},{5,1},{9... | collective-permute-start | bytes 786440 | tf_op jit(solution)/shard_map/ppermute | solution.py:237
  66.1 12.1 %copy-start.17 = (bf16[4,2,64,256]{3,2,1,0:T(8,128)(2,1)}, bf16[4,2,64,256]{3,2,1,0:T(8,128)(2,1)S(1)}, u32[]{:S(2)}) copy-start(bf16[4,2,64,256]{3,2,1,0:T(8,128)(2,1)S(1)} %collective-permute-done.6.refs_3_) | copy-start | bytes 786436
  66.1 28.7 %collective-permute-start.18 = (bf16[4,2,64,256]{3,2,1,0:T(8,128)(2,1)S(1)}, bf16[4,2,64,256]{3,2,1,0:T(8,128)(2,1)S(1)}, u32[]{:S(2)}, u32[]{:S(2)}) collective-permute-start(bf16[4,2,64,256]{3,2,1,0:T(8,128)(2,1)S(1)} %get-tuple-element.11.refs_0_), channel_id=1, source_target_pairs={{4,0},{8,4},{12,8},{16,12},{20,16},{24,20},{28,24},{0,28},{5,1},{9... | collective-permute-start | bytes 786440 | tf_op jit(solution)/shard_map/ppermute | solution.py:237
  69.9 25.0 %collective-permute-start.22 = (bf16[4,2,64,256]{3,2,1,0:T(8,128)(2,1)S(1)}, bf16[4,2,64,256]{3,2,1,0:T(8,128)(2,1)}, u32[]{:S(2)}, u32[]{:S(2)}) collective-permute-start(bf16[4,2,64,256]{3,2,1,0:T(8,128)(2,1)S(1)} %get-tuple-element.12.refs_1_), channel_id=1, source_target_pairs={{0,4},{4,8},{8,12},{12,16},{16,20},{20,24},{24,28},{28,0},{1,5},{5... | collective-permute-start | bytes 786440 | tf_op jit(solution)/shard_map/ppermute | solution.py:235
  75.5 20.9 %collective-permute-start.16 = (bf16[4,2,64,256]{3,2,1,0:T(8,128)(2,1)S(1)}, bf16[4,2,64,256]{3,2,1,0:T(8,128)(2,1)}, u32[]{:S(2)}, u32[]{:S(2)}) collective-permute-start(bf16[4,2,64,256]{3,2,1,0:T(8,128)(2,1)S(1)} %collective-permute-done.15.refs_2_), channel_id=1, source_target_pairs={{0,4},{4,8},{8,12},{12,16},{16,20},{20,24},{24,28},{28,0},{1,5},{5... | collective-permute-start | bytes 786440 | tf_op jit(solution)/shard_map/ppermute | solution.py:235
  75.5 20.9 %collective-permute-start.26 = (bf16[4,2,64,256]{3,2,1,0:T(8,128)(2,1)S(1)}, bf16[4,2,64,256]{3,2,1,0:T(8,128)(2,1)}, u32[]{:S(2)}, u32[]{:S(2)}) collective-permute-start(bf16[4,2,64,256]{3,2,1,0:T(8,128)(2,1)S(1)} %collective-permute-done.25.refs_7_), channel_id=1, source_target_pairs={{4,0},{8,4},{12,8},{16,12},{20,16},{24,20},{28,24},{0,28},{5,1},{9... | collective-permute-start | bytes 786440 | tf_op jit(solution)/shard_map/ppermute | solution.py:237
  83.4 29.0 %copy-start.21 = (f32[8]{0:T(128)S(1)}, f32[8]{0:T(128)}, u32[]{:S(2)}) copy-start(f32[8]{0:T(128)} %constant.35.clone.coef_ref) | copy-start | bytes 100
  83.4 29.0 %copy-start.22 = (f32[8]{0:T(128)S(1)}, f32[8]{0:T(128)}, u32[]{:S(2)}) copy-start(f32[8]{0:T(128)} %constant.34.clone) | copy-start | bytes 100
  83.4 43.4 %all-to-all-start.1 = ((bf16[32,2,64,256]{3,2,1,0:T(8,128)(2,1)}), bf16[32,2,64,256]{3,2,1,0:T(8,128)(2,1)S(1)}, u32[]{:S(2)}, u32[]{:S(2)}) async-start(bf16[32,2,64,256]{3,2,1,0:T(8,128)(2,1)} %bitcast.9), calls=%async_computation.1 | async-start | bytes 4194304 | tf_op jit(solution)/shard_map/all_to_all | solution.py:255
  94.8 18.1 %copy-start.7 = (bf16[4,2,64,256]{3,2,1,0:T(8,128)(2,1)}, bf16[4,2,64,256]{3,2,1,0:T(8,128)(2,1)S(1)}, u32[]{:S(2)}) copy-start(bf16[4,2,64,256]{3,2,1,0:T(8,128)(2,1)S(1)} %collective-permute-done.18.refs_3_) | copy-start | bytes 786436
  94.8 7.8 %collective-permute-start.19 = (bf16[4,2,64,256]{3,2,1,0:T(8,128)(2,1)S(1)}, bf16[4,2,64,256]{3,2,1,0:T(8,128)(2,1)S(1)}, u32[]{:S(2)}, u32[]{:S(2)}) collective-permute-start(bf16[4,2,64,256]{3,2,1,0:T(8,128)(2,1)S(1)} %collective-permute-done.18.refs_3_), channel_id=1, source_target_pairs={{4,0},{8,4},{12,8},{16,12},{20,16},{24,20},{28,24},{0,28},{5,1},{9... | collective-permute-start | bytes 786440 | tf_op jit(solution)/shard_map/ppermute | solution.py:237
  94.9 9.2 %collective-permute-start.23 = (bf16[4,2,64,256]{3,2,1,0:T(8,128)(2,1)}, bf16[4,2,64,256]{3,2,1,0:T(8,128)(2,1)S(1)}, u32[]{:S(2)}, u32[]{:S(2)}) collective-permute-start(bf16[4,2,64,256]{3,2,1,0:T(8,128)(2,1)} %collective-permute-done.22.refs_6_), channel_id=1, source_target_pairs={{0,4},{4,8},{8,12},{12,16},{16,20},{20,24},{24,28},{28,0},{1,5},{5... | collective-permute-start | bytes 786440 | tf_op jit(solution)/shard_map/ppermute | solution.py:235
  96.4 13.3 %collective-permute-start.17 = (bf16[4,2,64,256]{3,2,1,0:T(8,128)(2,1)}, bf16[4,2,64,256]{3,2,1,0:T(8,128)(2,1)S(1)}, u32[]{:S(2)}, u32[]{:S(2)}) collective-permute-start(bf16[4,2,64,256]{3,2,1,0:T(8,128)(2,1)} %collective-permute-done.16.refs_4_), channel_id=1, source_target_pairs={{0,4},{4,8},{8,12},{12,16},{16,20},{20,24},{24,28},{28,0},{1,5},{5... | collective-permute-start | bytes 786440 | tf_op jit(solution)/shard_map/ppermute | solution.py:235
  96.4 13.2 %collective-permute-start.27 = (bf16[4,2,64,256]{3,2,1,0:T(8,128)(2,1)}, bf16[4,2,64,256]{3,2,1,0:T(8,128)(2,1)S(1)}, u32[]{:S(2)}, u32[]{:S(2)}) collective-permute-start(bf16[4,2,64,256]{3,2,1,0:T(8,128)(2,1)} %collective-permute-done.26.refs_9_), channel_id=1, source_target_pairs={{4,0},{8,4},{12,8},{16,12},{20,16},{24,20},{28,24},{0,28},{5,1},{9... | collective-permute-start | bytes 786440 | tf_op jit(solution)/shard_map/ppermute | solution.py:237
  102.6 10.4 %copy-start.10 = (bf16[4,2,64,256]{3,2,1,0:T(8,128)(2,1)}, bf16[4,2,64,256]{3,2,1,0:T(8,128)(2,1)S(1)}, u32[]{:S(2)}) copy-start(bf16[4,2,64,256]{3,2,1,0:T(8,128)(2,1)S(1)} %collective-permute-done.19.refs_5_) | copy-start | bytes 786436
  102.6 15.8 %collective-permute-start.20 = (bf16[4,2,64,256]{3,2,1,0:T(8,128)(2,1)S(1)}, bf16[4,2,64,256]{3,2,1,0:T(8,128)(2,1)S(1)}, u32[]{:S(2)}, u32[]{:S(2)}) collective-permute-start(bf16[4,2,64,256]{3,2,1,0:T(8,128)(2,1)S(1)} %collective-permute-done.19.refs_5_), channel_id=1, source_target_pairs={{4,0},{8,4},{12,8},{16,12},{20,16},{24,20},{28,24},{0,28},{5,1},{9... | collective-permute-start | bytes 786440 | tf_op jit(solution)/shard_map/ppermute | solution.py:237
  104.1 14.4 %collective-permute-start.24 = (bf16[4,2,64,256]{3,2,1,0:T(8,128)(2,1)S(1)}, bf16[4,2,64,256]{3,2,1,0:T(8,128)(2,1)S(1)}, u32[]{:S(2)}, u32[]{:S(2)}) collective-permute-start(bf16[4,2,64,256]{3,2,1,0:T(8,128)(2,1)S(1)} %collective-permute-done.23.refs_8_), channel_id=1, source_target_pairs={{0,4},{4,8},{8,12},{12,16},{16,20},{20,24},{24,28},{28,0},{1,5},{5... | collective-permute-start | bytes 786440 | tf_op jit(solution)/shard_map/ppermute | solution.py:235
  109.7 11.2 %collective-permute-start.21 = (bf16[4,2,64,256]{3,2,1,0:T(8,128)(2,1)S(1)}, bf16[4,2,64,256]{3,2,1,0:T(8,128)(2,1)S(1)}, u32[]{:S(2)}, u32[]{:S(2)}) collective-permute-start(bf16[4,2,64,256]{3,2,1,0:T(8,128)(2,1)S(1)} %collective-permute-done.17.refs_2_), channel_id=1, source_target_pairs={{0,4},{4,8},{8,12},{12,16},{16,20},{20,24},{24,28},{28,0},{1,5},{5... | collective-permute-start | bytes 786440 | tf_op jit(solution)/shard_map/ppermute | solution.py:235
  109.7 11.2 %collective-permute-start.28 = (bf16[4,2,64,256]{3,2,1,0:T(8,128)(2,1)S(1)}, bf16[4,2,64,256]{3,2,1,0:T(8,128)(2,1)S(1)}, u32[]{:S(2)}, u32[]{:S(2)}) collective-permute-start(bf16[4,2,64,256]{3,2,1,0:T(8,128)(2,1)S(1)} %collective-permute-done.27.refs_6_), channel_id=1, source_target_pairs={{4,0},{8,4},{12,8},{16,12},{20,16},{24,20},{28,24},{0,28},{5,1},{9... | collective-permute-start | bytes 786440 | tf_op jit(solution)/shard_map/ppermute | solution.py:237
  126.8 37.3 %copy-start = (bf16[32,2,64,256]{3,2,1,0:T(8,128)(2,1)}, bf16[32,2,64,256]{3,2,1,0:T(8,128)(2,1)S(1)}, u32[]{:S(2)}) copy-start(bf16[32,2,64,256]{3,2,1,0:T(8,128)(2,1)S(1)} %all-to-all-done.1.x1_ref) | copy-start | bytes 6291460
  (13 other events, 61.5 us)

commit v3 on v2

--- a/solution.py
+++ b/solution.py
@@ -19,7 +19,7 @@
 NK = YH * X
 NQ = YL * CO
 PLANE = ("yh", "x", "yl", "co")
-VMEM = 56 * 1024 * 1024
+VMEM = 20 * 1024 * 1024
 ROWS = 32
 FLOPS = 3 << 32
 
@@ -227,9 +227,11 @@
     up = [(i, (i + 1) % Z) for i in range(Z)]
     dn = [((i + 1) % Z, i) for i in range(Z)]
 
-    def ring(own):
+    def ring(own, before=None):
         ups, dns = ([], []), ([], [])
         for s in range(4):
+            if s == 1 and before is not None:
+                ups, dns = jax.tree.map(lambda v: lax.optimization_barrier((v, before))[0], (ups, dns))
             for side in range(2):
                 if s < 3 or side == 0:
                     ups[side].append(lax.ppermute(ups[side][-1] if s else own[side], "z", up))
@@ -238,15 +240,15 @@
         return ups, dns
 
     table = jnp.asarray(lag_matrix())
-    owns = {t: regroup(t) for t in (1, 0)}
     moved = []
     for t in (1, 0):
-        own = owns[t]
         if t == 1:
-            own, _ = lax.optimization_barrier((own, white[0]))
+            own, _ = lax.optimization_barrier((regroup(t), white[0]))
         else:
+            white[0], _ = lax.optimization_barrier((white[0], ups[0][0]))
+            own = regroup(t)
             own, _ = lax.optimization_barrier((own, (ups[1][2], near_parts)))
-        ups, dns = ring(own)
+        ups, dns = ring(own, parts if t == 0 else None)
         near = [(ups[i][s] if d == 0 else dns[i][s]) for i in range(2) for s in range(2) for d in range(2)]
         near_parts = parts = cross(zpos, coefs[t], own, near[:4], near[4:], 0)
         far = ([ups[0][2], dns[0][2], ups[0][3]], [ups[1][2], dns[1][2], dns[1][3]])

time: 172 us -> 163 us (0.948)
  Pallas kernels: 31.3 us -> 23.8 us
  local copies, waits for them, and re-layouts: 3.74 us -> 10.6 us
  waiting for transfers between devices: 34.7 us -> 28 us
    unnamed x58 -> x30, local copies, waits for them, and re-layouts: 2.81 us -> 9.5 us
    ppermute x14, waiting for transfers between devices: 20.3 us -> 14.6 us  [ring(): ups[side].append(lax.ppermute(ups[side][-1] if s else own[side], 'z', up))]
    pallas_call x4, Pallas kernels: 19.9 us -> 14.5 us  [cross(): pl.pallas_call(functools.partial(cross_kernel, first, count), grid_spec=p...]
    ppermute x14, starting transfers between devices: 34.1 us -> 30.2 us  [ring(): dns[side].append(lax.ppermute(dns[side][-1] if s else own[side], 'z', dn))]
    ppermute x14, waiting for transfers between devices: 8.14 us -> 4.8 us  [ring(): dns[side].append(lax.ppermute(dns[side][-1] if s else own[side], 'z', dn))]
    all_to_all x2, starting transfers between devices: 12.7 us -> 15.4 us  [regroup(): lax.all_to_all(white[t], PLANE, split_axis=0, concat_axis=0, tiled=True,...]
    pallas_call x2, Pallas kernels: 4.1 us -> 2.27 us  [whiten(): pl.pallas_call(functools.partial(whiten_kernel, t), grid_spec=pltpu.Prefe...]
    ppermute x14, starting transfers between devices: 3.28 us -> 5.06 us  [ring(): ups[side].append(lax.ppermute(ups[side][-1] if s else own[side], 'z', up))]
  transfers between devices with their start and end apart: 32 -> 32, of which waited for: 15 -> 9; matrix products, arithmetic and copies ran while one was open for 1% -> 1% of each run, Pallas kernels for 13% -> 10%
where the time goes in v3:
time: 163 us
  starting transfers between devices  62.9 us (39%)
  blocking collectives  37.3 us (23%)
  waiting for transfers between devices  28 us (17%)
  Pallas kernels  23.8 us (15%)
  local copies, waits for them, and re-layouts  10.6 us (7%)
    all_to_all x1, blocking collectives, shards(): lax.all_to_all(parts, PLANE, split_axis=0, concat_axis=0, tiled=True)  37.3 us
    ppermute x14, starting transfers between devices, ring(): dns[side].append(lax.ppermute(dns[side][-1] if s else own[side], 'z', dn))  30.2 us
    all_to_all x2, starting transfers between devices, regroup(): lax.all_to_all(white[t], PLANE, split_axis=0, concat_axis=0, tiled=True,...  15.4 us
    ppermute x14, waiting for transfers between devices, ring(): ups[side].append(lax.ppermute(ups[side][-1] if s else own[side], 'z', up))  14.6 us
    pallas_call x4, Pallas kernels, cross(): pl.pallas_call(functools.partial(cross_kernel, first, count), grid_spec=p...  14.5 us
    all_to_all x1, starting transfers between devices, shards(): lax.all_to_all(parts, PLANE, split_axis=0, concat_axis=0, tiled=True)  10.1 us
    unnamed x30, local copies, waits for them, and re-layouts  9.5 us
    pallas_call x1, Pallas kernels, lags(): pl.pallas_call(lags_kernel, grid=(CH // ROWS,), in_specs=[pl.BlockSpec((L...  7.05 us
  transfers between devices with their start and end apart: 32, of which 9 were waited for; matrix products, arithmetic and copies ran while one was open for 1% of the time, Pallas kernels for 10%

profile of v3, /device:TPU:1, one launch (start us, length us, event | category | flops | bytes accessed | tf_op | source)
XLA Modules:
  0.0 162.7 jit_solution(16274784994565570327)
XLA Ops:
  0.0 1.2 copy-done
  1.2 1.1 whiten.2
  2.4 8.2 %all-to-all-start = ((bf16[8,2,64,256]{3,2,1,0:T(8,128)(2,1)}), bf16[8,2,64,256]{3,2,1,0:T(8,128)(2,1)S(1)}, u32[]{:S(2)}, u32[]{:S(2)}) async-start(bf16[8,2,64,256]{3,2,1,0:T(8,128)(2,1)} %whiten.2), calls=%async_computation | async-start | bytes 1048576 | tf_op jit(solution)/shard_map/all_to_all | solution.py:214
  10.5 2.1 %collective-permute-start = (bf16[2,64,256]{2,1,0:T(8,128)(2,1)S(1)}, bf16[2,64,256]{2,1,0:T(8,128)(2,1)S(1)}, u32[]{:S(2)}, u32[]{:S(2)}) collective-permute-start(bf16[2,64,256]{2,1,0:T(8,128)(2,1)S(1)} %slice_bitcast_fusion), channel_id=1, source_target_pairs={{32,0},{64,32},{96,64},{0,96},{33,1},{65,33},{97,65},{1,97},{34,2}... | collective-permute-start | bytes 196616 | tf_op jit(solution)/shard_map/ppermute | solution.py:207
  12.7 5.4 %collective-permute-done.refs_0_ = bf16[2,64,256]{2,1,0:T(8,128)(2,1)S(1)} collective-permute-done((bf16[2,64,256]{2,1,0:T(8,128)(2,1)S(1)}, bf16[2,64,256]{2,1,0:T(8,128)(2,1)S(1)}, u32[]{:S(2)}, u32[]{:S(2)}) %collective-permute-start) | collective-permute-done | bytes 65568 | tf_op jit(solution)/shard_map/ppermute | solution.py:207
  18.1 1.1 whiten.3
  19.2 3.2 %all-to-all-done = bf16[8,2,64,256]{3,2,1,0:T(8,128)(2,1)S(1)} async-done(((bf16[8,2,64,256]{3,2,1,0:T(8,128)(2,1)}), bf16[8,2,64,256]{3,2,1,0:T(8,128)(2,1)S(1)}, u32[]{:S(2)}, u32[]{:S(2)}) %all-to-all-start) | async-done | bytes 524320 | tf_op jit(solution)/shard_map/all_to_all | solution.py:214
  22.4 1.7 %collective-permute-start.1 = (bf16[4,2,64,256]{3,2,1,0:T(8,128)(2,1)S(1)}, bf16[4,2,64,256]{3,2,1,0:T(8,128)(2,1)S(1)}, u32[]{:S(2)}, u32[]{:S(2)}) collective-permute-start(bf16[4,2,64,256]{3,2,1,0:T(8,128)(2,1)S(1)} %get-tuple-element.14.refs_0_), channel_id=1, source_target_pairs={{0,4},{4,8},{8,12},{12,16},{16,20},{20,24},{24,28},{28,0},{1,5},{5... | collective-permute-start | bytes 786440 | tf_op jit(solution)/shard_map/ppermute | solution.py:237
  24.2 4.0 %collective-permute-start.11 = (bf16[4,2,64,256]{3,2,1,0:T(8,128)(2,1)S(1)}, bf16[4,2,64,256]{3,2,1,0:T(8,128)(2,1)S(1)}, u32[]{:S(2)}, u32[]{:S(2)}) collective-permute-start(bf16[4,2,64,256]{3,2,1,0:T(8,128)(2,1)S(1)} %get-tuple-element.15.refs_1_), channel_id=1, source_target_pairs={{4,0},{8,4},{12,8},{16,12},{20,16},{24,20},{28,24},{0,28},{5,1},{9... | collective-permute-start | bytes 786440 | tf_op jit(solution)/shard_map/ppermute | solution.py:239
  28.2 1.4 collective-permute-start.4
  29.7 4.2 %collective-permute-done.1.refs_2_ = bf16[4,2,64,256]{3,2,1,0:T(8,128)(2,1)S(1)} collective-permute-done((bf16[4,2,64,256]{3,2,1,0:T(8,128)(2,1)S(1)}, bf16[4,2,64,256]{3,2,1,0:T(8,128)(2,1)S(1)}, u32[]{:S(2)}, u32[]{:S(2)}) %collective-permute-start.1) | collective-permute-done | bytes 262176 | tf_op jit(solution)/shard_map/ppermute | solution.py:237
  33.9 2.7 %collective-permute-start.12 = (bf16[4,2,64,256]{3,2,1,0:T(8,128)(2,1)S(1)}, bf16[4,2,64,256]{3,2,1,0:T(8,128)(2,1)S(1)}, u32[]{:S(2)}, u32[]{:S(2)}) collective-permute-start(bf16[4,2,64,256]{3,2,1,0:T(8,128)(2,1)S(1)} %collective-permute-done.11.refs_7_), channel_id=1, source_target_pairs={{4,0},{8,4},{12,8},{16,12},{20,16},{24,20},{28,24},{0,28},{5,1},{9... | collective-permute-start | bytes 786440 | tf_op jit(solution)/shard_map/ppermute | solution.py:239
  36.6 7.2 %all-to-all-start.2 = ((bf16[8,2,64,256]{3,2,1,0:T(8,128)(2,1)}), bf16[8,2,64,256]{3,2,1,0:T(8,128)(2,1)}, u32[]{:S(2)}, u32[]{:S(2)}) async-start(bf16[8,2,64,256]{3,2,1,0:T(8,128)(2,1)} %whiten.3), calls=%async_computation.2 | async-start | bytes 1048576 | tf_op jit(solution)/shard_map/all_to_all | solution.py:214
  44.3 1.0 collective-permute-start.9
  45.4 2.6 %collective-permute-start.13 = (bf16[4,2,64,256]{3,2,1,0:T(8,128)(2,1)S(1)}, bf16[4,2,64,256]{3,2,1,0:T(8,128)(2,1)}, u32[]{:S(2)}, u32[]{:S(2)}) collective-permute-start(bf16[4,2,64,256]{3,2,1,0:T(8,128)(2,1)S(1)} %collective-permute-done.12.refs_9_), channel_id=1, source_target_pairs={{4,0},{8,4},{12,8},{16,12},{20,16},{24,20},{28,24},{0,28},{5,1},{9... | collective-permute-start | bytes 786440 | tf_op jit(solution)/shard_map/ppermute | solution.py:239
  47.9 3.5 %collective-permute-done.5.refs_5_ = bf16[4,2,64,256]{3,2,1,0:T(8,128)(2,1)S(1)} collective-permute-done((bf16[4,2,64,256]{3,2,1,0:T(8,128)(2,1)S(1)}, bf16[4,2,64,256]{3,2,1,0:T(8,128)(2,1)S(1)}, u32[]{:S(2)}, u32[]{:S(2)}) %collective-permute-start.5) | collective-permute-done | bytes 262176 | tf_op jit(solution)/shard_map/ppermute | solution.py:239
  51.5 2.5 %collective-permute-start.6 = (bf16[4,2,64,256]{3,2,1,0:T(8,128)(2,1)S(1)}, bf16[4,2,64,256]{3,2,1,0:T(8,128)(2,1)S(1)}, u32[]{:S(2)}, u32[]{:S(2)}) collective-permute-start(bf16[4,2,64,256]{3,2,1,0:T(8,128)(2,1)S(1)} %collective-permute-done.5.refs_5_), channel_id=1, source_target_pairs={{4,0},{8,4},{12,8},{16,12},{20,16},{24,20},{28,24},{0,28},{5,1},{9... | collective-permute-start | bytes 786440 | tf_op jit(solution)/shard_map/ppermute | solution.py:239
  54.0 4.1 %cross.4.refs_8_ = bf16[8,4,2,64,256]{4,3,2,1,0:T(8,128)(2,1)} custom-call(s32[1]{0:T(128)} %bitcast.z_ref, f32[8]{0:T(128)S(1)} %copy-done.13, bf16[4,2,64,256]{3,2,1,0:T(8,128)(2,1)S(1)} %get-tuple-element.14.refs_0_, bf16[4,2,64,256]{3,2,1,0:T(8,128)(2,1)S(1)} %get-tuple-element.15.refs_1_, bf16[4,2,64,256]{3,2,1,0:T(8,128)(2,1)S(1)} %collective-permute-done.1.refs_2_, ...), custom_call_target="tpu_custom_call" | custom-call | flops 1073741824 | bytes 4194304 | tf_op jit(solution)/shard_map/cross/pallas_call | solution.py:154
  58.4 2.8 %collective-permute-start.14 = (bf16[4,2,64,256]{3,2,1,0:T(8,128)(2,1)}, bf16[4,2,64,256]{3,2,1,0:T(8,128)(2,1)S(1)}, u32[]{:S(2)}, u32[]{:S(2)}) collective-permute-start(bf16[4,2,64,256]{3,2,1,0:T(8,128)(2,1)} %collective-permute-done.13.refs_6_), channel_id=1, source_target_pairs={{4,0},{8,4},{12,8},{16,12},{20,16},{24,20},{28,24},{0,28},{5,1},{9... | collective-permute-start | bytes 786440 | tf_op jit(solution)/shard_map/ppermute | solution.py:239
  61.1 1.1 fusion
  62.2 1.4 collective-permute-done.10.refs_5_
  63.6 0.7 copy-done.10
  64.3 1.5 collective-permute-start.15
  65.7 0.7 copy-done.8
  66.4 1.3 collective-permute-start.18
  67.7 1.4 collective-permute-done.7.refs_4_
  69.5 0.9 copy-done.9
  70.4 0.9 copy-done.11
  71.4 3.8 %cross.5 = bf16[8,4,2,64,256]{4,3,2,1,0:T(8,128)(2,1)} custom-call(s32[1]{0:T(128)} %bitcast.z_ref, f32[8]{0:T(128)S(1)} %copy-done.13, bf16[4,2,64,256]{3,2,1,0:T(8,128)(2,1)S(1)} %get-tuple-element.14.refs_0_, bf16[4,2,64,256]{3,2,1,0:T(8,128)(2,1)S(1)} %get-tuple-element.15.refs_1_, ...), custom_call_target="tpu_custom_call", output_to_operand_aliasing={{}: (10, {})} | custom-call | flops 536870912 | bytes 4194304 | tf_op jit(solution)/shard_map/cross/pallas_call | solution.py:154
  75.3 2.7 %collective-permute-start.26 = (bf16[4,2,64,256]{3,2,1,0:T(8,128)(2,1)S(1)}, bf16[4,2,64,256]{3,2,1,0:T(8,128)(2,1)S(1)}, u32[]{:S(2)}, u32[]{:S(2)}) collective-permute-start(bf16[4,2,64,256]{3,2,1,0:T(8,128)(2,1)S(1)} %collective-permute-done.25.refs_7_), channel_id=1, source_target_pairs={{4,0},{8,4},{12,8},{16,12},{20,16},{24,20},{28,24},{0,28},{5,1},{9... | collective-permute-start | bytes 786440 | tf_op jit(solution)/shard_map/ppermute | solution.py:239
  77.9 10.1 %all-to-all-start.1 = ((bf16[32,2,64,256]{3,2,1,0:T(8,128)(2,1)}), bf16[32,2,64,256]{3,2,1,0:T(8,128)(2,1)}, u32[]{:S(2)}, u32[]{:S(2)}) async-start(bf16[32,2,64,256]{3,2,1,0:T(8,128)(2,1)} %bitcast.4), calls=%async_computation.1 | async-start | bytes 4194304 | tf_op jit(solution)/shard_map/all_to_all | solution.py:257
  88.1 1.7 %collective-permute-start.19 = (bf16[4,2,64,256]{3,2,1,0:T(8,128)(2,1)S(1)}, bf16[4,2,64,256]{3,2,1,0:T(8,128)(2,1)}, u32[]{:S(2)}, u32[]{:S(2)}) collective-permute-start(bf16[4,2,64,256]{3,2,1,0:T(8,128)(2,1)S(1)} %collective-permute-done.18.refs_3_), channel_id=1, source_target_pairs={{4,0},{8,4},{12,8},{16,12},{20,16},{24,20},{28,24},{0,28},{5,1},{9... | collective-permute-start | bytes 786440 | tf_op jit(solution)/shard_map/ppermute | solution.py:239
  89.8 0.7 copy-done.2
  90.6 0.7 copy-done.4
  91.3 2.6 %collective-permute-start.27 = (bf16[4,2,64,256]{3,2,1,0:T(8,128)(2,1)S(1)}, bf16[4,2,64,256]{3,2,1,0:T(8,128)(2,1)}, u32[]{:S(2)}, u32[]{:S(2)}) collective-permute-start(bf16[4,2,64,256]{3,2,1,0:T(8,128)(2,1)S(1)} %collective-permute-done.26.refs_9_), channel_id=1, source_target_pairs={{4,0},{8,4},{12,8},{16,12},{20,16},{24,20},{28,24},{0,28},{5,1},{9... | collective-permute-start | bytes 786440 | tf_op jit(solution)/shard_map/ppermute | solution.py:239
  93.9 0.7 copy-done.6
  94.6 1.2 collective-permute-done.19.refs_5_
  95.8 2.9 %collective-permute-start.20 = (bf16[4,2,64,256]{3,2,1,0:T(8,128)(2,1)}, bf16[4,2,64,256]{3,2,1,0:T(8,128)(2,1)S(1)}, u32[]{:S(2)}, u32[]{:S(2)}) collective-permute-start(bf16[4,2,64,256]{3,2,1,0:T(8,128)(2,1)} %collective-permute-done.19.refs_5_), channel_id=1, source_target_pairs={{4,0},{8,4},{12,8},{16,12},{20,16},{24,20},{28,24},{0,28},{5,1},{9... | collective-permute-start | bytes 786440 | tf_op jit(solution)/shard_map/ppermute | solution.py:239
  98.7 5.3 %collective-permute-done.17.refs_2_ = bf16[4,2,64,256]{3,2,1,0:T(8,128)(2,1)} collective-permute-done((bf16[4,2,64,256]{3,2,1,0:T(8,128)(2,1)S(1)}, bf16[4,2,64,256]{3,2,1,0:T(8,128)(2,1)}, u32[]{:S(2)}, u32[]{:S(2)}) %collective-permute-start.17) | collective-permute-done | bytes 262176 | tf_op jit(solution)/shard_map/ppermute | solution.py:237
  104.0 2.7 %collective-permute-start.28 = (bf16[4,2,64,256]{3,2,1,0:T(8,128)(2,1)}, bf16[4,2,64,256]{3,2,1,0:T(8,128)(2,1)S(1)}, u32[]{:S(2)}, u32[]{:S(2)}) collective-permute-start(bf16[4,2,64,256]{3,2,1,0:T(8,128)(2,1)} %collective-permute-done.27.refs_6_), channel_id=1, source_target_pairs={{4,0},{8,4},{12,8},{16,12},{20,16},{24,20},{28,24},{0,28},{5,1},{9... | collective-permute-start | bytes 786440 | tf_op jit(solution)/shard_map/ppermute | solution.py:239
  106.7 0.9 copy-done.3
  107.6 0.9 copy-done.5
  108.6 0.9 copy-done.7
  109.5 3.5 %cross.6.refs_8_ = bf16[8,4,2,64,256]{4,3,2,1,0:T(8,128)(2,1)S(1)} custom-call(s32[1]{0:T(128)} %bitcast.z_ref, f32[8]{0:T(128)S(1)} %broadcast_select_fusion.coef_ref, bf16[4,2,64,256]{3,2,1,0:T(8,128)(2,1)S(1)} %get-tuple-element.17.refs_0_, bf16[4,2,64,256]{3,2,1,0:T(8,128)(2,1)S(1)} %get-tuple-element.18.refs_1_, ...), custom_call_target="tpu_custom_call" | custom-call | flops 1073741824 | bytes 4194304 | tf_op jit(solution)/shard_map/cross/pallas_call | solution.py:154
  113.0 2.2 %collective-permute-done.21.refs_4_ = bf16[4,2,64,256]{3,2,1,0:T(8,128)(2,1)S(1)} collective-permute-done((bf16[4,2,64,256]{3,2,1,0:T(8,128)(2,1)}, bf16[4,2,64,256]{3,2,1,0:T(8,128)(2,1)S(1)}, u32[]{:S(2)}, u32[]{:S(2)}) %collective-permute-start.21) | collective-permute-done | bytes 262176 | tf_op jit(solution)/shard_map/ppermute | solution.py:237
  115.2 3.1 %cross.7 = bf16[8,4,2,64,256]{4,3,2,1,0:T(8,128)(2,1)S(1)} custom-call(s32[1]{0:T(128)} %bitcast.z_ref, f32[8]{0:T(128)S(1)} %broadcast_select_fusion.coef_ref, bf16[4,2,64,256]{3,2,1,0:T(8,128)(2,1)S(1)} %get-tuple-element.17.refs_0_, bf16[4,2,64,256]{3,2,1,0:T(8,128)(2,1)S(1)} %get-tuple-element.18.refs_1_, ...), custom_call_target="tpu_custom_call", output_to_operand_aliasing={{}: (10, {})} | custom-call | flops 12884901888 | bytes 4194304 | tf_op jit(solution)/shard_map/cross/pallas_call | solution.py:154
  118.4 37.3 %all_to_all.20.x0_ref = bf16[32,2,64,256]{3,2,1,0:T(8,128)(2,1)S(1)} all-to-all(bf16[32,2,64,256]{3,2,1,0:T(8,128)(2,1)S(1)} %bitcast.9), channel_id=1, replica_groups=mesh['yh'=2,'x'=4,'z'=8,'yl'=2,'co'=2] {'yh','x','yl','co'}, dimensions={0} | all-to-all | bytes 4194304 | tf_op jit(solution)/shard_map/all_to_all | solution.py:257
  155.7 7.1 %lags.1 = f32[128,64,256]{2,1,0:T(8,128)} custom-call(bf16[128,128]{1,0:T(8,128)(2,1)S(1)} %copy-done.12, bf16[32,2,64,256]{3,2,1,0:T(8,128)(2,1)} %all-to-all-done.1.x1_ref, bf16[32,2,64,256]{3,2,1,0:T(8,128)(2,1)S(1)} %all_to_all.20.x0_ref), custom_call_target="tpu_custom_call" | custom-call | flops 536870912 | bytes 12582912 | tf_op jit(solution)/shard_map/lags/pallas_call | solution.py:189
  (58 shorter events, 1.5 us)
Async XLA Ops:
  0.0 1.2 copy-start
  1.2 9.3 %copy-start.1 = (bf16[2,16,64,256]{3,2,1,0:T(8,128)(2,1)S(1)}, bf16[2,16,64,256]{3,2,1,0:T(8,128)(2,1)}, u32[]{:S(2)}) copy-start(bf16[2,16,64,256]{3,2,1,0:T(8,128)(2,1)} %param.4) | copy-start | bytes 3145732
  2.4 20.0 %all-to-all-start = ((bf16[8,2,64,256]{3,2,1,0:T(8,128)(2,1)}), bf16[8,2,64,256]{3,2,1,0:T(8,128)(2,1)S(1)}, u32[]{:S(2)}, u32[]{:S(2)}) async-start(bf16[8,2,64,256]{3,2,1,0:T(8,128)(2,1)} %whiten.2), calls=%async_computation | async-start | bytes 1048576 | tf_op jit(solution)/shard_map/all_to_all | solution.py:214
  10.5 43.5 %copy-start.13 = (f32[8]{0:T(128)S(1)}, f32[8]{0:T(128)}, u32[]{:S(2)}) copy-start(f32[8]{0:T(128)} %constant.35.clone.coef_ref) | copy-start | bytes 100
  10.5 7.5 %collective-permute-start = (bf16[2,64,256]{2,1,0:T(8,128)(2,1)S(1)}, bf16[2,64,256]{2,1,0:T(8,128)(2,1)S(1)}, u32[]{:S(2)}, u32[]{:S(2)}) collective-permute-start(bf16[2,64,256]{2,1,0:T(8,128)(2,1)S(1)} %slice_bitcast_fusion), channel_id=1, source_target_pairs={{32,0},{64,32},{96,64},{0,96},{33,1},{65,33},{97,65},{1,97},{34,2}... | collective-permute-start | bytes 196616 | tf_op jit(solution)/shard_map/ppermute | solution.py:207
  22.4 11.5 %collective-permute-start.1 = (bf16[4,2,64,256]{3,2,1,0:T(8,128)(2,1)S(1)}, bf16[4,2,64,256]{3,2,1,0:T(8,128)(2,1)S(1)}, u32[]{:S(2)}, u32[]{:S(2)}) collective-permute-start(bf16[4,2,64,256]{3,2,1,0:T(8,128)(2,1)S(1)} %get-tuple-element.14.refs_0_), channel_id=1, source_target_pairs={{0,4},{4,8},{8,12},{12,16},{16,20},{20,24},{24,28},{28,0},{1,5},{5... | collective-permute-start | bytes 786440 | tf_op jit(solution)/shard_map/ppermute | solution.py:237
  24.2 9.8 %collective-permute-start.11 = (bf16[4,2,64,256]{3,2,1,0:T(8,128)(2,1)S(1)}, bf16[4,2,64,256]{3,2,1,0:T(8,128)(2,1)S(1)}, u32[]{:S(2)}, u32[]{:S(2)}) collective-permute-start(bf16[4,2,64,256]{3,2,1,0:T(8,128)(2,1)S(1)} %get-tuple-element.15.refs_1_), channel_id=1, source_target_pairs={{4,0},{8,4},{12,8},{16,12},{20,16},{24,20},{28,24},{0,28},{5,1},{9... | collective-permute-start | bytes 786440 | tf_op jit(solution)/shard_map/ppermute | solution.py:239
  28.2 15.6 %collective-permute-start.4 = (bf16[4,2,64,256]{3,2,1,0:T(8,128)(2,1)S(1)}, bf16[4,2,64,256]{3,2,1,0:T(8,128)(2,1)S(1)}, u32[]{:S(2)}, u32[]{:S(2)}) collective-permute-start(bf16[4,2,64,256]{3,2,1,0:T(8,128)(2,1)S(1)} %get-tuple-element.14.refs_0_), channel_id=1, source_target_pairs={{4,0},{8,4},{12,8},{16,12},{20,16},{24,20},{28,24},{0,28},{5,1},{9... | collective-permute-start | bytes 786440 | tf_op jit(solution)/shard_map/ppermute | solution.py:239
  29.6 14.7 %collective-permute-start.8 = (bf16[4,2,64,256]{3,2,1,0:T(8,128)(2,1)S(1)}, bf16[4,2,64,256]{3,2,1,0:T(8,128)(2,1)S(1)}, u32[]{:S(2)}, u32[]{:S(2)}) collective-permute-start(bf16[4,2,64,256]{3,2,1,0:T(8,128)(2,1)S(1)} %get-tuple-element.15.refs_1_), channel_id=1, source_target_pairs={{0,4},{4,8},{8,12},{12,16},{16,20},{20,24},{24,28},{28,0},{1,5},{5... | collective-permute-start | bytes 786440 | tf_op jit(solution)/shard_map/ppermute | solution.py:237
  33.9 11.4 %collective-permute-start.2 = (bf16[4,2,64,256]{3,2,1,0:T(8,128)(2,1)S(1)}, bf16[4,2,64,256]{3,2,1,0:T(8,128)(2,1)S(1)}, u32[]{:S(2)}, u32[]{:S(2)}) collective-permute-start(bf16[4,2,64,256]{3,2,1,0:T(8,128)(2,1)S(1)} %collective-permute-done.1.refs_2_), channel_id=1, source_target_pairs={{0,4},{4,8},{8,12},{12,16},{16,20},{20,24},{24,28},{28,0},{1,5},{5... | collective-permute-start | bytes 786440 | tf_op jit(solution)/shard_map/ppermute | solution.py:237
  33.9 11.4 %collective-permute-start.12 = (bf16[4,2,64,256]{3,2,1,0:T(8,128)(2,1)S(1)}, bf16[4,2,64,256]{3,2,1,0:T(8,128)(2,1)S(1)}, u32[]{:S(2)}, u32[]{:S(2)}) collective-permute-start(bf16[4,2,64,256]{3,2,1,0:T(8,128)(2,1)S(1)} %collective-permute-done.11.refs_7_), channel_id=1, source_target_pairs={{4,0},{8,4},{12,8},{16,12},{20,16},{24,20},{28,24},{0,28},{5,1},{9... | collective-permute-start | bytes 786440 | tf_op jit(solution)/shard_map/ppermute | solution.py:239
  36.6 24.5 %all-to-all-start.2 = ((bf16[8,2,64,256]{3,2,1,0:T(8,128)(2,1)}), bf16[8,2,64,256]{3,2,1,0:T(8,128)(2,1)}, u32[]{:S(2)}, u32[]{:S(2)}) async-start(bf16[8,2,64,256]{3,2,1,0:T(8,128)(2,1)} %whiten.3), calls=%async_computation.2 | async-start | bytes 1048576 | tf_op jit(solution)/shard_map/all_to_all | solution.py:214
  43.8 7.7 %collective-permute-start.5 = (bf16[4,2,64,256]{3,2,1,0:T(8,128)(2,1)S(1)}, bf16[4,2,64,256]{3,2,1,0:T(8,128)(2,1)S(1)}, u32[]{:S(2)}, u32[]{:S(2)}) collective-permute-start(bf16[4,2,64,256]{3,2,1,0:T(8,128)(2,1)S(1)} %collective-permute-done.4.refs_3_), channel_id=1, source_target_pairs={{4,0},{8,4},{12,8},{16,12},{20,16},{24,20},{28,24},{0,28},{5,1},{9... | collective-permute-start | bytes 786440 | tf_op jit(solution)/shard_map/ppermute | solution.py:239
  44.3 9.7 %collective-permute-start.9 = (bf16[4,2,64,256]{3,2,1,0:T(8,128)(2,1)S(1)}, bf16[4,2,64,256]{3,2,1,0:T(8,128)(2,1)S(1)}, u32[]{:S(2)}, u32[]{:S(2)}) collective-permute-start(bf16[4,2,64,256]{3,2,1,0:T(8,128)(2,1)S(1)} %collective-permute-done.8.refs_6_), channel_id=1, source_target_pairs={{0,4},{4,8},{8,12},{12,16},{16,20},{20,24},{24,28},{28,0},{1,5},{5... | collective-permute-start | bytes 786440 | tf_op jit(solution)/shard_map/ppermute | solution.py:237
  45.3 12.8 %collective-permute-start.3 = (bf16[4,2,64,256]{3,2,1,0:T(8,128)(2,1)S(1)}, bf16[4,2,64,256]{3,2,1,0:T(8,128)(2,1)}, u32[]{:S(2)}, u32[]{:S(2)}) collective-permute-start(bf16[4,2,64,256]{3,2,1,0:T(8,128)(2,1)S(1)} %collective-permute-done.2.refs_4_), channel_id=1, source_target_pairs={{0,4},{4,8},{8,12},{12,16},{16,20},{20,24},{24,28},{28,0},{1,5},{5... | collective-permute-start | bytes 786440 | tf_op jit(solution)/shard_map/ppermute | solution.py:237
  45.4 13.0 %collective-permute-start.13 = (bf16[4,2,64,256]{3,2,1,0:T(8,128)(2,1)S(1)}, bf16[4,2,64,256]{3,2,1,0:T(8,128)(2,1)}, u32[]{:S(2)}, u32[]{:S(2)}) collective-permute-start(bf16[4,2,64,256]{3,2,1,0:T(8,128)(2,1)S(1)} %collective-permute-done.12.refs_9_), channel_id=1, source_target_pairs={{4,0},{8,4},{12,8},{16,12},{20,16},{24,20},{28,24},{0,28},{5,1},{9... | collective-permute-start | bytes 786440 | tf_op jit(solution)/shard_map/ppermute | solution.py:239
  51.5 14.2 %collective-permute-start.6 = (bf16[4,2,64,256]{3,2,1,0:T(8,128)(2,1)S(1)}, bf16[4,2,64,256]{3,2,1,0:T(8,128)(2,1)S(1)}, u32[]{:S(2)}, u32[]{:S(2)}) collective-permute-start(bf16[4,2,64,256]{3,2,1,0:T(8,128)(2,1)S(1)} %collective-permute-done.5.refs_5_), channel_id=1, source_target_pairs={{4,0},{8,4},{12,8},{16,12},{20,16},{24,20},{28,24},{0,28},{5,1},{9... | collective-permute-start | bytes 786440 | tf_op jit(solution)/shard_map/ppermute | solution.py:239
  54.0 9.6 %collective-permute-start.10 = (bf16[4,2,64,256]{3,2,1,0:T(8,128)(2,1)S(1)}, bf16[4,2,64,256]{3,2,1,0:T(8,128)(2,1)S(1)}, u32[]{:S(2)}, u32[]{:S(2)}) collective-permute-start(bf16[4,2,64,256]{3,2,1,0:T(8,128)(2,1)S(1)} %collective-permute-done.9.refs_8_), channel_id=1, source_target_pairs={{0,4},{4,8},{8,12},{12,16},{16,20},{20,24},{24,28},{28,0},{1,5},{5... | collective-permute-start | bytes 786440 | tf_op jit(solution)/shard_map/ppermute | solution.py:237
  58.1 11.1 %collective-permute-start.7 = (bf16[4,2,64,256]{3,2,1,0:T(8,128)(2,1)}, bf16[4,2,64,256]{3,2,1,0:T(8,128)(2,1)S(1)}, u32[]{:S(2)}, u32[]{:S(2)}) collective-permute-start(bf16[4,2,64,256]{3,2,1,0:T(8,128)(2,1)} %collective-permute-done.3.refs_2_), channel_id=1, source_target_pairs={{0,4},{4,8},{8,12},{12,16},{16,20},{20,24},{24,28},{28,0},{1,5},{5... | collective-permute-start | bytes 786440 | tf_op jit(solution)/shard_map/ppermute | solution.py:237
  58.4 11.1 %collective-permute-start.14 = (bf16[4,2,64,256]{3,2,1,0:T(8,128)(2,1)}, bf16[4,2,64,256]{3,2,1,0:T(8,128)(2,1)S(1)}, u32[]{:S(2)}, u32[]{:S(2)}) collective-permute-start(bf16[4,2,64,256]{3,2,1,0:T(8,128)(2,1)} %collective-permute-done.13.refs_6_), channel_id=1, source_target_pairs={{4,0},{8,4},{12,8},{16,12},{20,16},{24,20},{28,24},{0,28},{5,1},{9... | collective-permute-start | bytes 786440 | tf_op jit(solution)/shard_map/ppermute | solution.py:239
  63.6 0.7 copy-start.10
  64.3 10.9 %collective-permute-start.25 = (bf16[4,2,64,256]{3,2,1,0:T(8,128)(2,1)S(1)}, bf16[4,2,64,256]{3,2,1,0:T(8,128)(2,1)S(1)}, u32[]{:S(2)}, u32[]{:S(2)}) collective-permute-start(bf16[4,2,64,256]{3,2,1,0:T(8,128)(2,1)S(1)} %get-tuple-element.18.refs_1_), channel_id=1, source_target_pairs={{4,0},{8,4},{12,8},{16,12},{20,16},{24,20},{28,24},{0,28},{5,1},{9... | collective-permute-start | bytes 786440 | tf_op jit(solution)/shard_map/ppermute | solution.py:239
  64.3 10.9 %collective-permute-start.15 = (bf16[4,2,64,256]{3,2,1,0:T(8,128)(2,1)S(1)}, bf16[4,2,64,256]{3,2,1,0:T(8,128)(2,1)S(1)}, u32[]{:S(2)}, u32[]{:S(2)}) collective-permute-start(bf16[4,2,64,256]{3,2,1,0:T(8,128)(2,1)S(1)} %get-tuple-element.17.refs_0_), channel_id=1, source_target_pairs={{0,4},{4,8},{8,12},{12,16},{16,20},{20,24},{24,28},{28,0},{1,5},{5... | collective-permute-start | bytes 786440 | tf_op jit(solution)/shard_map/ppermute | solution.py:237
  65.7 0.7 copy-start.8
  66.4 21.6 %collective-permute-start.18 = (bf16[4,2,64,256]{3,2,1,0:T(8,128)(2,1)S(1)}, bf16[4,2,64,256]{3,2,1,0:T(8,128)(2,1)S(1)}, u32[]{:S(2)}, u32[]{:S(2)}) collective-permute-start(bf16[4,2,64,256]{3,2,1,0:T(8,128)(2,1)S(1)} %get-tuple-element.17.refs_0_), channel_id=1, source_target_pairs={{4,0},{8,4},{12,8},{16,12},{20,16},{24,20},{28,24},{0,28},{5,1},{9... | collective-permute-start | bytes 786440 | tf_op jit(solution)/shard_map/ppermute | solution.py:239
  69.2 18.9 %collective-permute-start.22 = (bf16[4,2,64,256]{3,2,1,0:T(8,128)(2,1)S(1)}, bf16[4,2,64,256]{3,2,1,0:T(8,128)(2,1)S(1)}, u32[]{:S(2)}, u32[]{:S(2)}) collective-permute-start(bf16[4,2,64,256]{3,2,1,0:T(8,128)(2,1)S(1)} %get-tuple-element.18.refs_1_), channel_id=1, source_target_pairs={{0,4},{4,8},{8,12},{12,16},{16,20},{20,24},{24,28},{28,0},{1,5},{5... | collective-permute-start | bytes 786440 | tf_op jit(solution)/shard_map/ppermute | solution.py:237
  69.5 1.0 copy-start.9
  70.4 0.9 copy-start.11
  75.2 31.5 %copy-start.14 = (f32[8]{0:T(128)S(1)}, f32[8]{0:T(128)}, u32[]{:S(2)}) copy-start(f32[8]{0:T(128)} %constant.34.clone) | copy-start | bytes 100
  75.2 15.3 %collective-permute-start.16 = (bf16[4,2,64,256]{3,2,1,0:T(8,128)(2,1)S(1)}, bf16[4,2,64,256]{3,2,1,0:T(8,128)(2,1)S(1)}, u32[]{:S(2)}, u32[]{:S(2)}) collective-permute-start(bf16[4,2,64,256]{3,2,1,0:T(8,128)(2,1)S(1)} %collective-permute-done.15.refs_2_), channel_id=1, source_target_pairs={{0,4},{4,8},{8,12},{12,16},{16,20},{20,24},{24,28},{28,0},{1,5},{5... | collective-permute-start | bytes 786440 | tf_op jit(solution)/shard_map/ppermute | solution.py:237
  75.3 16.0 %collective-permute-start.26 = (bf16[4,2,64,256]{3,2,1,0:T(8,128)(2,1)S(1)}, bf16[4,2,64,256]{3,2,1,0:T(8,128)(2,1)S(1)}, u32[]{:S(2)}, u32[]{:S(2)}) collective-permute-start(bf16[4,2,64,256]{3,2,1,0:T(8,128)(2,1)S(1)} %collective-permute-done.25.refs_7_), channel_id=1, source_target_pairs={{4,0},{8,4},{12,8},{16,12},{20,16},{24,20},{28,24},{0,28},{5,1},{9... | collective-permute-start | bytes 786440 | tf_op jit(solution)/shard_map/ppermute | solution.py:239
  77.9 40.4 %all-to-all-start.1 = ((bf16[32,2,64,256]{3,2,1,0:T(8,128)(2,1)}), bf16[32,2,64,256]{3,2,1,0:T(8,128)(2,1)}, u32[]{:S(2)}, u32[]{:S(2)}) async-start(bf16[32,2,64,256]{3,2,1,0:T(8,128)(2,1)} %bitcast.4), calls=%async_computation.1 | async-start | bytes 4194304 | tf_op jit(solution)/shard_map/all_to_all | solution.py:257
  88.1 7.8 %collective-permute-start.19 = (bf16[4,2,64,256]{3,2,1,0:T(8,128)(2,1)S(1)}, bf16[4,2,64,256]{3,2,1,0:T(8,128)(2,1)}, u32[]{:S(2)}, u32[]{:S(2)}) collective-permute-start(bf16[4,2,64,256]{3,2,1,0:T(8,128)(2,1)S(1)} %collective-permute-done.18.refs_3_), channel_id=1, source_target_pairs={{4,0},{8,4},{12,8},{16,12},{20,16},{24,20},{28,24},{0,28},{5,1},{9... | collective-permute-start | bytes 786440 | tf_op jit(solution)/shard_map/ppermute | solution.py:239
  89.8 8.9 %collective-permute-start.23 = (bf16[4,2,64,256]{3,2,1,0:T(8,128)(2,1)S(1)}, bf16[4,2,64,256]{3,2,1,0:T(8,128)(2,1)}, u32[]{:S(2)}, u32[]{:S(2)}) collective-permute-start(bf16[4,2,64,256]{3,2,1,0:T(8,128)(2,1)S(1)} %collective-permute-done.22.refs_6_), channel_id=1, source_target_pairs={{0,4},{4,8},{8,12},{12,16},{16,20},{20,24},{24,28},{28,0},{1,5},{5... | collective-permute-start | bytes 786440 | tf_op jit(solution)/shard_map/ppermute | solution.py:237
  89.8 0.7 copy-start.2
  90.5 13.5 %collective-permute-start.17 = (bf16[4,2,64,256]{3,2,1,0:T(8,128)(2,1)S(1)}, bf16[4,2,64,256]{3,2,1,0:T(8,128)(2,1)}, u32[]{:S(2)}, u32[]{:S(2)}) collective-permute-start(bf16[4,2,64,256]{3,2,1,0:T(8,128)(2,1)S(1)} %collective-permute-done.16.refs_4_), channel_id=1, source_target_pairs={{0,4},{4,8},{8,12},{12,16},{16,20},{20,24},{24,28},{28,0},{1,5},{5... | collective-permute-start | bytes 786440 | tf_op jit(solution)/shard_map/ppermute | solution.py:237
  90.6 0.7 copy-start.4
  91.3 12.7 %collective-permute-start.27 = (bf16[4,2,64,256]{3,2,1,0:T(8,128)(2,1)S(1)}, bf16[4,2,64,256]{3,2,1,0:T(8,128)(2,1)}, u32[]{:S(2)}, u32[]{:S(2)}) collective-permute-start(bf16[4,2,64,256]{3,2,1,0:T(8,128)(2,1)S(1)} %collective-permute-done.26.refs_9_), channel_id=1, source_target_pairs={{4,0},{8,4},{12,8},{16,12},{20,16},{24,20},{28,24},{0,28},{5,1},{9... | collective-permute-start | bytes 786440 | tf_op jit(solution)/shard_map/ppermute | solution.py:239
  93.9 0.7 copy-start.6
  95.8 17.2 %collective-permute-start.20 = (bf16[4,2,64,256]{3,2,1,0:T(8,128)(2,1)}, bf16[4,2,64,256]{3,2,1,0:T(8,128)(2,1)S(1)}, u32[]{:S(2)}, u32[]{:S(2)}) collective-permute-start(bf16[4,2,64,256]{3,2,1,0:T(8,128)(2,1)} %collective-permute-done.19.refs_5_), channel_id=1, source_target_pairs={{4,0},{8,4},{12,8},{16,12},{20,16},{24,20},{28,24},{0,28},{5,1},{9... | collective-permute-start | bytes 786440 | tf_op jit(solution)/shard_map/ppermute | solution.py:239
  98.7 14.3 %collective-permute-start.24 = (bf16[4,2,64,256]{3,2,1,0:T(8,128)(2,1)}, bf16[4,2,64,256]{3,2,1,0:T(8,128)(2,1)S(1)}, u32[]{:S(2)}, u32[]{:S(2)}) collective-permute-start(bf16[4,2,64,256]{3,2,1,0:T(8,128)(2,1)} %collective-permute-done.23.refs_8_), channel_id=1, source_target_pairs={{0,4},{4,8},{8,12},{12,16},{16,20},{20,24},{24,28},{28,0},{1,5},{5... | collective-permute-start | bytes 786440 | tf_op jit(solution)/shard_map/ppermute | solution.py:237
  104.0 11.2 %collective-permute-start.21 = (bf16[4,2,64,256]{3,2,1,0:T(8,128)(2,1)}, bf16[4,2,64,256]{3,2,1,0:T(8,128)(2,1)S(1)}, u32[]{:S(2)}, u32[]{:S(2)}) collective-permute-start(bf16[4,2,64,256]{3,2,1,0:T(8,128)(2,1)} %collective-permute-done.17.refs_2_), channel_id=1, source_target_pairs={{0,4},{4,8},{8,12},{12,16},{16,20},{20,24},{24,28},{28,0},{1,5},{5... | collective-permute-start | bytes 786440 | tf_op jit(solution)/shard_map/ppermute | solution.py:237
  104.0 11.2 %collective-permute-start.28 = (bf16[4,2,64,256]{3,2,1,0:T(8,128)(2,1)}, bf16[4,2,64,256]{3,2,1,0:T(8,128)(2,1)S(1)}, u32[]{:S(2)}, u32[]{:S(2)}) collective-permute-start(bf16[4,2,64,256]{3,2,1,0:T(8,128)(2,1)} %collective-permute-done.27.refs_6_), channel_id=1, source_target_pairs={{4,0},{8,4},{12,8},{16,12},{20,16},{24,20},{28,24},{0,28},{5,1},{9... | collective-permute-start | bytes 786440 | tf_op jit(solution)/shard_map/ppermute | solution.py:239
  106.7 1.0 copy-start.3
  107.6 0.9 copy-start.5
  108.6 0.9 copy-start.7
  118.4 37.3 %copy-start.12 = (bf16[128,128]{1,0:T(8,128)(2,1)S(1)}, bf16[128,128]{1,0:T(8,128)(2,1)}, u32[]{:S(2)}) copy-start(bf16[128,128]{1,0:T(8,128)(2,1)} %constant.36.clone.t_ref) | copy-start | bytes 98308

commit v4 on v3

--- a/solution.py
+++ b/solution.py
@@ -57,7 +57,10 @@
             take = jnp.logical_and(jnp.logical_not(hi), pl.program_id(0) == 0)
             x = jnp.where(take, refs[0][...].astype(jnp.float32), x)
         power = jnp.sum(x[0] * x[0] + x[1] * x[1], axis=-1, keepdims=True) * (1.0 / W)
-        r = jnp.where(hi, 7 - u if t else lax.rem(8 - u, 8), u)
+        if t:
+            r = jnp.where(hi, 3 - j, j)
+        else:
+            r = jnp.where(hi, lax.rem(8 - u, 8), u)
         o_ref[r] = (x * lax.rsqrt(power + 1e-06)[None]).astype(jnp.bfloat16)
 
 
@@ -66,16 +69,21 @@
     specs = [pl.BlockSpec((2, 4, 1, CH, W), lambda i, hi_ref: (0, i, t, 0, 0))]
     if t == 0:
         specs.append(pl.BlockSpec((2, CH, W), lambda i, hi_ref: (0, 0, 0)))
+    if t:
+        half = lambda i, hi_ref: (jnp.where(hi_ref[0] == 1, 1 - i, i), 0, 0, 0)
+        out_spec = pl.BlockSpec((4, 2, CH, W), half)
+    else:
+        out_spec = pl.BlockSpec((8, 2, CH, W), lambda i, hi_ref: (0, 0, 0, 0))
     return pl.pallas_call(
         functools.partial(whiten_kernel, t),
         grid_spec=pltpu.PrefetchScalarGridSpec(
             num_scalar_prefetch=1,
             grid=(2,),
             in_specs=specs,
-            out_specs=pl.BlockSpec((8, 2, CH, W), lambda i, hi_ref: (0, 0, 0, 0)),
+            out_specs=out_spec,
         ),
         out_shape=jax.ShapeDtypeStruct((8, 2, CH, W), jnp.bfloat16),
-        compiler_params=pltpu.CompilerParams(vmem_limit_bytes=VMEM),
+        compiler_params=pltpu.CompilerParams(vmem_limit_bytes=56 * 1024 * 1024),
         cost_estimate=pl.CostEstimate(flops=2000000, bytes_accessed=1 << 20, transcendentals=0),
         name="whiten",
     )(hi, *ins)
@@ -227,9 +235,15 @@
     up = [(i, (i + 1) % Z) for i in range(Z)]
     dn = [((i + 1) % Z, i) for i in range(Z)]
 
-    def ring(own, before=None):
+    def ring(own, before=None, t=0):
         ups, dns = ([], []), ([], [])
         for s in range(4):
+            if s == 3:
+                near = [(ups[i][n] if d == 0 else dns[i][n]) for i in range(2) for n in range(2) for d in range(2)]
+                near_parts = cross(zpos, coefs[t], own, near[:4], near[4:], 0)
+                if True:
+                    ups, dns = [list(v) for v in ups], [list(v) for v in dns]
+                    ups[0][2], dns[1][2], _ = lax.optimization_barrier((ups[0][2], dns[1][2], near_parts))
             if s == 1 and before is not None:
                 ups, dns = jax.tree.map(lambda v: lax.optimization_barrier((v, before))[0], (ups, dns))
             for side in range(2):
@@ -237,7 +251,7 @@
                     ups[side].append(lax.ppermute(ups[side][-1] if s else own[side], "z", up))
                 if s < 3 or side == 1:
                     dns[side].append(lax.ppermute(dns[side][-1] if s else own[side], "z", dn))
-        return ups, dns
+        return ups, dns, near_parts
 
     table = jnp.asarray(lag_matrix())
     moved = []
@@ -247,10 +261,9 @@
         else:
             white[0], _ = lax.optimization_barrier((white[0], ups[0][0]))
             own = regroup(t)
-            own, _ = lax.optimization_barrier((own, (ups[1][2], near_parts)))
-        ups, dns = ring(own, parts if t == 0 else None)
-        near = [(ups[i][s] if d == 0 else dns[i][s]) for i in range(2) for s in range(2) for d in range(2)]
-        near_parts = parts = cross(zpos, coefs[t], own, near[:4], near[4:], 0)
+            own, _ = lax.optimization_barrier((own, ups[1][2]))
+        ups, dns, near_parts = ring(own, parts if t == 0 else None, t)
+        parts = near_parts
         far = ([ups[0][2], dns[0][2], ups[0][3]], [ups[1][2], dns[1][2], dns[1][3]])
         parts = cross(zpos, coefs[t], own, *far, 5, parts, FLOPS if t == 0 else 1 << 29)
         parts = parts.reshape(NK * NQ, 2, CH, COLS)

time: 163 us -> 162 us (level)
  local copies, waits for them, and re-layouts: 10.6 us -> 7.61 us
    unnamed x30 -> x20, local copies, waits for them, and re-layouts: 9.5 us -> 5.64 us
    pallas_call x2, Pallas kernels: 2.27 us -> 4.01 us  [whiten(): pl.pallas_call(functools.partial(whiten_kernel, t), grid_spec=pltpu.Prefe...]
    ppermute x14, waiting for transfers between devices: 4.8 us -> 6.49 us  [ring(): dns[side].append(lax.ppermute(dns[side][-1] if s else own[side], 'z', dn))]
  transfers between devices with their start and end apart: 32 -> 32, of which waited for: 9 -> 12; matrix products, arithmetic and copies ran while one was open for 1% -> 1% of each run, Pallas kernels for 10% -> 10%
where the time goes in v4:
time: 162 us
  starting transfers between devices  62.9 us (39%)
  blocking collectives  36.7 us (23%)
  waiting for transfers between devices  29.4 us (18%)
  Pallas kernels  24.9 us (15%)
  local copies, waits for them, and re-layouts  7.61 us (5%)
    all_to_all x1, blocking collectives, shards(): lax.all_to_all(parts, PLANE, split_axis=0, concat_axis=0, tiled=True)  36.7 us
    ppermute x14, starting transfers between devices, ring(): dns[side].append(lax.ppermute(dns[side][-1] if s else own[side], 'z', dn))  30.3 us
    ppermute x14, waiting for transfers between devices, ring(): ups[side].append(lax.ppermute(ups[side][-1] if s else own[side], 'z', up))  16.1 us
    all_to_all x2, starting transfers between devices, regroup(): lax.all_to_all(white[t], PLANE, split_axis=0, concat_axis=0, tiled=True,...  15.4 us
    pallas_call x4, Pallas kernels, cross(): pl.pallas_call(functools.partial(cross_kernel, first, count), grid_spec=p...  13.9 us
    all_to_all x1, starting transfers between devices, shards(): lax.all_to_all(parts, PLANE, split_axis=0, concat_axis=0, tiled=True)  10.1 us
    pallas_call x1, Pallas kernels, lags(): pl.pallas_call(lags_kernel, grid=(CH // ROWS,), in_specs=[pl.BlockSpec((L...  7.05 us
    ppermute x14, waiting for transfers between devices, ring(): dns[side].append(lax.ppermute(dns[side][-1] if s else own[side], 'z', dn))  6.49 us
  transfers between devices with their start and end apart: 32, of which 12 were waited for; matrix products, arithmetic and copies ran while one was open for 1% of the time, Pallas kernels for 10%

profile of v4, /device:TPU:1, one launch (start us, length us, event | category | flops | bytes accessed | tf_op | source)
XLA Modules:
  0.0 161.8 jit_solution(17040573345427431909)
XLA Ops:
  0.0 1.9 %whiten.2 = bf16[8,2,64,256]{3,2,1,0:T(8,128)(2,1)} custom-call(s32[1]{0:T(128)} %bitcast.1.hi_ref, bf16[2,8,2,64,256]{4,3,2,1,0:T(8,128)(2,1)} %bitcast.10), custom_call_target="tpu_custom_call" | custom-call | flops 2000000 | bytes 1048576 | tf_op jit(solution)/shard_map/whiten/pallas_call | solution.py:77
  1.9 8.2 %all-to-all-start = ((bf16[8,2,64,256]{3,2,1,0:T(8,128)(2,1)}), bf16[8,2,64,256]{3,2,1,0:T(8,128)(2,1)S(1)}, u32[]{:S(2)}, u32[]{:S(2)}) async-start(bf16[8,2,64,256]{3,2,1,0:T(8,128)(2,1)} %whiten.2), calls=%async_computation | async-start | bytes 1048576 | tf_op jit(solution)/shard_map/all_to_all | solution.py:222
  10.1 0.9 slice_bitcast_fusion
  11.0 2.1 %collective-permute-start = (bf16[2,64,256]{2,1,0:T(8,128)(2,1)S(1)}, bf16[2,64,256]{2,1,0:T(8,128)(2,1)S(1)}, u32[]{:S(2)}, u32[]{:S(2)}) collective-permute-start(bf16[2,64,256]{2,1,0:T(8,128)(2,1)S(1)} %slice_bitcast_fusion), channel_id=1, source_target_pairs={{32,0},{64,32},{96,64},{0,96},{33,1},{65,33},{97,65},{1,97},{34,2}... | collective-permute-start | bytes 196616 | tf_op jit(solution)/shard_map/ppermute | solution.py:215
  13.1 4.6 %collective-permute-done.refs_0_ = bf16[2,64,256]{2,1,0:T(8,128)(2,1)S(1)} collective-permute-done((bf16[2,64,256]{2,1,0:T(8,128)(2,1)S(1)}, bf16[2,64,256]{2,1,0:T(8,128)(2,1)S(1)}, u32[]{:S(2)}, u32[]{:S(2)}) %collective-permute-start) | collective-permute-done | bytes 65568 | tf_op jit(solution)/shard_map/ppermute | solution.py:215
  17.7 0.6 copy-done.8
  18.3 2.1 %whiten.3 = bf16[8,2,64,256]{3,2,1,0:T(8,128)(2,1)} custom-call(s32[1]{0:T(128)} %bitcast.1.hi_ref, bf16[2,8,2,64,256]{4,3,2,1,0:T(8,128)(2,1)} %bitcast.11, bf16[2,64,256]{2,1,0:T(8,128)(2,1)} %copy-done.8), custom_call_target="tpu_custom_call" | custom-call | flops 2000000 | bytes 1048576 | tf_op jit(solution)/shard_map/whiten/pallas_call | solution.py:77
  20.3 1.6 %all-to-all-done = bf16[8,2,64,256]{3,2,1,0:T(8,128)(2,1)S(1)} async-done(((bf16[8,2,64,256]{3,2,1,0:T(8,128)(2,1)}), bf16[8,2,64,256]{3,2,1,0:T(8,128)(2,1)S(1)}, u32[]{:S(2)}, u32[]{:S(2)}) %all-to-all-start) | async-done | bytes 524320 | tf_op jit(solution)/shard_map/all_to_all | solution.py:222
  22.0 1.7 %collective-permute-start.1 = (bf16[4,2,64,256]{3,2,1,0:T(8,128)(2,1)S(1)}, bf16[4,2,64,256]{3,2,1,0:T(8,128)(2,1)S(1)}, u32[]{:S(2)}, u32[]{:S(2)}) collective-permute-start(bf16[4,2,64,256]{3,2,1,0:T(8,128)(2,1)S(1)} %get-tuple-element.18.refs_0_), channel_id=1, source_target_pairs={{0,4},{4,8},{8,12},{12,16},{16,20},{20,24},{24,28},{28,0},{1,5},{5... | collective-permute-start | bytes 786440 | tf_op jit(solution)/shard_map/ppermute | solution.py:251
  23.8 4.0 %collective-permute-start.4 = (bf16[4,2,64,256]{3,2,1,0:T(8,128)(2,1)S(1)}, bf16[4,2,64,256]{3,2,1,0:T(8,128)(2,1)S(1)}, u32[]{:S(2)}, u32[]{:S(2)}) collective-permute-start(bf16[4,2,64,256]{3,2,1,0:T(8,128)(2,1)S(1)} %get-tuple-element.19.refs_1_), channel_id=1, source_target_pairs={{4,0},{8,4},{12,8},{16,12},{20,16},{24,20},{28,24},{0,28},{5,1},{9... | collective-permute-start | bytes 786440 | tf_op jit(solution)/shard_map/ppermute | solution.py:253
  27.8 1.4 collective-permute-start.7
  29.2 4.2 %collective-permute-done.1.refs_2_ = bf16[4,2,64,256]{3,2,1,0:T(8,128)(2,1)S(1)} collective-permute-done((bf16[4,2,64,256]{3,2,1,0:T(8,128)(2,1)S(1)}, bf16[4,2,64,256]{3,2,1,0:T(8,128)(2,1)S(1)}, u32[]{:S(2)}, u32[]{:S(2)}) %collective-permute-start.1) | collective-permute-done | bytes 262176 | tf_op jit(solution)/shard_map/ppermute | solution.py:251
  33.5 2.7 %collective-permute-start.5 = (bf16[4,2,64,256]{3,2,1,0:T(8,128)(2,1)S(1)}, bf16[4,2,64,256]{3,2,1,0:T(8,128)(2,1)S(1)}, u32[]{:S(2)}, u32[]{:S(2)}) collective-permute-start(bf16[4,2,64,256]{3,2,1,0:T(8,128)(2,1)S(1)} %collective-permute-done.4.refs_7_), channel_id=1, source_target_pairs={{4,0},{8,4},{12,8},{16,12},{20,16},{24,20},{28,24},{0,28},{5,1},{9... | collective-permute-start | bytes 786440 | tf_op jit(solution)/shard_map/ppermute | solution.py:253
  36.2 7.2 %all-to-all-start.2 = ((bf16[8,2,64,256]{3,2,1,0:T(8,128)(2,1)}), bf16[8,2,64,256]{3,2,1,0:T(8,128)(2,1)}, u32[]{:S(2)}, u32[]{:S(2)}) async-start(bf16[8,2,64,256]{3,2,1,0:T(8,128)(2,1)} %whiten.3), calls=%async_computation.2 | async-start | bytes 1048576 | tf_op jit(solution)/shard_map/all_to_all | solution.py:222
  43.4 0.5 collective-permute-start.8
  43.9 1.0 collective-permute-start.10
  44.9 2.6 %collective-permute-start.6 = (bf16[4,2,64,256]{3,2,1,0:T(8,128)(2,1)S(1)}, bf16[4,2,64,256]{3,2,1,0:T(8,128)(2,1)}, u32[]{:S(2)}, u32[]{:S(2)}) collective-permute-start(bf16[4,2,64,256]{3,2,1,0:T(8,128)(2,1)S(1)} %collective-permute-done.5.refs_9_), channel_id=1, source_target_pairs={{4,0},{8,4},{12,8},{16,12},{20,16},{24,20},{28,24},{0,28},{5,1},{9... | collective-permute-start | bytes 786440 | tf_op jit(solution)/shard_map/ppermute | solution.py:253
  47.5 3.5 %collective-permute-done.8.refs_5_ = bf16[4,2,64,256]{3,2,1,0:T(8,128)(2,1)S(1)} collective-permute-done((bf16[4,2,64,256]{3,2,1,0:T(8,128)(2,1)S(1)}, bf16[4,2,64,256]{3,2,1,0:T(8,128)(2,1)S(1)}, u32[]{:S(2)}, u32[]{:S(2)}) %collective-permute-start.8) | collective-permute-done | bytes 262176 | tf_op jit(solution)/shard_map/ppermute | solution.py:253
  51.1 2.5 %collective-permute-start.11 = (bf16[4,2,64,256]{3,2,1,0:T(8,128)(2,1)S(1)}, bf16[4,2,64,256]{3,2,1,0:T(8,128)(2,1)S(1)}, u32[]{:S(2)}, u32[]{:S(2)}) collective-permute-start(bf16[4,2,64,256]{3,2,1,0:T(8,128)(2,1)S(1)} %collective-permute-done.8.refs_5_), channel_id=1, source_target_pairs={{4,0},{8,4},{12,8},{16,12},{20,16},{24,20},{28,24},{0,28},{5,1},{9... | collective-permute-start | bytes 786440 | tf_op jit(solution)/shard_map/ppermute | solution.py:253
  53.6 4.1 %cross.4.refs_8_ = bf16[8,4,2,64,256]{4,3,2,1,0:T(8,128)(2,1)} custom-call(s32[1]{0:T(128)} %bitcast.z_ref, f32[8]{0:T(128)S(1)} %copy-done.7, bf16[4,2,64,256]{3,2,1,0:T(8,128)(2,1)S(1)} %get-tuple-element.18.refs_0_, bf16[4,2,64,256]{3,2,1,0:T(8,128)(2,1)S(1)} %get-tuple-element.19.refs_1_, bf16[4,2,64,256]{3,2,1,0:T(8,128)(2,1)S(1)} %collective-permute-done.1.refs_2_, ...), custom_call_target="tpu_custom_call" | custom-call | flops 1073741824 | bytes 4194304 | tf_op jit(solution)/shard_map/cross/pallas_call | solution.py:162
  57.9 2.8 %collective-permute-start.14 = (bf16[4,2,64,256]{3,2,1,0:T(8,128)(2,1)}, bf16[4,2,64,256]{3,2,1,0:T(8,128)(2,1)S(1)}, u32[]{:S(2)}, u32[]{:S(2)}) collective-permute-start(bf16[4,2,64,256]{3,2,1,0:T(8,128)(2,1)} %collective-permute-done.6.refs_6_), channel_id=1, source_target_pairs={{4,0},{8,4},{12,8},{16,12},{20,16},{24,20},{28,24},{0,28},{5,1},{9... | collective-permute-start | bytes 786440 | tf_op jit(solution)/shard_map/ppermute | solution.py:253
  60.7 1.1 fusion
  61.8 1.4 collective-permute-done.13.refs_5_
  63.2 0.7 copy-done.4
  63.9 1.5 collective-permute-start.15
  65.3 0.7 copy-done.2
  66.1 1.3 collective-permute-start.21
  67.4 1.4 collective-permute-done.12.refs_4_
  69.1 0.9 copy-done.3
  70.0 0.9 copy-done.5
  71.0 3.8 %cross.5 = bf16[8,4,2,64,256]{4,3,2,1,0:T(8,128)(2,1)} custom-call(s32[1]{0:T(128)} %bitcast.z_ref, f32[8]{0:T(128)S(1)} %copy-done.7, bf16[4,2,64,256]{3,2,1,0:T(8,128)(2,1)S(1)} %get-tuple-element.18.refs_0_, bf16[4,2,64,256]{3,2,1,0:T(8,128)(2,1)S(1)} %get-tuple-element.19.refs_1_, ...), custom_call_target="tpu_custom_call", output_to_operand_aliasing={{}: (10, {})} | custom-call | flops 536870912 | bytes 4194304 | tf_op jit(solution)/shard_map/cross/pallas_call | solution.py:162
  74.9 2.7 %collective-permute-start.19 = (bf16[4,2,64,256]{3,2,1,0:T(8,128)(2,1)S(1)}, bf16[4,2,64,256]{3,2,1,0:T(8,128)(2,1)}, u32[]{:S(2)}, u32[]{:S(2)}) collective-permute-start(bf16[4,2,64,256]{3,2,1,0:T(8,128)(2,1)S(1)} %collective-permute-done.18.refs_7_), channel_id=1, source_target_pairs={{4,0},{8,4},{12,8},{16,12},{20,16},{24,20},{28,24},{0,28},{5,1},{9... | collective-permute-start | bytes 786440 | tf_op jit(solution)/shard_map/ppermute | solution.py:253
  77.5 10.1 %all-to-all-start.1 = ((bf16[32,2,64,256]{3,2,1,0:T(8,128)(2,1)}), bf16[32,2,64,256]{3,2,1,0:T(8,128)(2,1)}, u32[]{:S(2)}, u32[]{:S(2)}) async-start(bf16[32,2,64,256]{3,2,1,0:T(8,128)(2,1)} %bitcast.4), calls=%async_computation.1 | async-start | bytes 4194304 | tf_op jit(solution)/shard_map/all_to_all | solution.py:270
  87.7 1.7 %collective-permute-start.22 = (bf16[4,2,64,256]{3,2,1,0:T(8,128)(2,1)S(1)}, bf16[4,2,64,256]{3,2,1,0:T(8,128)(2,1)}, u32[]{:S(2)}, u32[]{:S(2)}) collective-permute-start(bf16[4,2,64,256]{3,2,1,0:T(8,128)(2,1)S(1)} %collective-permute-done.21.refs_3_), channel_id=1, source_target_pairs={{4,0},{8,4},{12,8},{16,12},{20,16},{24,20},{28,24},{0,28},{5,1},{9... | collective-permute-start | bytes 786440 | tf_op jit(solution)/shard_map/ppermute | solution.py:253
  89.4 0.7 copy-done
  90.2 2.7 %collective-permute-start.20 = (bf16[4,2,64,256]{3,2,1,0:T(8,128)(2,1)}, bf16[4,2,64,256]{3,2,1,0:T(8,128)(2,1)S(1)}, u32[]{:S(2)}, u32[]{:S(2)}) collective-permute-start(bf16[4,2,64,256]{3,2,1,0:T(8,128)(2,1)} %collective-permute-done.19.refs_9_), channel_id=1, source_target_pairs={{4,0},{8,4},{12,8},{16,12},{20,16},{24,20},{28,24},{0,28},{5,1},{9... | collective-permute-start | bytes 786440 | tf_op jit(solution)/shard_map/ppermute | solution.py:253
  92.9 2.5 %collective-permute-done.22.refs_5_ = bf16[4,2,64,256]{3,2,1,0:T(8,128)(2,1)} collective-permute-done((bf16[4,2,64,256]{3,2,1,0:T(8,128)(2,1)S(1)}, bf16[4,2,64,256]{3,2,1,0:T(8,128)(2,1)}, u32[]{:S(2)}, u32[]{:S(2)}) %collective-permute-start.22) | collective-permute-done | bytes 262176 | tf_op jit(solution)/shard_map/ppermute | solution.py:253
  95.4 2.9 %collective-permute-start.25 = (bf16[4,2,64,256]{3,2,1,0:T(8,128)(2,1)}, bf16[4,2,64,256]{3,2,1,0:T(8,128)(2,1)S(1)}, u32[]{:S(2)}, u32[]{:S(2)}) collective-permute-start(bf16[4,2,64,256]{3,2,1,0:T(8,128)(2,1)} %collective-permute-done.22.refs_5_), channel_id=1, source_target_pairs={{4,0},{8,4},{12,8},{16,12},{20,16},{24,20},{28,24},{0,28},{5,1},{9... | collective-permute-start | bytes 786440 | tf_op jit(solution)/shard_map/ppermute | solution.py:253
  98.3 0.9 copy-done.1
  99.3 3.4 %cross.6.refs_8_ = bf16[8,4,2,64,256]{4,3,2,1,0:T(8,128)(2,1)S(1)} custom-call(s32[1]{0:T(128)} %bitcast.z_ref, f32[8]{0:T(128)S(1)} %broadcast_select_fusion.coef_ref, bf16[4,2,64,256]{3,2,1,0:T(8,128)(2,1)S(1)} %get-tuple-element.23.refs_0_, bf16[4,2,64,256]{3,2,1,0:T(8,128)(2,1)S(1)} %get-tuple-element.24.refs_1_, ...), custom_call_target="tpu_custom_call" | custom-call | flops 1073741824 | bytes 4194304 | tf_op jit(solution)/shard_map/cross/pallas_call | solution.py:162
  102.7 0.9 collective-permute-done.17.refs_2_
  103.6 2.7 %collective-permute-start.28 = (bf16[4,2,64,256]{3,2,1,0:T(8,128)(2,1)S(1)}, bf16[4,2,64,256]{3,2,1,0:T(8,128)(2,1)S(1)}, u32[]{:S(2)}, u32[]{:S(2)}) collective-permute-start(bf16[4,2,64,256]{3,2,1,0:T(8,128)(2,1)S(1)} %collective-permute-done.20.refs_6_), channel_id=1, source_target_pairs={{4,0},{8,4},{12,8},{16,12},{20,16},{24,20},{28,24},{0,28},{5,1},{9... | collective-permute-start | bytes 786440 | tf_op jit(solution)/shard_map/ppermute | solution.py:253
  106.7 2.5 %collective-permute-done.27.refs_5_ = bf16[4,2,64,256]{3,2,1,0:T(8,128)(2,1)S(1)} collective-permute-done((bf16[4,2,64,256]{3,2,1,0:T(8,128)(2,1)}, bf16[4,2,64,256]{3,2,1,0:T(8,128)(2,1)S(1)}, u32[]{:S(2)}, u32[]{:S(2)}) %collective-permute-start.27) | collective-permute-done | bytes 262176 | tf_op jit(solution)/shard_map/ppermute | solution.py:251
  109.2 5.6 %collective-permute-done.26.refs_4_ = bf16[4,2,64,256]{3,2,1,0:T(8,128)(2,1)S(1)} collective-permute-done((bf16[4,2,64,256]{3,2,1,0:T(8,128)(2,1)S(1)}, bf16[4,2,64,256]{3,2,1,0:T(8,128)(2,1)S(1)}, u32[]{:S(2)}, u32[]{:S(2)}) %collective-permute-start.26) | collective-permute-done | bytes 262176 | tf_op jit(solution)/shard_map/ppermute | solution.py:251
  114.8 2.6 %cross.7 = bf16[8,4,2,64,256]{4,3,2,1,0:T(8,128)(2,1)S(1)} custom-call(s32[1]{0:T(128)} %bitcast.z_ref, f32[8]{0:T(128)S(1)} %broadcast_select_fusion.coef_ref, bf16[4,2,64,256]{3,2,1,0:T(8,128)(2,1)S(1)} %get-tuple-element.23.refs_0_, bf16[4,2,64,256]{3,2,1,0:T(8,128)(2,1)S(1)} %get-tuple-element.24.refs_1_, ...), custom_call_target="tpu_custom_call", output_to_operand_aliasing={{}: (10, {})} | custom-call | flops 12884901888 | bytes 4194304 | tf_op jit(solution)/shard_map/cross/pallas_call | solution.py:162
  117.4 0.6 all-to-all-done.1.x1_ref
  118.0 36.7 %all_to_all.20.x0_ref = bf16[32,2,64,256]{3,2,1,0:T(8,128)(2,1)S(1)} all-to-all(bf16[32,2,64,256]{3,2,1,0:T(8,128)(2,1)S(1)} %bitcast.9), channel_id=1, replica_groups=mesh['yh'=2,'x'=4,'z'=8,'yl'=2,'co'=2] {'yh','x','yl','co'}, dimensions={0} | all-to-all | bytes 4194304 | tf_op jit(solution)/shard_map/all_to_all | solution.py:270
  154.7 7.0 %lags.1 = f32[128,64,256]{2,1,0:T(8,128)} custom-call(bf16[128,128]{1,0:T(8,128)(2,1)S(1)} %copy-done.6, bf16[32,2,64,256]{3,2,1,0:T(8,128)(2,1)} %all-to-all-done.1.x1_ref, bf16[32,2,64,256]{3,2,1,0:T(8,128)(2,1)S(1)} %all_to_all.20.x0_ref), custom_call_target="tpu_custom_call" | custom-call | flops 536870912 | bytes 12582912 | tf_op jit(solution)/shard_map/lags/pallas_call | solution.py:197
  (48 shorter events, 1.4 us)
Async XLA Ops:
  1.9 20.0 %all-to-all-start = ((bf16[8,2,64,256]{3,2,1,0:T(8,128)(2,1)}), bf16[8,2,64,256]{3,2,1,0:T(8,128)(2,1)S(1)}, u32[]{:S(2)}, u32[]{:S(2)}) async-start(bf16[8,2,64,256]{3,2,1,0:T(8,128)(2,1)} %whiten.2), calls=%async_computation | async-start | bytes 1048576 | tf_op jit(solution)/shard_map/all_to_all | solution.py:222
  10.1 43.4 %copy-start.7 = (f32[8]{0:T(128)S(1)}, f32[8]{0:T(128)}, u32[]{:S(2)}) copy-start(f32[8]{0:T(128)} %constant.35.clone.coef_ref) | copy-start | bytes 100
  11.0 6.7 %collective-permute-start = (bf16[2,64,256]{2,1,0:T(8,128)(2,1)S(1)}, bf16[2,64,256]{2,1,0:T(8,128)(2,1)S(1)}, u32[]{:S(2)}, u32[]{:S(2)}) collective-permute-start(bf16[2,64,256]{2,1,0:T(8,128)(2,1)S(1)} %slice_bitcast_fusion), channel_id=1, source_target_pairs={{32,0},{64,32},{96,64},{0,96},{33,1},{65,33},{97,65},{1,97},{34,2}... | collective-permute-start | bytes 196616 | tf_op jit(solution)/shard_map/ppermute | solution.py:215
  17.7 0.6 copy-start.8
  22.0 11.5 %collective-permute-start.1 = (bf16[4,2,64,256]{3,2,1,0:T(8,128)(2,1)S(1)}, bf16[4,2,64,256]{3,2,1,0:T(8,128)(2,1)S(1)}, u32[]{:S(2)}, u32[]{:S(2)}) collective-permute-start(bf16[4,2,64,256]{3,2,1,0:T(8,128)(2,1)S(1)} %get-tuple-element.18.refs_0_), channel_id=1, source_target_pairs={{0,4},{4,8},{8,12},{12,16},{16,20},{20,24},{24,28},{28,0},{1,5},{5... | collective-permute-start | bytes 786440 | tf_op jit(solution)/shard_map/ppermute | solution.py:251
  23.8 9.8 %collective-permute-start.4 = (bf16[4,2,64,256]{3,2,1,0:T(8,128)(2,1)S(1)}, bf16[4,2,64,256]{3,2,1,0:T(8,128)(2,1)S(1)}, u32[]{:S(2)}, u32[]{:S(2)}) collective-permute-start(bf16[4,2,64,256]{3,2,1,0:T(8,128)(2,1)S(1)} %get-tuple-element.19.refs_1_), channel_id=1, source_target_pairs={{4,0},{8,4},{12,8},{16,12},{20,16},{24,20},{28,24},{0,28},{5,1},{9... | collective-permute-start | bytes 786440 | tf_op jit(solution)/shard_map/ppermute | solution.py:253
  27.8 15.6 %collective-permute-start.7 = (bf16[4,2,64,256]{3,2,1,0:T(8,128)(2,1)S(1)}, bf16[4,2,64,256]{3,2,1,0:T(8,128)(2,1)S(1)}, u32[]{:S(2)}, u32[]{:S(2)}) collective-permute-start(bf16[4,2,64,256]{3,2,1,0:T(8,128)(2,1)S(1)} %get-tuple-element.18.refs_0_), channel_id=1, source_target_pairs={{4,0},{8,4},{12,8},{16,12},{20,16},{24,20},{28,24},{0,28},{5,1},{9... | collective-permute-start | bytes 786440 | tf_op jit(solution)/shard_map/ppermute | solution.py:253
  29.2 14.7 %collective-permute-start.9 = (bf16[4,2,64,256]{3,2,1,0:T(8,128)(2,1)S(1)}, bf16[4,2,64,256]{3,2,1,0:T(8,128)(2,1)S(1)}, u32[]{:S(2)}, u32[]{:S(2)}) collective-permute-start(bf16[4,2,64,256]{3,2,1,0:T(8,128)(2,1)S(1)} %get-tuple-element.19.refs_1_), channel_id=1, source_target_pairs={{0,4},{4,8},{8,12},{12,16},{16,20},{20,24},{24,28},{28,0},{1,5},{5... | collective-permute-start | bytes 786440 | tf_op jit(solution)/shard_map/ppermute | solution.py:251
  33.5 11.4 %collective-permute-start.2 = (bf16[4,2,64,256]{3,2,1,0:T(8,128)(2,1)S(1)}, bf16[4,2,64,256]{3,2,1,0:T(8,128)(2,1)S(1)}, u32[]{:S(2)}, u32[]{:S(2)}) collective-permute-start(bf16[4,2,64,256]{3,2,1,0:T(8,128)(2,1)S(1)} %collective-permute-done.1.refs_2_), channel_id=1, source_target_pairs={{0,4},{4,8},{8,12},{12,16},{16,20},{20,24},{24,28},{28,0},{1,5},{5... | collective-permute-start | bytes 786440 | tf_op jit(solution)/shard_map/ppermute | solution.py:251
  33.5 11.4 %collective-permute-start.5 = (bf16[4,2,64,256]{3,2,1,0:T(8,128)(2,1)S(1)}, bf16[4,2,64,256]{3,2,1,0:T(8,128)(2,1)S(1)}, u32[]{:S(2)}, u32[]{:S(2)}) collective-permute-start(bf16[4,2,64,256]{3,2,1,0:T(8,128)(2,1)S(1)} %collective-permute-done.4.refs_7_), channel_id=1, source_target_pairs={{4,0},{8,4},{12,8},{16,12},{20,16},{24,20},{28,24},{0,28},{5,1},{9... | collective-permute-start | bytes 786440 | tf_op jit(solution)/shard_map/ppermute | solution.py:253
  36.2 24.5 %all-to-all-start.2 = ((bf16[8,2,64,256]{3,2,1,0:T(8,128)(2,1)}), bf16[8,2,64,256]{3,2,1,0:T(8,128)(2,1)}, u32[]{:S(2)}, u32[]{:S(2)}) async-start(bf16[8,2,64,256]{3,2,1,0:T(8,128)(2,1)} %whiten.3), calls=%async_computation.2 | async-start | bytes 1048576 | tf_op jit(solution)/shard_map/all_to_all | solution.py:222
  43.4 7.7 %collective-permute-start.8 = (bf16[4,2,64,256]{3,2,1,0:T(8,128)(2,1)S(1)}, bf16[4,2,64,256]{3,2,1,0:T(8,128)(2,1)S(1)}, u32[]{:S(2)}, u32[]{:S(2)}) collective-permute-start(bf16[4,2,64,256]{3,2,1,0:T(8,128)(2,1)S(1)} %collective-permute-done.7.refs_3_), channel_id=1, source_target_pairs={{4,0},{8,4},{12,8},{16,12},{20,16},{24,20},{28,24},{0,28},{5,1},{9... | collective-permute-start | bytes 786440 | tf_op jit(solution)/shard_map/ppermute | solution.py:253
  43.9 9.7 %collective-permute-start.10 = (bf16[4,2,64,256]{3,2,1,0:T(8,128)(2,1)S(1)}, bf16[4,2,64,256]{3,2,1,0:T(8,128)(2,1)S(1)}, u32[]{:S(2)}, u32[]{:S(2)}) collective-permute-start(bf16[4,2,64,256]{3,2,1,0:T(8,128)(2,1)S(1)} %collective-permute-done.9.refs_6_), channel_id=1, source_target_pairs={{0,4},{4,8},{8,12},{12,16},{16,20},{20,24},{24,28},{28,0},{1,5},{5... | collective-permute-start | bytes 786440 | tf_op jit(solution)/shard_map/ppermute | solution.py:251
  44.9 12.8 %collective-permute-start.3 = (bf16[4,2,64,256]{3,2,1,0:T(8,128)(2,1)S(1)}, bf16[4,2,64,256]{3,2,1,0:T(8,128)(2,1)}, u32[]{:S(2)}, u32[]{:S(2)}) collective-permute-start(bf16[4,2,64,256]{3,2,1,0:T(8,128)(2,1)S(1)} %collective-permute-done.2.refs_4_), channel_id=1, source_target_pairs={{0,4},{4,8},{8,12},{12,16},{16,20},{20,24},{24,28},{28,0},{1,5},{5... | collective-permute-start | bytes 786440 | tf_op jit(solution)/shard_map/ppermute | solution.py:251
  44.9 12.7 %collective-permute-start.6 = (bf16[4,2,64,256]{3,2,1,0:T(8,128)(2,1)S(1)}, bf16[4,2,64,256]{3,2,1,0:T(8,128)(2,1)}, u32[]{:S(2)}, u32[]{:S(2)}) collective-permute-start(bf16[4,2,64,256]{3,2,1,0:T(8,128)(2,1)S(1)} %collective-permute-done.5.refs_9_), channel_id=1, source_target_pairs={{4,0},{8,4},{12,8},{16,12},{20,16},{24,20},{28,24},{0,28},{5,1},{9... | collective-permute-start | bytes 786440 | tf_op jit(solution)/shard_map/ppermute | solution.py:253
  51.1 14.3 %collective-permute-start.11 = (bf16[4,2,64,256]{3,2,1,0:T(8,128)(2,1)S(1)}, bf16[4,2,64,256]{3,2,1,0:T(8,128)(2,1)S(1)}, u32[]{:S(2)}, u32[]{:S(2)}) collective-permute-start(bf16[4,2,64,256]{3,2,1,0:T(8,128)(2,1)S(1)} %collective-permute-done.8.refs_5_), channel_id=1, source_target_pairs={{4,0},{8,4},{12,8},{16,12},{20,16},{24,20},{28,24},{0,28},{5,1},{9... | collective-permute-start | bytes 786440 | tf_op jit(solution)/shard_map/ppermute | solution.py:253
  53.6 9.6 %collective-permute-start.13 = (bf16[4,2,64,256]{3,2,1,0:T(8,128)(2,1)S(1)}, bf16[4,2,64,256]{3,2,1,0:T(8,128)(2,1)S(1)}, u32[]{:S(2)}, u32[]{:S(2)}) collective-permute-start(bf16[4,2,64,256]{3,2,1,0:T(8,128)(2,1)S(1)} %collective-permute-done.10.refs_8_), channel_id=1, source_target_pairs={{0,4},{4,8},{8,12},{12,16},{16,20},{20,24},{24,28},{28,0},{1,5},{5... | collective-permute-start | bytes 786440 | tf_op jit(solution)/shard_map/ppermute | solution.py:251
  57.7 11.1 %collective-permute-start.12 = (bf16[4,2,64,256]{3,2,1,0:T(8,128)(2,1)}, bf16[4,2,64,256]{3,2,1,0:T(8,128)(2,1)S(1)}, u32[]{:S(2)}, u32[]{:S(2)}) collective-permute-start(bf16[4,2,64,256]{3,2,1,0:T(8,128)(2,1)} %collective-permute-done.3.refs_2_), channel_id=1, source_target_pairs={{0,4},{4,8},{8,12},{12,16},{16,20},{20,24},{24,28},{28,0},{1,5},{5... | collective-permute-start | bytes 786440 | tf_op jit(solution)/shard_map/ppermute | solution.py:251
  57.9 11.1 %collective-permute-start.14 = (bf16[4,2,64,256]{3,2,1,0:T(8,128)(2,1)}, bf16[4,2,64,256]{3,2,1,0:T(8,128)(2,1)S(1)}, u32[]{:S(2)}, u32[]{:S(2)}) collective-permute-start(bf16[4,2,64,256]{3,2,1,0:T(8,128)(2,1)} %collective-permute-done.6.refs_6_), channel_id=1, source_target_pairs={{4,0},{8,4},{12,8},{16,12},{20,16},{24,20},{28,24},{0,28},{5,1},{9... | collective-permute-start | bytes 786440 | tf_op jit(solution)/shard_map/ppermute | solution.py:253
  63.2 0.7 copy-start.4
  63.9 10.9 %collective-permute-start.18 = (bf16[4,2,64,256]{3,2,1,0:T(8,128)(2,1)S(1)}, bf16[4,2,64,256]{3,2,1,0:T(8,128)(2,1)S(1)}, u32[]{:S(2)}, u32[]{:S(2)}) collective-permute-start(bf16[4,2,64,256]{3,2,1,0:T(8,128)(2,1)S(1)} %get-tuple-element.24.refs_1_), channel_id=1, source_target_pairs={{4,0},{8,4},{12,8},{16,12},{20,16},{24,20},{28,24},{0,28},{5,1},{9... | collective-permute-start | bytes 786440 | tf_op jit(solution)/shard_map/ppermute | solution.py:253
  63.9 10.9 %collective-permute-start.15 = (bf16[4,2,64,256]{3,2,1,0:T(8,128)(2,1)S(1)}, bf16[4,2,64,256]{3,2,1,0:T(8,128)(2,1)S(1)}, u32[]{:S(2)}, u32[]{:S(2)}) collective-permute-start(bf16[4,2,64,256]{3,2,1,0:T(8,128)(2,1)S(1)} %get-tuple-element.23.refs_0_), channel_id=1, source_target_pairs={{0,4},{4,8},{8,12},{12,16},{16,20},{20,24},{24,28},{28,0},{1,5},{5... | collective-permute-start | bytes 786440 | tf_op jit(solution)/shard_map/ppermute | solution.py:251
  65.3 0.7 copy-start.2
  66.1 21.6 %collective-permute-start.21 = (bf16[4,2,64,256]{3,2,1,0:T(8,128)(2,1)S(1)}, bf16[4,2,64,256]{3,2,1,0:T(8,128)(2,1)S(1)}, u32[]{:S(2)}, u32[]{:S(2)}) collective-permute-start(bf16[4,2,64,256]{3,2,1,0:T(8,128)(2,1)S(1)} %get-tuple-element.23.refs_0_), channel_id=1, source_target_pairs={{4,0},{8,4},{12,8},{16,12},{20,16},{24,20},{28,24},{0,28},{5,1},{9... | collective-permute-start | bytes 786440 | tf_op jit(solution)/shard_map/ppermute | solution.py:253
  68.8 18.9 %collective-permute-start.23 = (bf16[4,2,64,256]{3,2,1,0:T(8,128)(2,1)S(1)}, bf16[4,2,64,256]{3,2,1,0:T(8,128)(2,1)S(1)}, u32[]{:S(2)}, u32[]{:S(2)}) collective-permute-start(bf16[4,2,64,256]{3,2,1,0:T(8,128)(2,1)S(1)} %get-tuple-element.24.refs_1_), channel_id=1, source_target_pairs={{0,4},{4,8},{8,12},{12,16},{16,20},{20,24},{24,28},{28,0},{1,5},{5... | collective-permute-start | bytes 786440 | tf_op jit(solution)/shard_map/ppermute | solution.py:251
  69.1 1.0 copy-start.3
  70.0 0.9 copy-start.5
  74.7 18.1 %copy-start.9 = (f32[8]{0:T(128)S(1)}, f32[8]{0:T(128)}, u32[]{:S(2)}) copy-start(f32[8]{0:T(128)} %constant.34.clone) | copy-start | bytes 100
  74.8 15.4 %collective-permute-start.16 = (bf16[4,2,64,256]{3,2,1,0:T(8,128)(2,1)S(1)}, bf16[4,2,64,256]{3,2,1,0:T(8,128)(2,1)}, u32[]{:S(2)}, u32[]{:S(2)}) collective-permute-start(bf16[4,2,64,256]{3,2,1,0:T(8,128)(2,1)S(1)} %collective-permute-done.15.refs_2_), channel_id=1, source_target_pairs={{0,4},{4,8},{8,12},{12,16},{16,20},{20,24},{24,28},{28,0},{1,5},{5... | collective-permute-start | bytes 786440 | tf_op jit(solution)/shard_map/ppermute | solution.py:251
  74.9 15.3 %collective-permute-start.19 = (bf16[4,2,64,256]{3,2,1,0:T(8,128)(2,1)S(1)}, bf16[4,2,64,256]{3,2,1,0:T(8,128)(2,1)}, u32[]{:S(2)}, u32[]{:S(2)}) collective-permute-start(bf16[4,2,64,256]{3,2,1,0:T(8,128)(2,1)S(1)} %collective-permute-done.18.refs_7_), channel_id=1, source_target_pairs={{4,0},{8,4},{12,8},{16,12},{20,16},{24,20},{28,24},{0,28},{5,1},{9... | collective-permute-start | bytes 786440 | tf_op jit(solution)/shard_map/ppermute | solution.py:253
  77.5 40.5 %all-to-all-start.1 = ((bf16[32,2,64,256]{3,2,1,0:T(8,128)(2,1)}), bf16[32,2,64,256]{3,2,1,0:T(8,128)(2,1)}, u32[]{:S(2)}, u32[]{:S(2)}) async-start(bf16[32,2,64,256]{3,2,1,0:T(8,128)(2,1)} %bitcast.4), calls=%async_computation.1 | async-start | bytes 4194304 | tf_op jit(solution)/shard_map/all_to_all | solution.py:270
  87.7 7.8 %collective-permute-start.22 = (bf16[4,2,64,256]{3,2,1,0:T(8,128)(2,1)S(1)}, bf16[4,2,64,256]{3,2,1,0:T(8,128)(2,1)}, u32[]{:S(2)}, u32[]{:S(2)}) collective-permute-start(bf16[4,2,64,256]{3,2,1,0:T(8,128)(2,1)S(1)} %collective-permute-done.21.refs_3_), channel_id=1, source_target_pairs={{4,0},{8,4},{12,8},{16,12},{20,16},{24,20},{28,24},{0,28},{5,1},{9... | collective-permute-start | bytes 786440 | tf_op jit(solution)/shard_map/ppermute | solution.py:253
  89.4 8.9 %collective-permute-start.24 = (bf16[4,2,64,256]{3,2,1,0:T(8,128)(2,1)S(1)}, bf16[4,2,64,256]{3,2,1,0:T(8,128)(2,1)}, u32[]{:S(2)}, u32[]{:S(2)}) collective-permute-start(bf16[4,2,64,256]{3,2,1,0:T(8,128)(2,1)S(1)} %collective-permute-done.23.refs_6_), channel_id=1, source_target_pairs={{0,4},{4,8},{8,12},{12,16},{16,20},{20,24},{24,28},{28,0},{1,5},{5... | collective-permute-start | bytes 786440 | tf_op jit(solution)/shard_map/ppermute | solution.py:251
  89.4 0.7 copy-start
  90.1 13.5 %collective-permute-start.17 = (bf16[4,2,64,256]{3,2,1,0:T(8,128)(2,1)}, bf16[4,2,64,256]{3,2,1,0:T(8,128)(2,1)S(1)}, u32[]{:S(2)}, u32[]{:S(2)}) collective-permute-start(bf16[4,2,64,256]{3,2,1,0:T(8,128)(2,1)} %collective-permute-done.16.refs_4_), channel_id=1, source_target_pairs={{0,4},{4,8},{8,12},{12,16},{16,20},{20,24},{24,28},{28,0},{1,5},{5... | collective-permute-start | bytes 786440 | tf_op jit(solution)/shard_map/ppermute | solution.py:251
  90.2 13.4 %collective-permute-start.20 = (bf16[4,2,64,256]{3,2,1,0:T(8,128)(2,1)}, bf16[4,2,64,256]{3,2,1,0:T(8,128)(2,1)S(1)}, u32[]{:S(2)}, u32[]{:S(2)}) collective-permute-start(bf16[4,2,64,256]{3,2,1,0:T(8,128)(2,1)} %collective-permute-done.19.refs_9_), channel_id=1, source_target_pairs={{4,0},{8,4},{12,8},{16,12},{20,16},{24,20},{28,24},{0,28},{5,1},{9... | collective-permute-start | bytes 786440 | tf_op jit(solution)/shard_map/ppermute | solution.py:253
  95.4 11.2 %collective-permute-start.25 = (bf16[4,2,64,256]{3,2,1,0:T(8,128)(2,1)}, bf16[4,2,64,256]{3,2,1,0:T(8,128)(2,1)S(1)}, u32[]{:S(2)}, u32[]{:S(2)}) collective-permute-start(bf16[4,2,64,256]{3,2,1,0:T(8,128)(2,1)} %collective-permute-done.22.refs_5_), channel_id=1, source_target_pairs={{4,0},{8,4},{12,8},{16,12},{20,16},{24,20},{28,24},{0,28},{5,1},{9... | collective-permute-start | bytes 786440 | tf_op jit(solution)/shard_map/ppermute | solution.py:253
  98.3 10.9 %collective-permute-start.27 = (bf16[4,2,64,256]{3,2,1,0:T(8,128)(2,1)}, bf16[4,2,64,256]{3,2,1,0:T(8,128)(2,1)S(1)}, u32[]{:S(2)}, u32[]{:S(2)}) collective-permute-start(bf16[4,2,64,256]{3,2,1,0:T(8,128)(2,1)} %collective-permute-done.24.refs_8_), channel_id=1, source_target_pairs={{0,4},{4,8},{8,12},{12,16},{16,20},{20,24},{24,28},{28,0},{1,5},{5... | collective-permute-start | bytes 786440 | tf_op jit(solution)/shard_map/ppermute | solution.py:251
  98.3 1.0 copy-start.1
  103.6 11.2 %collective-permute-start.26 = (bf16[4,2,64,256]{3,2,1,0:T(8,128)(2,1)S(1)}, bf16[4,2,64,256]{3,2,1,0:T(8,128)(2,1)S(1)}, u32[]{:S(2)}, u32[]{:S(2)}) collective-permute-start(bf16[4,2,64,256]{3,2,1,0:T(8,128)(2,1)S(1)} %collective-permute-done.17.refs_2_), channel_id=1, source_target_pairs={{0,4},{4,8},{8,12},{12,16},{16,20},{20,24},{24,28},{28,0},{1,5},{5... | collective-permute-start | bytes 786440 | tf_op jit(solution)/shard_map/ppermute | solution.py:251
  103.6 11.2 %collective-permute-start.28 = (bf16[4,2,64,256]{3,2,1,0:T(8,128)(2,1)S(1)}, bf16[4,2,64,256]{3,2,1,0:T(8,128)(2,1)S(1)}, u32[]{:S(2)}, u32[]{:S(2)}) collective-permute-start(bf16[4,2,64,256]{3,2,1,0:T(8,128)(2,1)S(1)} %collective-permute-done.20.refs_6_), channel_id=1, source_target_pairs={{4,0},{8,4},{12,8},{16,12},{20,16},{24,20},{28,24},{0,28},{5,1},{9... | collective-permute-start | bytes 786440 | tf_op jit(solution)/shard_map/ppermute | solution.py:253
  118.0 36.7 %copy-start.6 = (bf16[128,128]{1,0:T(8,128)(2,1)S(1)}, bf16[128,128]{1,0:T(8,128)(2,1)}, u32[]{:S(2)}) copy-start(bf16[128,128]{1,0:T(8,128)(2,1)} %constant.36.clone.t_ref) | copy-start | bytes 98308

commit v5 on v4

--- a/solution.py
+++ b/solution.py
@@ -20,7 +20,7 @@
 NQ = YL * CO
 PLANE = ("yh", "x", "yl", "co")
 VMEM = 20 * 1024 * 1024
-ROWS = 32
+ROWS = 16
 FLOPS = 3 << 32
 
 
@@ -184,26 +184,46 @@
     )(zpos, coef, *ins)
 
 
+def arrange_kernel(x_ref, o_ref):
+    o_ref[0] = x_ref[...].reshape(o_ref.shape[1:])
+
+
+def arrange(moved):
+    n = NK * NQ * 2
+    return pl.pallas_call(
+        arrange_kernel,
+        grid=(CH // ROWS,),
+        in_specs=[pl.BlockSpec((n, ROWS, COLS), lambda i: (0, i, 0))],
+        out_specs=pl.BlockSpec((1, n, ROWS * COLS), lambda i: (i, 0, 0)),
+        out_shape=jax.ShapeDtypeStruct((CH // ROWS, n, ROWS * COLS), jnp.bfloat16),
+        compiler_params=pltpu.CompilerParams(vmem_limit_bytes=VMEM),
+        cost_estimate=pl.CostEstimate(flops=1 << 20, bytes_accessed=4 << 20, transcendentals=0),
+        name="arrange",
+    )(moved.reshape(n, CH, COLS))
+
+
 def lags_kernel(t_ref, x1_ref, x0_ref, out_ref):
-    x = jnp.concatenate([r[...].reshape(NK * NQ * 2, ROWS, COLS) for r in (x1_ref, x0_ref)])
-    x = x.reshape(NK * NQ * 4, ROWS * COLS)
+    x = jnp.concatenate([x1_ref[0], x0_ref[...].reshape(NK * NQ * 2, ROWS * COLS)])
     y = jnp.dot(t_ref[...], x, preferred_element_type=jnp.float32) * math.sqrt(W / NF)
     out_ref[...] = y.reshape(LAGS, ROWS, COLS)
 
 
-def lags(table, moved):
-    n = NK * NQ * 4
-    part = pl.BlockSpec((NK * NQ, 2, ROWS, COLS), lambda i: (0, 0, i, 0))
+def lags(table, first, second):
+    n = NK * NQ * 2
     return pl.pallas_call(
         lags_kernel,
         grid=(CH // ROWS,),
-        in_specs=[pl.BlockSpec((LAGS, n), lambda i: (0, 0)), part, part],
+        in_specs=[
+            pl.BlockSpec((LAGS, 2 * n), lambda i: (0, 0)),
+            pl.BlockSpec((1, n, ROWS * COLS), lambda i: (i, 0, 0)),
+            pl.BlockSpec((n, ROWS, COLS), lambda i: (0, i, 0)),
+        ],
         out_specs=pl.BlockSpec((LAGS, ROWS, COLS), lambda i: (0, i, 0)),
         out_shape=jax.ShapeDtypeStruct((LAGS, CH, COLS), jnp.float32),
         compiler_params=pltpu.CompilerParams(vmem_limit_bytes=VMEM),
         cost_estimate=pl.CostEstimate(flops=1 << 29, bytes_accessed=12 << 20, transcendentals=0),
         name="lags",
-    )(table, *moved)
+    )(table, first, second.reshape(n, CH, COLS))
 
 
 def shards(spectra):
@@ -266,9 +286,12 @@
         parts = near_parts
         far = ([ups[0][2], dns[0][2], ups[0][3]], [ups[1][2], dns[1][2], dns[1][3]])
         parts = cross(zpos, coefs[t], own, *far, 5, parts, FLOPS if t == 0 else 1 << 29)
+        if t == 0:
+            ready = arrange(moved[0])
+            parts, ready = lax.optimization_barrier((parts, ready))
         parts = parts.reshape(NK * NQ, 2, CH, COLS)
         moved.append(lax.all_to_all(parts, PLANE, split_axis=0, concat_axis=0, tiled=True))
-    return lags(table, moved)
+    return lags(table, ready, moved[1])
 
 
 def solution(mesh):

time: 162 us -> 163 us (level)
    pallas_call x0 -> x1, Pallas kernels: none -> 2.59 us  [arrange(): pl.pallas_call(arrange_kernel, grid=(CH // ROWS,), in_specs=[pl.BlockSpec...]
    pallas_call x1, Pallas kernels: 7.05 us -> 5.28 us  [lags(): pl.pallas_call(lags_kernel, grid=(CH // ROWS,), in_specs=[pl.BlockSpec((L...]
where the time goes in v5:
time: 163 us
  starting transfers between devices  62.7 us (38%)
  blocking collectives  35.7 us (22%)
  waiting for transfers between devices  30.7 us (19%)
  Pallas kernels  25.7 us (16%)
  local copies, waits for them, and re-layouts  7.61 us (5%)
    all_to_all x1, blocking collectives, shards(): lax.all_to_all(parts, PLANE, split_axis=0, concat_axis=0, tiled=True)  35.7 us
    ppermute x14, starting transfers between devices, ring(): dns[side].append(lax.ppermute(dns[side][-1] if s else own[side], 'z', dn))  29.4 us
    all_to_all x2, starting transfers between devices, regroup(): lax.all_to_all(white[t], PLANE, split_axis=0, concat_axis=0, tiled=True,...  15.4 us
    ppermute x14, waiting for transfers between devices, ring(): ups[side].append(lax.ppermute(ups[side][-1] if s else own[side], 'z', up))  15.1 us
    pallas_call x4, Pallas kernels, cross(): pl.pallas_call(functools.partial(cross_kernel, first, count), grid_spec=p...  13.9 us
    all_to_all x1, starting transfers between devices, shards(): lax.all_to_all(parts, PLANE, split_axis=0, concat_axis=0, tiled=True)  11.1 us
    ppermute x14, waiting for transfers between devices, ring(): dns[side].append(lax.ppermute(dns[side][-1] if s else own[side], 'z', dn))  7.74 us
    unnamed x20, local copies, waits for them, and re-layouts  5.65 us
  transfers between devices with their start and end apart: 32, of which 12 were waited for; matrix products, arithmetic and copies ran while one was open for 1% of the time, Pallas kernels for 10%

profile of v5, /device:TPU:1, one launch (start us, length us, event | category | flops | bytes accessed | tf_op | source)
XLA Modules:
  0.0 162.6 jit_solution(17001444884540865130)
XLA Ops:
  0.0 1.9 %whiten.3 = bf16[8,2,64,256]{3,2,1,0:T(8,128)(2,1)} custom-call(s32[1]{0:T(128)} %bitcast.1.hi_ref, bf16[2,8,2,64,256]{4,3,2,1,0:T(8,128)(2,1)} %bitcast.13), custom_call_target="tpu_custom_call" | custom-call | flops 2000000 | bytes 1048576 | tf_op jit(solution)/shard_map/whiten/pallas_call | solution.py:77
  1.9 8.2 %all-to-all-start = ((bf16[8,2,64,256]{3,2,1,0:T(8,128)(2,1)}), bf16[8,2,64,256]{3,2,1,0:T(8,128)(2,1)S(1)}, u32[]{:S(2)}, u32[]{:S(2)}) async-start(bf16[8,2,64,256]{3,2,1,0:T(8,128)(2,1)} %whiten.3), calls=%async_computation | async-start | bytes 1048576 | tf_op jit(solution)/shard_map/all_to_all | solution.py:242
  10.1 0.9 slice_bitcast_fusion
  11.0 2.1 %collective-permute-start = (bf16[2,64,256]{2,1,0:T(8,128)(2,1)S(1)}, bf16[2,64,256]{2,1,0:T(8,128)(2,1)S(1)}, u32[]{:S(2)}, u32[]{:S(2)}) collective-permute-start(bf16[2,64,256]{2,1,0:T(8,128)(2,1)S(1)} %slice_bitcast_fusion), channel_id=1, source_target_pairs={{32,0},{64,32},{96,64},{0,96},{33,1},{65,33},{97,65},{1,97},{34,2}... | collective-permute-start | bytes 196616 | tf_op jit(solution)/shard_map/ppermute | solution.py:235
  13.1 4.6 %collective-permute-done.refs_0_ = bf16[2,64,256]{2,1,0:T(8,128)(2,1)S(1)} collective-permute-done((bf16[2,64,256]{2,1,0:T(8,128)(2,1)S(1)}, bf16[2,64,256]{2,1,0:T(8,128)(2,1)S(1)}, u32[]{:S(2)}, u32[]{:S(2)}) %collective-permute-start) | collective-permute-done | bytes 65568 | tf_op jit(solution)/shard_map/ppermute | solution.py:235
  18.3 2.1 %whiten.2 = bf16[8,2,64,256]{3,2,1,0:T(8,128)(2,1)} custom-call(s32[1]{0:T(128)} %bitcast.1.hi_ref, bf16[2,8,2,64,256]{4,3,2,1,0:T(8,128)(2,1)} %bitcast.14, bf16[2,64,256]{2,1,0:T(8,128)(2,1)} %copy-done.8), custom_call_target="tpu_custom_call" | custom-call | flops 2000000 | bytes 1048576 | tf_op jit(solution)/shard_map/whiten/pallas_call | solution.py:77
  20.3 1.6 %all-to-all-done = bf16[8,2,64,256]{3,2,1,0:T(8,128)(2,1)S(1)} async-done(((bf16[8,2,64,256]{3,2,1,0:T(8,128)(2,1)}), bf16[8,2,64,256]{3,2,1,0:T(8,128)(2,1)S(1)}, u32[]{:S(2)}, u32[]{:S(2)}) %all-to-all-start) | async-done | bytes 524320 | tf_op jit(solution)/shard_map/all_to_all | solution.py:242
  22.0 1.7 %collective-permute-start.1 = (bf16[4,2,64,256]{3,2,1,0:T(8,128)(2,1)S(1)}, bf16[4,2,64,256]{3,2,1,0:T(8,128)(2,1)S(1)}, u32[]{:S(2)}, u32[]{:S(2)}) collective-permute-start(bf16[4,2,64,256]{3,2,1,0:T(8,128)(2,1)S(1)} %get-tuple-element.20.refs_0_), channel_id=1, source_target_pairs={{0,4},{4,8},{8,12},{12,16},{16,20},{20,24},{24,28},{28,0},{1,5},{5... | collective-permute-start | bytes 786440 | tf_op jit(solution)/shard_map/ppermute | solution.py:271
  23.8 4.0 %collective-permute-start.8 = (bf16[4,2,64,256]{3,2,1,0:T(8,128)(2,1)S(1)}, bf16[4,2,64,256]{3,2,1,0:T(8,128)(2,1)S(1)}, u32[]{:S(2)}, u32[]{:S(2)}) collective-permute-start(bf16[4,2,64,256]{3,2,1,0:T(8,128)(2,1)S(1)} %get-tuple-element.22.refs_1_), channel_id=1, source_target_pairs={{4,0},{8,4},{12,8},{16,12},{20,16},{24,20},{28,24},{0,28},{5,1},{9... | collective-permute-start | bytes 786440 | tf_op jit(solution)/shard_map/ppermute | solution.py:273
  27.8 1.4 collective-permute-start.11
  29.2 4.2 %collective-permute-done.1.refs_2_ = bf16[4,2,64,256]{3,2,1,0:T(8,128)(2,1)S(1)} collective-permute-done((bf16[4,2,64,256]{3,2,1,0:T(8,128)(2,1)S(1)}, bf16[4,2,64,256]{3,2,1,0:T(8,128)(2,1)S(1)}, u32[]{:S(2)}, u32[]{:S(2)}) %collective-permute-start.1) | collective-permute-done | bytes 262176 | tf_op jit(solution)/shard_map/ppermute | solution.py:271
  33.5 2.7 %collective-permute-start.9 = (bf16[4,2,64,256]{3,2,1,0:T(8,128)(2,1)S(1)}, bf16[4,2,64,256]{3,2,1,0:T(8,128)(2,1)S(1)}, u32[]{:S(2)}, u32[]{:S(2)}) collective-permute-start(bf16[4,2,64,256]{3,2,1,0:T(8,128)(2,1)S(1)} %collective-permute-done.8.refs_7_), channel_id=1, source_target_pairs={{4,0},{8,4},{12,8},{16,12},{20,16},{24,20},{28,24},{0,28},{5,1},{9... | collective-permute-start | bytes 786440 | tf_op jit(solution)/shard_map/ppermute | solution.py:273
  36.2 7.2 %all-to-all-start.1 = ((bf16[8,2,64,256]{3,2,1,0:T(8,128)(2,1)}), bf16[8,2,64,256]{3,2,1,0:T(8,128)(2,1)}, u32[]{:S(2)}, u32[]{:S(2)}) async-start(bf16[8,2,64,256]{3,2,1,0:T(8,128)(2,1)} %whiten.2), calls=%async_computation.1 | async-start | bytes 1048576 | tf_op jit(solution)/shard_map/all_to_all | solution.py:242
  43.9 1.0 collective-permute-start.3
  44.9 2.6 %collective-permute-start.10 = (bf16[4,2,64,256]{3,2,1,0:T(8,128)(2,1)S(1)}, bf16[4,2,64,256]{3,2,1,0:T(8,128)(2,1)}, u32[]{:S(2)}, u32[]{:S(2)}) collective-permute-start(bf16[4,2,64,256]{3,2,1,0:T(8,128)(2,1)S(1)} %collective-permute-done.9.refs_9_), channel_id=1, source_target_pairs={{4,0},{8,4},{12,8},{16,12},{20,16},{24,20},{28,24},{0,28},{5,1},{9... | collective-permute-start | bytes 786440 | tf_op jit(solution)/shard_map/ppermute | solution.py:273
  47.5 3.5 %collective-permute-done.12.refs_5_ = bf16[4,2,64,256]{3,2,1,0:T(8,128)(2,1)S(1)} collective-permute-done((bf16[4,2,64,256]{3,2,1,0:T(8,128)(2,1)S(1)}, bf16[4,2,64,256]{3,2,1,0:T(8,128)(2,1)S(1)}, u32[]{:S(2)}, u32[]{:S(2)}) %collective-permute-start.12) | collective-permute-done | bytes 262176 | tf_op jit(solution)/shard_map/ppermute | solution.py:273
  51.1 2.5 %collective-permute-start.13 = (bf16[4,2,64,256]{3,2,1,0:T(8,128)(2,1)S(1)}, bf16[4,2,64,256]{3,2,1,0:T(8,128)(2,1)S(1)}, u32[]{:S(2)}, u32[]{:S(2)}) collective-permute-start(bf16[4,2,64,256]{3,2,1,0:T(8,128)(2,1)S(1)} %collective-permute-done.12.refs_5_), channel_id=1, source_target_pairs={{4,0},{8,4},{12,8},{16,12},{20,16},{24,20},{28,24},{0,28},{5,1},{9... | collective-permute-start | bytes 786440 | tf_op jit(solution)/shard_map/ppermute | solution.py:273
  53.6 4.1 %cross.4.refs_8_ = bf16[8,4,2,64,256]{4,3,2,1,0:T(8,128)(2,1)} custom-call(s32[1]{0:T(128)} %bitcast.z_ref, f32[8]{0:T(128)S(1)} %copy-done.7, bf16[4,2,64,256]{3,2,1,0:T(8,128)(2,1)S(1)} %get-tuple-element.20.refs_0_, bf16[4,2,64,256]{3,2,1,0:T(8,128)(2,1)S(1)} %get-tuple-element.22.refs_1_, bf16[4,2,64,256]{3,2,1,0:T(8,128)(2,1)S(1)} %collective-permute-done.1.refs_2_, ...), custom_call_target="tpu_custom_call" | custom-call | flops 1073741824 | bytes 4194304 | tf_op jit(solution)/shard_map/cross/pallas_call | solution.py:162
  57.9 2.8 %collective-permute-start.15 = (bf16[4,2,64,256]{3,2,1,0:T(8,128)(2,1)}, bf16[4,2,64,256]{3,2,1,0:T(8,128)(2,1)S(1)}, u32[]{:S(2)}, u32[]{:S(2)}) collective-permute-start(bf16[4,2,64,256]{3,2,1,0:T(8,128)(2,1)} %collective-permute-done.10.refs_6_), channel_id=1, source_target_pairs={{4,0},{8,4},{12,8},{16,12},{20,16},{24,20},{28,24},{0,28},{5,1},{9... | collective-permute-start | bytes 786440 | tf_op jit(solution)/shard_map/ppermute | solution.py:273
  60.7 1.1 fusion
  61.8 1.4 collective-permute-done.4.refs_5_
  63.2 0.7 copy-done.4
  64.2 2.4 %collective-permute-start.18 = (bf16[4,2,64,256]{3,2,1,0:T(8,128)(2,1)S(1)}, bf16[4,2,64,256]{3,2,1,0:T(8,128)(2,1)S(1)}, u32[]{:S(2)}, u32[]{:S(2)}) collective-permute-start(bf16[4,2,64,256]{3,2,1,0:T(8,128)(2,1)S(1)} %get-tuple-element.24.refs_1_), channel_id=1, source_target_pairs={{4,0},{8,4},{12,8},{16,12},{20,16},{24,20},{28,24},{0,28},{5,1},{9... | collective-permute-start | bytes 786440 | tf_op jit(solution)/shard_map/ppermute | solution.py:273
  66.6 0.7 copy-done.2
  67.4 1.4 collective-permute-done.14.refs_4_
  69.1 0.9 copy-done.3
  70.0 0.9 copy-done.5
  71.0 3.8 %cross.5 = bf16[8,4,2,64,256]{4,3,2,1,0:T(8,128)(2,1)} custom-call(s32[1]{0:T(128)} %bitcast.z_ref, f32[8]{0:T(128)S(1)} %copy-done.7, bf16[4,2,64,256]{3,2,1,0:T(8,128)(2,1)S(1)} %get-tuple-element.20.refs_0_, bf16[4,2,64,256]{3,2,1,0:T(8,128)(2,1)S(1)} %get-tuple-element.22.refs_1_, ...), custom_call_target="tpu_custom_call", output_to_operand_aliasing={{}: (10, {})} | custom-call | flops 536870912 | bytes 4194304 | tf_op jit(solution)/shard_map/cross/pallas_call | solution.py:162
  74.9 2.7 %collective-permute-start.19 = (bf16[4,2,64,256]{3,2,1,0:T(8,128)(2,1)S(1)}, bf16[4,2,64,256]{3,2,1,0:T(8,128)(2,1)}, u32[]{:S(2)}, u32[]{:S(2)}) collective-permute-start(bf16[4,2,64,256]{3,2,1,0:T(8,128)(2,1)S(1)} %collective-permute-done.18.refs_7_), channel_id=1, source_target_pairs={{4,0},{8,4},{12,8},{16,12},{20,16},{24,20},{28,24},{0,28},{5,1},{9... | collective-permute-start | bytes 786440 | tf_op jit(solution)/shard_map/ppermute | solution.py:273
  77.5 11.1 %all-to-all-start.2 = ((bf16[32,2,64,256]{3,2,1,0:T(8,128)(2,1)}), bf16[32,2,64,256]{3,2,1,0:T(8,128)(2,1)}, u32[]{:S(2)}, u32[]{:S(2)}) async-start(bf16[32,2,64,256]{3,2,1,0:T(8,128)(2,1)} %bitcast.4), calls=%async_computation.2 | async-start | bytes 4194304 | tf_op jit(solution)/shard_map/all_to_all | solution.py:293
  88.6 0.7 collective-permute-start.22
  89.4 0.8 collective-permute-start.24
  90.2 0.7 copy-done
  90.9 2.7 %collective-permute-start.20 = (bf16[4,2,64,256]{3,2,1,0:T(8,128)(2,1)}, bf16[4,2,64,256]{3,2,1,0:T(8,128)(2,1)S(1)}, u32[]{:S(2)}, u32[]{:S(2)}) collective-permute-start(bf16[4,2,64,256]{3,2,1,0:T(8,128)(2,1)} %collective-permute-done.19.refs_9_), channel_id=1, source_target_pairs={{4,0},{8,4},{12,8},{16,12},{20,16},{24,20},{28,24},{0,28},{5,1},{9... | collective-permute-start | bytes 786440 | tf_op jit(solution)/shard_map/ppermute | solution.py:273
  93.6 2.8 %collective-permute-done.22.refs_5_ = bf16[4,2,64,256]{3,2,1,0:T(8,128)(2,1)} collective-permute-done((bf16[4,2,64,256]{3,2,1,0:T(8,128)(2,1)S(1)}, bf16[4,2,64,256]{3,2,1,0:T(8,128)(2,1)}, u32[]{:S(2)}, u32[]{:S(2)}) %collective-permute-start.22) | collective-permute-done | bytes 262176 | tf_op jit(solution)/shard_map/ppermute | solution.py:273
  96.4 1.9 %collective-permute-start.25 = (bf16[4,2,64,256]{3,2,1,0:T(8,128)(2,1)}, bf16[4,2,64,256]{3,2,1,0:T(8,128)(2,1)S(1)}, u32[]{:S(2)}, u32[]{:S(2)}) collective-permute-start(bf16[4,2,64,256]{3,2,1,0:T(8,128)(2,1)} %collective-permute-done.22.refs_5_), channel_id=1, source_target_pairs={{4,0},{8,4},{12,8},{16,12},{20,16},{24,20},{28,24},{0,28},{5,1},{9... | collective-permute-start | bytes 786440 | tf_op jit(solution)/shard_map/ppermute | solution.py:273
  98.3 0.9 copy-done.1
  99.2 3.4 %cross.6.refs_8_ = bf16[8,4,2,64,256]{4,3,2,1,0:T(8,128)(2,1)S(1)} custom-call(s32[1]{0:T(128)} %bitcast.z_ref, f32[8]{0:T(128)S(1)} %broadcast_select_fusion.coef_ref, bf16[4,2,64,256]{3,2,1,0:T(8,128)(2,1)S(1)} %get-tuple-element.23.refs_0_, bf16[4,2,64,256]{3,2,1,0:T(8,128)(2,1)S(1)} %get-tuple-element.24.refs_1_, ...), custom_call_target="tpu_custom_call" | custom-call | flops 1073741824 | bytes 4194304 | tf_op jit(solution)/shard_map/cross/pallas_call | solution.py:162
  102.7 0.9 collective-permute-done.17.refs_2_
  103.6 2.7 %collective-permute-start.28 = (bf16[4,2,64,256]{3,2,1,0:T(8,128)(2,1)S(1)}, bf16[4,2,64,256]{3,2,1,0:T(8,128)(2,1)S(1)}, u32[]{:S(2)}, u32[]{:S(2)}) collective-permute-start(bf16[4,2,64,256]{3,2,1,0:T(8,128)(2,1)S(1)} %collective-permute-done.20.refs_6_), channel_id=1, source_target_pairs={{4,0},{8,4},{12,8},{16,12},{20,16},{24,20},{28,24},{0,28},{5,1},{9... | collective-permute-start | bytes 786440 | tf_op jit(solution)/shard_map/ppermute | solution.py:273
  106.3 1.4 collective-permute-done.25.refs_3_
  107.6 1.4 collective-permute-done.27.refs_5_
  109.1 5.7 %collective-permute-done.26.refs_4_ = bf16[4,2,64,256]{3,2,1,0:T(8,128)(2,1)S(1)} collective-permute-done((bf16[4,2,64,256]{3,2,1,0:T(8,128)(2,1)S(1)}, bf16[4,2,64,256]{3,2,1,0:T(8,128)(2,1)S(1)}, u32[]{:S(2)}, u32[]{:S(2)}) %collective-permute-start.26) | collective-permute-done | bytes 262176 | tf_op jit(solution)/shard_map/ppermute | solution.py:271
  114.8 2.6 %cross.7 = bf16[8,4,2,64,256]{4,3,2,1,0:T(8,128)(2,1)S(1)} custom-call(s32[1]{0:T(128)} %bitcast.z_ref, f32[8]{0:T(128)S(1)} %broadcast_select_fusion.coef_ref, bf16[4,2,64,256]{3,2,1,0:T(8,128)(2,1)S(1)} %get-tuple-element.23.refs_0_, bf16[4,2,64,256]{3,2,1,0:T(8,128)(2,1)S(1)} %get-tuple-element.24.refs_1_, ...), custom_call_target="tpu_custom_call", output_to_operand_aliasing={{}: (10, {})} | custom-call | flops 12884901888 | bytes 4194304 | tf_op jit(solution)/shard_map/cross/pallas_call | solution.py:162
  117.4 1.6 all-to-all-done.2
  119.0 2.6 %arrange.1.x1_ref = bf16[4,64,4096]{2,1,0:T(8,128)(2,1)S(1)} custom-call(bf16[64,64,256]{2,1,0:T(8,128)(2,1)} %bitcast.5.x_ref), custom_call_target="tpu_custom_call" | custom-call | flops 1048576 | bytes 4194304 | tf_op jit(solution)/shard_map/arrange/pallas_call | solution.py:193
  121.6 35.7 %all_to_all.20 = bf16[32,2,64,256]{3,2,1,0:T(8,128)(2,1)S(1)} all-to-all(bf16[32,2,64,256]{3,2,1,0:T(8,128)(2,1)S(1)} %bitcast.11), channel_id=1, replica_groups=mesh['yh'=2,'x'=4,'z'=8,'yl'=2,'co'=2] {'yh','x','yl','co'}, dimensions={0} | all-to-all | bytes 4194304 | tf_op jit(solution)/shard_map/all_to_all | solution.py:293
  157.3 5.3 %lags.1 = f32[128,64,256]{2,1,0:T(8,128)} custom-call(bf16[128,128]{1,0:T(8,128)(2,1)S(1)} %copy-done.6, bf16[4,64,4096]{2,1,0:T(8,128)(2,1)S(1)} %arrange.1.x1_ref, bf16[64,64,256]{2,1,0:T(8,128)(2,1)S(1)} %bitcast.12), custom_call_target="tpu_custom_call" | custom-call | flops 536870912 | bytes 12582912 | tf_op jit(solution)/shard_map/lags/pallas_call | solution.py:213
  (49 shorter events, 2.4 us)
Async XLA Ops:
  1.9 20.0 %all-to-all-start = ((bf16[8,2,64,256]{3,2,1,0:T(8,128)(2,1)}), bf16[8,2,64,256]{3,2,1,0:T(8,128)(2,1)S(1)}, u32[]{:S(2)}, u32[]{:S(2)}) async-start(bf16[8,2,64,256]{3,2,1,0:T(8,128)(2,1)} %whiten.3), calls=%async_computation | async-start | bytes 1048576 | tf_op jit(solution)/shard_map/all_to_all | solution.py:242
  10.1 43.4 %copy-start.7 = (f32[8]{0:T(128)S(1)}, f32[8]{0:T(128)}, u32[]{:S(2)}) copy-start(f32[8]{0:T(128)} %constant.35.clone.coef_ref) | copy-start | bytes 100
  11.0 6.7 %collective-permute-start = (bf16[2,64,256]{2,1,0:T(8,128)(2,1)S(1)}, bf16[2,64,256]{2,1,0:T(8,128)(2,1)S(1)}, u32[]{:S(2)}, u32[]{:S(2)}) collective-permute-start(bf16[2,64,256]{2,1,0:T(8,128)(2,1)S(1)} %slice_bitcast_fusion), channel_id=1, source_target_pairs={{32,0},{64,32},{96,64},{0,96},{33,1},{65,33},{97,65},{1,97},{34,2}... | collective-permute-start | bytes 196616 | tf_op jit(solution)/shard_map/ppermute | solution.py:235
  17.7 0.6 copy-start.8
  22.0 11.5 %collective-permute-start.1 = (bf16[4,2,64,256]{3,2,1,0:T(8,128)(2,1)S(1)}, bf16[4,2,64,256]{3,2,1,0:T(8,128)(2,1)S(1)}, u32[]{:S(2)}, u32[]{:S(2)}) collective-permute-start(bf16[4,2,64,256]{3,2,1,0:T(8,128)(2,1)S(1)} %get-tuple-element.20.refs_0_), channel_id=1, source_target_pairs={{0,4},{4,8},{8,12},{12,16},{16,20},{20,24},{24,28},{28,0},{1,5},{5... | collective-permute-start | bytes 786440 | tf_op jit(solution)/shard_map/ppermute | solution.py:271
  23.8 9.8 %collective-permute-start.8 = (bf16[4,2,64,256]{3,2,1,0:T(8,128)(2,1)S(1)}, bf16[4,2,64,256]{3,2,1,0:T(8,128)(2,1)S(1)}, u32[]{:S(2)}, u32[]{:S(2)}) collective-permute-start(bf16[4,2,64,256]{3,2,1,0:T(8,128)(2,1)S(1)} %get-tuple-element.22.refs_1_), channel_id=1, source_target_pairs={{4,0},{8,4},{12,8},{16,12},{20,16},{24,20},{28,24},{0,28},{5,1},{9... | collective-permute-start | bytes 786440 | tf_op jit(solution)/shard_map/ppermute | solution.py:273
  27.8 15.6 %collective-permute-start.11 = (bf16[4,2,64,256]{3,2,1,0:T(8,128)(2,1)S(1)}, bf16[4,2,64,256]{3,2,1,0:T(8,128)(2,1)S(1)}, u32[]{:S(2)}, u32[]{:S(2)}) collective-permute-start(bf16[4,2,64,256]{3,2,1,0:T(8,128)(2,1)S(1)} %get-tuple-element.20.refs_0_), channel_id=1, source_target_pairs={{4,0},{8,4},{12,8},{16,12},{20,16},{24,20},{28,24},{0,28},{5,1},{9... | collective-permute-start | bytes 786440 | tf_op jit(solution)/shard_map/ppermute | solution.py:273
  29.2 14.7 %collective-permute-start.2 = (bf16[4,2,64,256]{3,2,1,0:T(8,128)(2,1)S(1)}, bf16[4,2,64,256]{3,2,1,0:T(8,128)(2,1)S(1)}, u32[]{:S(2)}, u32[]{:S(2)}) collective-permute-start(bf16[4,2,64,256]{3,2,1,0:T(8,128)(2,1)S(1)} %get-tuple-element.22.refs_1_), channel_id=1, source_target_pairs={{0,4},{4,8},{8,12},{12,16},{16,20},{20,24},{24,28},{28,0},{1,5},{5... | collective-permute-start | bytes 786440 | tf_op jit(solution)/shard_map/ppermute | solution.py:271
  33.5 11.4 %collective-permute-start.6 = (bf16[4,2,64,256]{3,2,1,0:T(8,128)(2,1)S(1)}, bf16[4,2,64,256]{3,2,1,0:T(8,128)(2,1)S(1)}, u32[]{:S(2)}, u32[]{:S(2)}) collective-permute-start(bf16[4,2,64,256]{3,2,1,0:T(8,128)(2,1)S(1)} %collective-permute-done.1.refs_2_), channel_id=1, source_target_pairs={{0,4},{4,8},{8,12},{12,16},{16,20},{20,24},{24,28},{28,0},{1,5},{5... | collective-permute-start | bytes 786440 | tf_op jit(solution)/shard_map/ppermute | solution.py:271
  33.5 11.4 %collective-permute-start.9 = (bf16[4,2,64,256]{3,2,1,0:T(8,128)(2,1)S(1)}, bf16[4,2,64,256]{3,2,1,0:T(8,128)(2,1)S(1)}, u32[]{:S(2)}, u32[]{:S(2)}) collective-permute-start(bf16[4,2,64,256]{3,2,1,0:T(8,128)(2,1)S(1)} %collective-permute-done.8.refs_7_), channel_id=1, source_target_pairs={{4,0},{8,4},{12,8},{16,12},{20,16},{24,20},{28,24},{0,28},{5,1},{9... | collective-permute-start | bytes 786440 | tf_op jit(solution)/shard_map/ppermute | solution.py:273
  36.2 24.5 %all-to-all-start.1 = ((bf16[8,2,64,256]{3,2,1,0:T(8,128)(2,1)}), bf16[8,2,64,256]{3,2,1,0:T(8,128)(2,1)}, u32[]{:S(2)}, u32[]{:S(2)}) async-start(bf16[8,2,64,256]{3,2,1,0:T(8,128)(2,1)} %whiten.2), calls=%async_computation.1 | async-start | bytes 1048576 | tf_op jit(solution)/shard_map/all_to_all | solution.py:242
  43.4 7.7 %collective-permute-start.12 = (bf16[4,2,64,256]{3,2,1,0:T(8,128)(2,1)S(1)}, bf16[4,2,64,256]{3,2,1,0:T(8,128)(2,1)S(1)}, u32[]{:S(2)}, u32[]{:S(2)}) collective-permute-start(bf16[4,2,64,256]{3,2,1,0:T(8,128)(2,1)S(1)} %collective-permute-done.11.refs_3_), channel_id=1, source_target_pairs={{4,0},{8,4},{12,8},{16,12},{20,16},{24,20},{28,24},{0,28},{5,1},{9... | collective-permute-start | bytes 786440 | tf_op jit(solution)/shard_map/ppermute | solution.py:273
  43.9 9.7 %collective-permute-start.3 = (bf16[4,2,64,256]{3,2,1,0:T(8,128)(2,1)S(1)}, bf16[4,2,64,256]{3,2,1,0:T(8,128)(2,1)S(1)}, u32[]{:S(2)}, u32[]{:S(2)}) collective-permute-start(bf16[4,2,64,256]{3,2,1,0:T(8,128)(2,1)S(1)} %collective-permute-done.2.refs_6_), channel_id=1, source_target_pairs={{0,4},{4,8},{8,12},{12,16},{16,20},{20,24},{24,28},{28,0},{1,5},{5... | collective-permute-start | bytes 786440 | tf_op jit(solution)/shard_map/ppermute | solution.py:271
  44.9 12.8 %collective-permute-start.7 = (bf16[4,2,64,256]{3,2,1,0:T(8,128)(2,1)S(1)}, bf16[4,2,64,256]{3,2,1,0:T(8,128)(2,1)}, u32[]{:S(2)}, u32[]{:S(2)}) collective-permute-start(bf16[4,2,64,256]{3,2,1,0:T(8,128)(2,1)S(1)} %collective-permute-done.6.refs_4_), channel_id=1, source_target_pairs={{0,4},{4,8},{8,12},{12,16},{16,20},{20,24},{24,28},{28,0},{1,5},{5... | collective-permute-start | bytes 786440 | tf_op jit(solution)/shard_map/ppermute | solution.py:271
  44.9 12.7 %collective-permute-start.10 = (bf16[4,2,64,256]{3,2,1,0:T(8,128)(2,1)S(1)}, bf16[4,2,64,256]{3,2,1,0:T(8,128)(2,1)}, u32[]{:S(2)}, u32[]{:S(2)}) collective-permute-start(bf16[4,2,64,256]{3,2,1,0:T(8,128)(2,1)S(1)} %collective-permute-done.9.refs_9_), channel_id=1, source_target_pairs={{4,0},{8,4},{12,8},{16,12},{20,16},{24,20},{28,24},{0,28},{5,1},{9... | collective-permute-start | bytes 786440 | tf_op jit(solution)/shard_map/ppermute | solution.py:273
  51.1 15.5 %collective-permute-start.13 = (bf16[4,2,64,256]{3,2,1,0:T(8,128)(2,1)S(1)}, bf16[4,2,64,256]{3,2,1,0:T(8,128)(2,1)S(1)}, u32[]{:S(2)}, u32[]{:S(2)}) collective-permute-start(bf16[4,2,64,256]{3,2,1,0:T(8,128)(2,1)S(1)} %collective-permute-done.12.refs_5_), channel_id=1, source_target_pairs={{4,0},{8,4},{12,8},{16,12},{20,16},{24,20},{28,24},{0,28},{5,1},{9... | collective-permute-start | bytes 786440 | tf_op jit(solution)/shard_map/ppermute | solution.py:273
  53.6 9.6 %collective-permute-start.4 = (bf16[4,2,64,256]{3,2,1,0:T(8,128)(2,1)S(1)}, bf16[4,2,64,256]{3,2,1,0:T(8,128)(2,1)S(1)}, u32[]{:S(2)}, u32[]{:S(2)}) collective-permute-start(bf16[4,2,64,256]{3,2,1,0:T(8,128)(2,1)S(1)} %collective-permute-done.3.refs_8_), channel_id=1, source_target_pairs={{0,4},{4,8},{8,12},{12,16},{16,20},{20,24},{24,28},{28,0},{1,5},{5... | collective-permute-start | bytes 786440 | tf_op jit(solution)/shard_map/ppermute | solution.py:271
  57.7 11.1 %collective-permute-start.14 = (bf16[4,2,64,256]{3,2,1,0:T(8,128)(2,1)}, bf16[4,2,64,256]{3,2,1,0:T(8,128)(2,1)S(1)}, u32[]{:S(2)}, u32[]{:S(2)}) collective-permute-start(bf16[4,2,64,256]{3,2,1,0:T(8,128)(2,1)} %collective-permute-done.7.refs_2_), channel_id=1, source_target_pairs={{0,4},{4,8},{8,12},{12,16},{16,20},{20,24},{24,28},{28,0},{1,5},{5... | collective-permute-start | bytes 786440 | tf_op jit(solution)/shard_map/ppermute | solution.py:271
  57.9 11.1 %collective-permute-start.15 = (bf16[4,2,64,256]{3,2,1,0:T(8,128)(2,1)}, bf16[4,2,64,256]{3,2,1,0:T(8,128)(2,1)S(1)}, u32[]{:S(2)}, u32[]{:S(2)}) collective-permute-start(bf16[4,2,64,256]{3,2,1,0:T(8,128)(2,1)} %collective-permute-done.10.refs_6_), channel_id=1, source_target_pairs={{4,0},{8,4},{12,8},{16,12},{20,16},{24,20},{28,24},{0,28},{5,1},{9... | collective-permute-start | bytes 786440 | tf_op jit(solution)/shard_map/ppermute | solution.py:273
  63.2 0.7 copy-start.4
  63.9 10.9 %collective-permute-start.5 = (bf16[4,2,64,256]{3,2,1,0:T(8,128)(2,1)S(1)}, bf16[4,2,64,256]{3,2,1,0:T(8,128)(2,1)S(1)}, u32[]{:S(2)}, u32[]{:S(2)}) collective-permute-start(bf16[4,2,64,256]{3,2,1,0:T(8,128)(2,1)S(1)} %get-tuple-element.23.refs_0_), channel_id=1, source_target_pairs={{0,4},{4,8},{8,12},{12,16},{16,20},{20,24},{24,28},{28,0},{1,5},{5... | collective-permute-start | bytes 786440 | tf_op jit(solution)/shard_map/ppermute | solution.py:271
  64.2 10.7 %collective-permute-start.18 = (bf16[4,2,64,256]{3,2,1,0:T(8,128)(2,1)S(1)}, bf16[4,2,64,256]{3,2,1,0:T(8,128)(2,1)S(1)}, u32[]{:S(2)}, u32[]{:S(2)}) collective-permute-start(bf16[4,2,64,256]{3,2,1,0:T(8,128)(2,1)S(1)} %get-tuple-element.24.refs_1_), channel_id=1, source_target_pairs={{4,0},{8,4},{12,8},{16,12},{20,16},{24,20},{28,24},{0,28},{5,1},{9... | collective-permute-start | bytes 786440 | tf_op jit(solution)/shard_map/ppermute | solution.py:273
  66.6 0.7 copy-start.2
  67.3 21.4 %collective-permute-start.21 = (bf16[4,2,64,256]{3,2,1,0:T(8,128)(2,1)S(1)}, bf16[4,2,64,256]{3,2,1,0:T(8,128)(2,1)S(1)}, u32[]{:S(2)}, u32[]{:S(2)}) collective-permute-start(bf16[4,2,64,256]{3,2,1,0:T(8,128)(2,1)S(1)} %get-tuple-element.23.refs_0_), channel_id=1, source_target_pairs={{4,0},{8,4},{12,8},{16,12},{20,16},{24,20},{28,24},{0,28},{5,1},{9... | collective-permute-start | bytes 786440 | tf_op jit(solution)/shard_map/ppermute | solution.py:273
  68.8 20.6 %collective-permute-start.23 = (bf16[4,2,64,256]{3,2,1,0:T(8,128)(2,1)S(1)}, bf16[4,2,64,256]{3,2,1,0:T(8,128)(2,1)S(1)}, u32[]{:S(2)}, u32[]{:S(2)}) collective-permute-start(bf16[4,2,64,256]{3,2,1,0:T(8,128)(2,1)S(1)} %get-tuple-element.24.refs_1_), channel_id=1, source_target_pairs={{0,4},{4,8},{8,12},{12,16},{16,20},{20,24},{24,28},{28,0},{1,5},{5... | collective-permute-start | bytes 786440 | tf_op jit(solution)/shard_map/ppermute | solution.py:271
  69.1 1.0 copy-start.3
  70.0 0.9 copy-start.5
  74.7 18.9 %copy-start.9 = (f32[8]{0:T(128)S(1)}, f32[8]{0:T(128)}, u32[]{:S(2)}) copy-start(f32[8]{0:T(128)} %constant.34.clone) | copy-start | bytes 100
  74.8 16.2 %collective-permute-start.16 = (bf16[4,2,64,256]{3,2,1,0:T(8,128)(2,1)S(1)}, bf16[4,2,64,256]{3,2,1,0:T(8,128)(2,1)}, u32[]{:S(2)}, u32[]{:S(2)}) collective-permute-start(bf16[4,2,64,256]{3,2,1,0:T(8,128)(2,1)S(1)} %collective-permute-done.5.refs_2_), channel_id=1, source_target_pairs={{0,4},{4,8},{8,12},{12,16},{16,20},{20,24},{24,28},{28,0},{1,5},{5... | collective-permute-start | bytes 786440 | tf_op jit(solution)/shard_map/ppermute | solution.py:271
  74.9 16.1 %collective-permute-start.19 = (bf16[4,2,64,256]{3,2,1,0:T(8,128)(2,1)S(1)}, bf16[4,2,64,256]{3,2,1,0:T(8,128)(2,1)}, u32[]{:S(2)}, u32[]{:S(2)}) collective-permute-start(bf16[4,2,64,256]{3,2,1,0:T(8,128)(2,1)S(1)} %collective-permute-done.18.refs_7_), channel_id=1, source_target_pairs={{4,0},{8,4},{12,8},{16,12},{20,16},{24,20},{28,24},{0,28},{5,1},{9... | collective-permute-start | bytes 786440 | tf_op jit(solution)/shard_map/ppermute | solution.py:273
  77.5 41.5 %all-to-all-start.2 = ((bf16[32,2,64,256]{3,2,1,0:T(8,128)(2,1)}), bf16[32,2,64,256]{3,2,1,0:T(8,128)(2,1)}, u32[]{:S(2)}, u32[]{:S(2)}) async-start(bf16[32,2,64,256]{3,2,1,0:T(8,128)(2,1)} %bitcast.4), calls=%async_computation.2 | async-start | bytes 4194304 | tf_op jit(solution)/shard_map/all_to_all | solution.py:293
  88.6 7.8 %collective-permute-start.22 = (bf16[4,2,64,256]{3,2,1,0:T(8,128)(2,1)S(1)}, bf16[4,2,64,256]{3,2,1,0:T(8,128)(2,1)}, u32[]{:S(2)}, u32[]{:S(2)}) collective-permute-start(bf16[4,2,64,256]{3,2,1,0:T(8,128)(2,1)S(1)} %collective-permute-done.21.refs_3_), channel_id=1, source_target_pairs={{4,0},{8,4},{12,8},{16,12},{20,16},{24,20},{28,24},{0,28},{5,1},{9... | collective-permute-start | bytes 786440 | tf_op jit(solution)/shard_map/ppermute | solution.py:273
  89.4 8.9 %collective-permute-start.24 = (bf16[4,2,64,256]{3,2,1,0:T(8,128)(2,1)S(1)}, bf16[4,2,64,256]{3,2,1,0:T(8,128)(2,1)}, u32[]{:S(2)}, u32[]{:S(2)}) collective-permute-start(bf16[4,2,64,256]{3,2,1,0:T(8,128)(2,1)S(1)} %collective-permute-done.23.refs_6_), channel_id=1, source_target_pairs={{0,4},{4,8},{8,12},{12,16},{16,20},{20,24},{24,28},{28,0},{1,5},{5... | collective-permute-start | bytes 786440 | tf_op jit(solution)/shard_map/ppermute | solution.py:271
  90.2 0.7 copy-start
  90.9 12.7 %collective-permute-start.17 = (bf16[4,2,64,256]{3,2,1,0:T(8,128)(2,1)}, bf16[4,2,64,256]{3,2,1,0:T(8,128)(2,1)S(1)}, u32[]{:S(2)}, u32[]{:S(2)}) collective-permute-start(bf16[4,2,64,256]{3,2,1,0:T(8,128)(2,1)} %collective-permute-done.16.refs_4_), channel_id=1, source_target_pairs={{0,4},{4,8},{8,12},{12,16},{16,20},{20,24},{24,28},{28,0},{1,5},{5... | collective-permute-start | bytes 786440 | tf_op jit(solution)/shard_map/ppermute | solution.py:271
  90.9 12.7 %collective-permute-start.20 = (bf16[4,2,64,256]{3,2,1,0:T(8,128)(2,1)}, bf16[4,2,64,256]{3,2,1,0:T(8,128)(2,1)S(1)}, u32[]{:S(2)}, u32[]{:S(2)}) collective-permute-start(bf16[4,2,64,256]{3,2,1,0:T(8,128)(2,1)} %collective-permute-done.19.refs_9_), channel_id=1, source_target_pairs={{4,0},{8,4},{12,8},{16,12},{20,16},{24,20},{28,24},{0,28},{5,1},{9... | collective-permute-start | bytes 786440 | tf_op jit(solution)/shard_map/ppermute | solution.py:273
  96.4 11.2 %collective-permute-start.25 = (bf16[4,2,64,256]{3,2,1,0:T(8,128)(2,1)}, bf16[4,2,64,256]{3,2,1,0:T(8,128)(2,1)S(1)}, u32[]{:S(2)}, u32[]{:S(2)}) collective-permute-start(bf16[4,2,64,256]{3,2,1,0:T(8,128)(2,1)} %collective-permute-done.22.refs_5_), channel_id=1, source_target_pairs={{4,0},{8,4},{12,8},{16,12},{20,16},{24,20},{28,24},{0,28},{5,1},{9... | collective-permute-start | bytes 786440 | tf_op jit(solution)/shard_map/ppermute | solution.py:273
  98.3 10.8 %collective-permute-start.27 = (bf16[4,2,64,256]{3,2,1,0:T(8,128)(2,1)}, bf16[4,2,64,256]{3,2,1,0:T(8,128)(2,1)S(1)}, u32[]{:S(2)}, u32[]{:S(2)}) collective-permute-start(bf16[4,2,64,256]{3,2,1,0:T(8,128)(2,1)} %collective-permute-done.24.refs_8_), channel_id=1, source_target_pairs={{0,4},{4,8},{8,12},{12,16},{16,20},{20,24},{24,28},{28,0},{1,5},{5... | collective-permute-start | bytes 786440 | tf_op jit(solution)/shard_map/ppermute | solution.py:271
  98.3 1.0 copy-start.1
  103.6 11.2 %collective-permute-start.26 = (bf16[4,2,64,256]{3,2,1,0:T(8,128)(2,1)S(1)}, bf16[4,2,64,256]{3,2,1,0:T(8,128)(2,1)S(1)}, u32[]{:S(2)}, u32[]{:S(2)}) collective-permute-start(bf16[4,2,64,256]{3,2,1,0:T(8,128)(2,1)S(1)} %collective-permute-done.17.refs_2_), channel_id=1, source_target_pairs={{0,4},{4,8},{8,12},{12,16},{16,20},{20,24},{24,28},{28,0},{1,5},{5... | collective-permute-start | bytes 786440 | tf_op jit(solution)/shard_map/ppermute | solution.py:271
  103.6 11.2 %collective-permute-start.28 = (bf16[4,2,64,256]{3,2,1,0:T(8,128)(2,1)S(1)}, bf16[4,2,64,256]{3,2,1,0:T(8,128)(2,1)S(1)}, u32[]{:S(2)}, u32[]{:S(2)}) collective-permute-start(bf16[4,2,64,256]{3,2,1,0:T(8,128)(2,1)S(1)} %collective-permute-done.20.refs_6_), channel_id=1, source_target_pairs={{4,0},{8,4},{12,8},{16,12},{20,16},{24,20},{28,24},{0,28},{5,1},{9... | collective-permute-start | bytes 786440 | tf_op jit(solution)/shard_map/ppermute | solution.py:273
  121.6 35.8 %copy-start.6 = (bf16[128,128]{1,0:T(8,128)(2,1)S(1)}, bf16[128,128]{1,0:T(8,128)(2,1)}, u32[]{:S(2)}) copy-start(bf16[128,128]{1,0:T(8,128)(2,1)} %constant.36.clone.t_ref) | copy-start | bytes 98308

commit v6 on v4

--- a/solution.py
+++ b/solution.py
@@ -259,7 +259,6 @@
         if t == 1:
             own, _ = lax.optimization_barrier((regroup(t), white[0]))
         else:
-            white[0], _ = lax.optimization_barrier((white[0], ups[0][0]))
             own = regroup(t)
             own, _ = lax.optimization_barrier((own, ups[1][2]))
         ups, dns, near_parts = ring(own, parts if t == 0 else None, t)

time: 162 us -> 162 us (level)
  no operation moved by 1% of the time
where the time goes in v6:
time: 162 us
  starting transfers between devices  62.9 us (39%)
  blocking collectives  36.7 us (23%)
  waiting for transfers between devices  29.4 us (18%)
  Pallas kernels  24.9 us (15%)
  local copies, waits for them, and re-layouts  7.61 us (5%)
    all_to_all x1, blocking collectives, shards(): lax.all_to_all(parts, PLANE, split_axis=0, concat_axis=0, tiled=True)  36.7 us
    ppermute x14, starting transfers between devices, ring(): dns[side].append(lax.ppermute(dns[side][-1] if s else own[side], 'z', dn))  30.3 us
    ppermute x14, waiting for transfers between devices, ring(): ups[side].append(lax.ppermute(ups[side][-1] if s else own[side], 'z', up))  16.1 us
    all_to_all x2, starting transfers between devices, regroup(): lax.all_to_all(white[t], PLANE, split_axis=0, concat_axis=0, tiled=True,...  15.4 us
    pallas_call x4, Pallas kernels, cross(): pl.pallas_call(functools.partial(cross_kernel, first, count), grid_spec=p...  13.9 us
    all_to_all x1, starting transfers between devices, shards(): lax.all_to_all(parts, PLANE, split_axis=0, concat_axis=0, tiled=True)  10.1 us
    pallas_call x1, Pallas kernels, lags(): pl.pallas_call(lags_kernel, grid=(CH // ROWS,), in_specs=[pl.BlockSpec((L...  7.05 us
    ppermute x14, waiting for transfers between devices, ring(): dns[side].append(lax.ppermute(dns[side][-1] if s else own[side], 'z', dn))  6.49 us
  transfers between devices with their start and end apart: 32, of which 12 were waited for; matrix products, arithmetic and copies ran while one was open for 1% of the time, Pallas kernels for 10%

profile of v6, /device:TPU:1, one launch (start us, length us, event | category | flops | bytes accessed | tf_op | source)
XLA Modules:
  0.0 161.8 jit_solution(17040573345427431909)
XLA Ops:
  0.0 1.9 %whiten.2 = bf16[8,2,64,256]{3,2,1,0:T(8,128)(2,1)} custom-call(s32[1]{0:T(128)} %bitcast.1.hi_ref, bf16[2,8,2,64,256]{4,3,2,1,0:T(8,128)(2,1)} %bitcast.10), custom_call_target="tpu_custom_call" | custom-call | flops 2000000 | bytes 1048576 | tf_op jit(solution)/shard_map/whiten/pallas_call | solution.py:77
  1.9 8.2 %all-to-all-start = ((bf16[8,2,64,256]{3,2,1,0:T(8,128)(2,1)}), bf16[8,2,64,256]{3,2,1,0:T(8,128)(2,1)S(1)}, u32[]{:S(2)}, u32[]{:S(2)}) async-start(bf16[8,2,64,256]{3,2,1,0:T(8,128)(2,1)} %whiten.2), calls=%async_computation | async-start | bytes 1048576 | tf_op jit(solution)/shard_map/all_to_all | solution.py:222
  10.1 0.9 slice_bitcast_fusion
  11.0 2.1 %collective-permute-start = (bf16[2,64,256]{2,1,0:T(8,128)(2,1)S(1)}, bf16[2,64,256]{2,1,0:T(8,128)(2,1)S(1)}, u32[]{:S(2)}, u32[]{:S(2)}) collective-permute-start(bf16[2,64,256]{2,1,0:T(8,128)(2,1)S(1)} %slice_bitcast_fusion), channel_id=1, source_target_pairs={{32,0},{64,32},{96,64},{0,96},{33,1},{65,33},{97,65},{1,97},{34,2}... | collective-permute-start | bytes 196616 | tf_op jit(solution)/shard_map/ppermute | solution.py:215
  13.1 4.6 %collective-permute-done.refs_0_ = bf16[2,64,256]{2,1,0:T(8,128)(2,1)S(1)} collective-permute-done((bf16[2,64,256]{2,1,0:T(8,128)(2,1)S(1)}, bf16[2,64,256]{2,1,0:T(8,128)(2,1)S(1)}, u32[]{:S(2)}, u32[]{:S(2)}) %collective-permute-start) | collective-permute-done | bytes 65568 | tf_op jit(solution)/shard_map/ppermute | solution.py:215
  17.7 0.6 copy-done.8
  18.3 2.1 %whiten.3 = bf16[8,2,64,256]{3,2,1,0:T(8,128)(2,1)} custom-call(s32[1]{0:T(128)} %bitcast.1.hi_ref, bf16[2,8,2,64,256]{4,3,2,1,0:T(8,128)(2,1)} %bitcast.11, bf16[2,64,256]{2,1,0:T(8,128)(2,1)} %copy-done.8), custom_call_target="tpu_custom_call" | custom-call | flops 2000000 | bytes 1048576 | tf_op jit(solution)/shard_map/whiten/pallas_call | solution.py:77
  20.3 1.6 %all-to-all-done = bf16[8,2,64,256]{3,2,1,0:T(8,128)(2,1)S(1)} async-done(((bf16[8,2,64,256]{3,2,1,0:T(8,128)(2,1)}), bf16[8,2,64,256]{3,2,1,0:T(8,128)(2,1)S(1)}, u32[]{:S(2)}, u32[]{:S(2)}) %all-to-all-start) | async-done | bytes 524320 | tf_op jit(solution)/shard_map/all_to_all | solution.py:222
  22.0 1.7 %collective-permute-start.1 = (bf16[4,2,64,256]{3,2,1,0:T(8,128)(2,1)S(1)}, bf16[4,2,64,256]{3,2,1,0:T(8,128)(2,1)S(1)}, u32[]{:S(2)}, u32[]{:S(2)}) collective-permute-start(bf16[4,2,64,256]{3,2,1,0:T(8,128)(2,1)S(1)} %get-tuple-element.17.refs_0_), channel_id=1, source_target_pairs={{0,4},{4,8},{8,12},{12,16},{16,20},{20,24},{24,28},{28,0},{1,5},{5... | collective-permute-start | bytes 786440 | tf_op jit(solution)/shard_map/ppermute | solution.py:251
  23.8 4.0 %collective-permute-start.4 = (bf16[4,2,64,256]{3,2,1,0:T(8,128)(2,1)S(1)}, bf16[4,2,64,256]{3,2,1,0:T(8,128)(2,1)S(1)}, u32[]{:S(2)}, u32[]{:S(2)}) collective-permute-start(bf16[4,2,64,256]{3,2,1,0:T(8,128)(2,1)S(1)} %get-tuple-element.18.refs_1_), channel_id=1, source_target_pairs={{4,0},{8,4},{12,8},{16,12},{20,16},{24,20},{28,24},{0,28},{5,1},{9... | collective-permute-start | bytes 786440 | tf_op jit(solution)/shard_map/ppermute | solution.py:253
  27.8 1.4 collective-permute-start.7
  29.2 4.2 %collective-permute-done.1.refs_2_ = bf16[4,2,64,256]{3,2,1,0:T(8,128)(2,1)S(1)} collective-permute-done((bf16[4,2,64,256]{3,2,1,0:T(8,128)(2,1)S(1)}, bf16[4,2,64,256]{3,2,1,0:T(8,128)(2,1)S(1)}, u32[]{:S(2)}, u32[]{:S(2)}) %collective-permute-start.1) | collective-permute-done | bytes 262176 | tf_op jit(solution)/shard_map/ppermute | solution.py:251
  33.5 2.7 %collective-permute-start.5 = (bf16[4,2,64,256]{3,2,1,0:T(8,128)(2,1)S(1)}, bf16[4,2,64,256]{3,2,1,0:T(8,128)(2,1)S(1)}, u32[]{:S(2)}, u32[]{:S(2)}) collective-permute-start(bf16[4,2,64,256]{3,2,1,0:T(8,128)(2,1)S(1)} %collective-permute-done.4.refs_7_), channel_id=1, source_target_pairs={{4,0},{8,4},{12,8},{16,12},{20,16},{24,20},{28,24},{0,28},{5,1},{9... | collective-permute-start | bytes 786440 | tf_op jit(solution)/shard_map/ppermute | solution.py:253
  36.2 7.2 %all-to-all-start.2 = ((bf16[8,2,64,256]{3,2,1,0:T(8,128)(2,1)}), bf16[8,2,64,256]{3,2,1,0:T(8,128)(2,1)}, u32[]{:S(2)}, u32[]{:S(2)}) async-start(bf16[8,2,64,256]{3,2,1,0:T(8,128)(2,1)} %whiten.3), calls=%async_computation.2 | async-start | bytes 1048576 | tf_op jit(solution)/shard_map/all_to_all | solution.py:222
  43.4 0.5 collective-permute-start.8
  43.9 1.0 collective-permute-start.10
  44.9 2.6 %collective-permute-start.6 = (bf16[4,2,64,256]{3,2,1,0:T(8,128)(2,1)S(1)}, bf16[4,2,64,256]{3,2,1,0:T(8,128)(2,1)}, u32[]{:S(2)}, u32[]{:S(2)}) collective-permute-start(bf16[4,2,64,256]{3,2,1,0:T(8,128)(2,1)S(1)} %collective-permute-done.5.refs_9_), channel_id=1, source_target_pairs={{4,0},{8,4},{12,8},{16,12},{20,16},{24,20},{28,24},{0,28},{5,1},{9... | collective-permute-start | bytes 786440 | tf_op jit(solution)/shard_map/ppermute | solution.py:253
  47.5 3.5 %collective-permute-done.8.refs_5_ = bf16[4,2,64,256]{3,2,1,0:T(8,128)(2,1)S(1)} collective-permute-done((bf16[4,2,64,256]{3,2,1,0:T(8,128)(2,1)S(1)}, bf16[4,2,64,256]{3,2,1,0:T(8,128)(2,1)S(1)}, u32[]{:S(2)}, u32[]{:S(2)}) %collective-permute-start.8) | collective-permute-done | bytes 262176 | tf_op jit(solution)/shard_map/ppermute | solution.py:253
  51.1 2.5 %collective-permute-start.11 = (bf16[4,2,64,256]{3,2,1,0:T(8,128)(2,1)S(1)}, bf16[4,2,64,256]{3,2,1,0:T(8,128)(2,1)S(1)}, u32[]{:S(2)}, u32[]{:S(2)}) collective-permute-start(bf16[4,2,64,256]{3,2,1,0:T(8,128)(2,1)S(1)} %collective-permute-done.8.refs_5_), channel_id=1, source_target_pairs={{4,0},{8,4},{12,8},{16,12},{20,16},{24,20},{28,24},{0,28},{5,1},{9... | collective-permute-start | bytes 786440 | tf_op jit(solution)/shard_map/ppermute | solution.py:253
  53.6 4.1 %cross.4.refs_8_ = bf16[8,4,2,64,256]{4,3,2,1,0:T(8,128)(2,1)} custom-call(s32[1]{0:T(128)} %bitcast.z_ref, f32[8]{0:T(128)S(1)} %copy-done.7, bf16[4,2,64,256]{3,2,1,0:T(8,128)(2,1)S(1)} %get-tuple-element.17.refs_0_, bf16[4,2,64,256]{3,2,1,0:T(8,128)(2,1)S(1)} %get-tuple-element.18.refs_1_, bf16[4,2,64,256]{3,2,1,0:T(8,128)(2,1)S(1)} %collective-permute-done.1.refs_2_, ...), custom_call_target="tpu_custom_call" | custom-call | flops 1073741824 | bytes 4194304 | tf_op jit(solution)/shard_map/cross/pallas_call | solution.py:162
  57.9 2.8 %collective-permute-start.14 = (bf16[4,2,64,256]{3,2,1,0:T(8,128)(2,1)}, bf16[4,2,64,256]{3,2,1,0:T(8,128)(2,1)S(1)}, u32[]{:S(2)}, u32[]{:S(2)}) collective-permute-start(bf16[4,2,64,256]{3,2,1,0:T(8,128)(2,1)} %collective-permute-done.6.refs_6_), channel_id=1, source_target_pairs={{4,0},{8,4},{12,8},{16,12},{20,16},{24,20},{28,24},{0,28},{5,1},{9... | collective-permute-start | bytes 786440 | tf_op jit(solution)/shard_map/ppermute | solution.py:253
  60.7 1.1 fusion
  61.8 1.4 collective-permute-done.13.refs_5_
  63.2 0.7 copy-done.4
  63.9 1.5 collective-permute-start.15
  65.3 0.7 copy-done.2
  66.1 1.3 collective-permute-start.21
  67.4 1.4 collective-permute-done.12.refs_4_
  69.1 0.9 copy-done.3
  70.0 0.9 copy-done.5
  71.0 3.8 %cross.5 = bf16[8,4,2,64,256]{4,3,2,1,0:T(8,128)(2,1)} custom-call(s32[1]{0:T(128)} %bitcast.z_ref, f32[8]{0:T(128)S(1)} %copy-done.7, bf16[4,2,64,256]{3,2,1,0:T(8,128)(2,1)S(1)} %get-tuple-element.17.refs_0_, bf16[4,2,64,256]{3,2,1,0:T(8,128)(2,1)S(1)} %get-tuple-element.18.refs_1_, ...), custom_call_target="tpu_custom_call", output_to_operand_aliasing={{}: (10, {})} | custom-call | flops 536870912 | bytes 4194304 | tf_op jit(solution)/shard_map/cross/pallas_call | solution.py:162
  74.9 2.7 %collective-permute-start.19 = (bf16[4,2,64,256]{3,2,1,0:T(8,128)(2,1)S(1)}, bf16[4,2,64,256]{3,2,1,0:T(8,128)(2,1)}, u32[]{:S(2)}, u32[]{:S(2)}) collective-permute-start(bf16[4,2,64,256]{3,2,1,0:T(8,128)(2,1)S(1)} %collective-permute-done.18.refs_7_), channel_id=1, source_target_pairs={{4,0},{8,4},{12,8},{16,12},{20,16},{24,20},{28,24},{0,28},{5,1},{9... | collective-permute-start | bytes 786440 | tf_op jit(solution)/shard_map/ppermute | solution.py:253
  77.5 10.1 %all-to-all-start.1 = ((bf16[32,2,64,256]{3,2,1,0:T(8,128)(2,1)}), bf16[32,2,64,256]{3,2,1,0:T(8,128)(2,1)}, u32[]{:S(2)}, u32[]{:S(2)}) async-start(bf16[32,2,64,256]{3,2,1,0:T(8,128)(2,1)} %bitcast.4), calls=%async_computation.1 | async-start | bytes 4194304 | tf_op jit(solution)/shard_map/all_to_all | solution.py:269
  87.7 1.7 %collective-permute-start.22 = (bf16[4,2,64,256]{3,2,1,0:T(8,128)(2,1)S(1)}, bf16[4,2,64,256]{3,2,1,0:T(8,128)(2,1)}, u32[]{:S(2)}, u32[]{:S(2)}) collective-permute-start(bf16[4,2,64,256]{3,2,1,0:T(8,128)(2,1)S(1)} %collective-permute-done.21.refs_3_), channel_id=1, source_target_pairs={{4,0},{8,4},{12,8},{16,12},{20,16},{24,20},{28,24},{0,28},{5,1},{9... | collective-permute-start | bytes 786440 | tf_op jit(solution)/shard_map/ppermute | solution.py:253
  89.4 0.7 copy-done
  90.2 2.7 %collective-permute-start.20 = (bf16[4,2,64,256]{3,2,1,0:T(8,128)(2,1)}, bf16[4,2,64,256]{3,2,1,0:T(8,128)(2,1)S(1)}, u32[]{:S(2)}, u32[]{:S(2)}) collective-permute-start(bf16[4,2,64,256]{3,2,1,0:T(8,128)(2,1)} %collective-permute-done.19.refs_9_), channel_id=1, source_target_pairs={{4,0},{8,4},{12,8},{16,12},{20,16},{24,20},{28,24},{0,28},{5,1},{9... | collective-permute-start | bytes 786440 | tf_op jit(solution)/shard_map/ppermute | solution.py:253
  92.9 2.5 %collective-permute-done.22.refs_5_ = bf16[4,2,64,256]{3,2,1,0:T(8,128)(2,1)} collective-permute-done((bf16[4,2,64,256]{3,2,1,0:T(8,128)(2,1)S(1)}, bf16[4,2,64,256]{3,2,1,0:T(8,128)(2,1)}, u32[]{:S(2)}, u32[]{:S(2)}) %collective-permute-start.22) | collective-permute-done | bytes 262176 | tf_op jit(solution)/shard_map/ppermute | solution.py:253
  95.4 2.9 %collective-permute-start.25 = (bf16[4,2,64,256]{3,2,1,0:T(8,128)(2,1)}, bf16[4,2,64,256]{3,2,1,0:T(8,128)(2,1)S(1)}, u32[]{:S(2)}, u32[]{:S(2)}) collective-permute-start(bf16[4,2,64,256]{3,2,1,0:T(8,128)(2,1)} %collective-permute-done.22.refs_5_), channel_id=1, source_target_pairs={{4,0},{8,4},{12,8},{16,12},{20,16},{24,20},{28,24},{0,28},{5,1},{9... | collective-permute-start | bytes 786440 | tf_op jit(solution)/shard_map/ppermute | solution.py:253
  98.3 0.9 copy-done.1
  99.3 3.4 %cross.6.refs_8_ = bf16[8,4,2,64,256]{4,3,2,1,0:T(8,128)(2,1)S(1)} custom-call(s32[1]{0:T(128)} %bitcast.z_ref, f32[8]{0:T(128)S(1)} %broadcast_select_fusion.coef_ref, bf16[4,2,64,256]{3,2,1,0:T(8,128)(2,1)S(1)} %get-tuple-element.21.refs_0_, bf16[4,2,64,256]{3,2,1,0:T(8,128)(2,1)S(1)} %get-tuple-element.22.refs_1_, ...), custom_call_target="tpu_custom_call" | custom-call | flops 1073741824 | bytes 4194304 | tf_op jit(solution)/shard_map/cross/pallas_call | solution.py:162
  102.7 0.9 collective-permute-done.17.refs_2_
  103.6 2.7 %collective-permute-start.28 = (bf16[4,2,64,256]{3,2,1,0:T(8,128)(2,1)S(1)}, bf16[4,2,64,256]{3,2,1,0:T(8,128)(2,1)S(1)}, u32[]{:S(2)}, u32[]{:S(2)}) collective-permute-start(bf16[4,2,64,256]{3,2,1,0:T(8,128)(2,1)S(1)} %collective-permute-done.20.refs_6_), channel_id=1, source_target_pairs={{4,0},{8,4},{12,8},{16,12},{20,16},{24,20},{28,24},{0,28},{5,1},{9... | collective-permute-start | bytes 786440 | tf_op jit(solution)/shard_map/ppermute | solution.py:253
  106.7 2.5 %collective-permute-done.27.refs_5_ = bf16[4,2,64,256]{3,2,1,0:T(8,128)(2,1)S(1)} collective-permute-done((bf16[4,2,64,256]{3,2,1,0:T(8,128)(2,1)}, bf16[4,2,64,256]{3,2,1,0:T(8,128)(2,1)S(1)}, u32[]{:S(2)}, u32[]{:S(2)}) %collective-permute-start.27) | collective-permute-done | bytes 262176 | tf_op jit(solution)/shard_map/ppermute | solution.py:251
  109.2 5.6 %collective-permute-done.26.refs_4_ = bf16[4,2,64,256]{3,2,1,0:T(8,128)(2,1)S(1)} collective-permute-done((bf16[4,2,64,256]{3,2,1,0:T(8,128)(2,1)S(1)}, bf16[4,2,64,256]{3,2,1,0:T(8,128)(2,1)S(1)}, u32[]{:S(2)}, u32[]{:S(2)}) %collective-permute-start.26) | collective-permute-done | bytes 262176 | tf_op jit(solution)/shard_map/ppermute | solution.py:251
  114.8 2.6 %cross.7 = bf16[8,4,2,64,256]{4,3,2,1,0:T(8,128)(2,1)S(1)} custom-call(s32[1]{0:T(128)} %bitcast.z_ref, f32[8]{0:T(128)S(1)} %broadcast_select_fusion.coef_ref, bf16[4,2,64,256]{3,2,1,0:T(8,128)(2,1)S(1)} %get-tuple-element.21.refs_0_, bf16[4,2,64,256]{3,2,1,0:T(8,128)(2,1)S(1)} %get-tuple-element.22.refs_1_, ...), custom_call_target="tpu_custom_call", output_to_operand_aliasing={{}: (10, {})} | custom-call | flops 12884901888 | bytes 4194304 | tf_op jit(solution)/shard_map/cross/pallas_call | solution.py:162
  117.4 0.6 all-to-all-done.1.x1_ref
  118.0 36.7 %all_to_all.20.x0_ref = bf16[32,2,64,256]{3,2,1,0:T(8,128)(2,1)S(1)} all-to-all(bf16[32,2,64,256]{3,2,1,0:T(8,128)(2,1)S(1)} %bitcast.9), channel_id=1, replica_groups=mesh['yh'=2,'x'=4,'z'=8,'yl'=2,'co'=2] {'yh','x','yl','co'}, dimensions={0} | all-to-all | bytes 4194304 | tf_op jit(solution)/shard_map/all_to_all | solution.py:269
  154.7 7.0 %lags.1 = f32[128,64,256]{2,1,0:T(8,128)} custom-call(bf16[128,128]{1,0:T(8,128)(2,1)S(1)} %copy-done.6, bf16[32,2,64,256]{3,2,1,0:T(8,128)(2,1)} %all-to-all-done.1.x1_ref, bf16[32,2,64,256]{3,2,1,0:T(8,128)(2,1)S(1)} %all_to_all.20.x0_ref), custom_call_target="tpu_custom_call" | custom-call | flops 536870912 | bytes 12582912 | tf_op jit(solution)/shard_map/lags/pallas_call | solution.py:197
  (48 shorter events, 1.4 us)
Async XLA Ops:
  1.9 20.0 %all-to-all-start = ((bf16[8,2,64,256]{3,2,1,0:T(8,128)(2,1)}), bf16[8,2,64,256]{3,2,1,0:T(8,128)(2,1)S(1)}, u32[]{:S(2)}, u32[]{:S(2)}) async-start(bf16[8,2,64,256]{3,2,1,0:T(8,128)(2,1)} %whiten.2), calls=%async_computation | async-start | bytes 1048576 | tf_op jit(solution)/shard_map/all_to_all | solution.py:222
  10.1 43.4 %copy-start.7 = (f32[8]{0:T(128)S(1)}, f32[8]{0:T(128)}, u32[]{:S(2)}) copy-start(f32[8]{0:T(128)} %constant.35.clone.coef_ref) | copy-start | bytes 100
  11.0 6.7 %collective-permute-start = (bf16[2,64,256]{2,1,0:T(8,128)(2,1)S(1)}, bf16[2,64,256]{2,1,0:T(8,128)(2,1)S(1)}, u32[]{:S(2)}, u32[]{:S(2)}) collective-permute-start(bf16[2,64,256]{2,1,0:T(8,128)(2,1)S(1)} %slice_bitcast_fusion), channel_id=1, source_target_pairs={{32,0},{64,32},{96,64},{0,96},{33,1},{65,33},{97,65},{1,97},{34,2}... | collective-permute-start | bytes 196616 | tf_op jit(solution)/shard_map/ppermute | solution.py:215
  17.7 0.6 copy-start.8
  22.0 11.5 %collective-permute-start.1 = (bf16[4,2,64,256]{3,2,1,0:T(8,128)(2,1)S(1)}, bf16[4,2,64,256]{3,2,1,0:T(8,128)(2,1)S(1)}, u32[]{:S(2)}, u32[]{:S(2)}) collective-permute-start(bf16[4,2,64,256]{3,2,1,0:T(8,128)(2,1)S(1)} %get-tuple-element.17.refs_0_), channel_id=1, source_target_pairs={{0,4},{4,8},{8,12},{12,16},{16,20},{20,24},{24,28},{28,0},{1,5},{5... | collective-permute-start | bytes 786440 | tf_op jit(solution)/shard_map/ppermute | solution.py:251
  23.8 9.8 %collective-permute-start.4 = (bf16[4,2,64,256]{3,2,1,0:T(8,128)(2,1)S(1)}, bf16[4,2,64,256]{3,2,1,0:T(8,128)(2,1)S(1)}, u32[]{:S(2)}, u32[]{:S(2)}) collective-permute-start(bf16[4,2,64,256]{3,2,1,0:T(8,128)(2,1)S(1)} %get-tuple-element.18.refs_1_), channel_id=1, source_target_pairs={{4,0},{8,4},{12,8},{16,12},{20,16},{24,20},{28,24},{0,28},{5,1},{9... | collective-permute-start | bytes 786440 | tf_op jit(solution)/shard_map/ppermute | solution.py:253
  27.8 15.6 %collective-permute-start.7 = (bf16[4,2,64,256]{3,2,1,0:T(8,128)(2,1)S(1)}, bf16[4,2,64,256]{3,2,1,0:T(8,128)(2,1)S(1)}, u32[]{:S(2)}, u32[]{:S(2)}) collective-permute-start(bf16[4,2,64,256]{3,2,1,0:T(8,128)(2,1)S(1)} %get-tuple-element.17.refs_0_), channel_id=1, source_target_pairs={{4,0},{8,4},{12,8},{16,12},{20,16},{24,20},{28,24},{0,28},{5,1},{9... | collective-permute-start | bytes 786440 | tf_op jit(solution)/shard_map/ppermute | solution.py:253
  29.2 14.7 %collective-permute-start.9 = (bf16[4,2,64,256]{3,2,1,0:T(8,128)(2,1)S(1)}, bf16[4,2,64,256]{3,2,1,0:T(8,128)(2,1)S(1)}, u32[]{:S(2)}, u32[]{:S(2)}) collective-permute-start(bf16[4,2,64,256]{3,2,1,0:T(8,128)(2,1)S(1)} %get-tuple-element.18.refs_1_), channel_id=1, source_target_pairs={{0,4},{4,8},{8,12},{12,16},{16,20},{20,24},{24,28},{28,0},{1,5},{5... | collective-permute-start | bytes 786440 | tf_op jit(solution)/shard_map/ppermute | solution.py:251
  33.5 11.4 %collective-permute-start.2 = (bf16[4,2,64,256]{3,2,1,0:T(8,128)(2,1)S(1)}, bf16[4,2,64,256]{3,2,1,0:T(8,128)(2,1)S(1)}, u32[]{:S(2)}, u32[]{:S(2)}) collective-permute-start(bf16[4,2,64,256]{3,2,1,0:T(8,128)(2,1)S(1)} %collective-permute-done.1.refs_2_), channel_id=1, source_target_pairs={{0,4},{4,8},{8,12},{12,16},{16,20},{20,24},{24,28},{28,0},{1,5},{5... | collective-permute-start | bytes 786440 | tf_op jit(solution)/shard_map/ppermute | solution.py:251
  33.5 11.4 %collective-permute-start.5 = (bf16[4,2,64,256]{3,2,1,0:T(8,128)(2,1)S(1)}, bf16[4,2,64,256]{3,2,1,0:T(8,128)(2,1)S(1)}, u32[]{:S(2)}, u32[]{:S(2)}) collective-permute-start(bf16[4,2,64,256]{3,2,1,0:T(8,128)(2,1)S(1)} %collective-permute-done.4.refs_7_), channel_id=1, source_target_pairs={{4,0},{8,4},{12,8},{16,12},{20,16},{24,20},{28,24},{0,28},{5,1},{9... | collective-permute-start | bytes 786440 | tf_op jit(solution)/shard_map/ppermute | solution.py:253
  36.2 24.5 %all-to-all-start.2 = ((bf16[8,2,64,256]{3,2,1,0:T(8,128)(2,1)}), bf16[8,2,64,256]{3,2,1,0:T(8,128)(2,1)}, u32[]{:S(2)}, u32[]{:S(2)}) async-start(bf16[8,2,64,256]{3,2,1,0:T(8,128)(2,1)} %whiten.3), calls=%async_computation.2 | async-start | bytes 1048576 | tf_op jit(solution)/shard_map/all_to_all | solution.py:222
  43.4 7.7 %collective-permute-start.8 = (bf16[4,2,64,256]{3,2,1,0:T(8,128)(2,1)S(1)}, bf16[4,2,64,256]{3,2,1,0:T(8,128)(2,1)S(1)}, u32[]{:S(2)}, u32[]{:S(2)}) collective-permute-start(bf16[4,2,64,256]{3,2,1,0:T(8,128)(2,1)S(1)} %collective-permute-done.7.refs_3_), channel_id=1, source_target_pairs={{4,0},{8,4},{12,8},{16,12},{20,16},{24,20},{28,24},{0,28},{5,1},{9... | collective-permute-start | bytes 786440 | tf_op jit(solution)/shard_map/ppermute | solution.py:253
  43.9 9.7 %collective-permute-start.10 = (bf16[4,2,64,256]{3,2,1,0:T(8,128)(2,1)S(1)}, bf16[4,2,64,256]{3,2,1,0:T(8,128)(2,1)S(1)}, u32[]{:S(2)}, u32[]{:S(2)}) collective-permute-start(bf16[4,2,64,256]{3,2,1,0:T(8,128)(2,1)S(1)} %collective-permute-done.9.refs_6_), channel_id=1, source_target_pairs={{0,4},{4,8},{8,12},{12,16},{16,20},{20,24},{24,28},{28,0},{1,5},{5... | collective-permute-start | bytes 786440 | tf_op jit(solution)/shard_map/ppermute | solution.py:251
  44.9 12.8 %collective-permute-start.3 = (bf16[4,2,64,256]{3,2,1,0:T(8,128)(2,1)S(1)}, bf16[4,2,64,256]{3,2,1,0:T(8,128)(2,1)}, u32[]{:S(2)}, u32[]{:S(2)}) collective-permute-start(bf16[4,2,64,256]{3,2,1,0:T(8,128)(2,1)S(1)} %collective-permute-done.2.refs_4_), channel_id=1, source_target_pairs={{0,4},{4,8},{8,12},{12,16},{16,20},{20,24},{24,28},{28,0},{1,5},{5... | collective-permute-start | bytes 786440 | tf_op jit(solution)/shard_map/ppermute | solution.py:251
  44.9 12.7 %collective-permute-start.6 = (bf16[4,2,64,256]{3,2,1,0:T(8,128)(2,1)S(1)}, bf16[4,2,64,256]{3,2,1,0:T(8,128)(2,1)}, u32[]{:S(2)}, u32[]{:S(2)}) collective-permute-start(bf16[4,2,64,256]{3,2,1,0:T(8,128)(2,1)S(1)} %collective-permute-done.5.refs_9_), channel_id=1, source_target_pairs={{4,0},{8,4},{12,8},{16,12},{20,16},{24,20},{28,24},{0,28},{5,1},{9... | collective-permute-start | bytes 786440 | tf_op jit(solution)/shard_map/ppermute | solution.py:253
  51.1 14.3 %collective-permute-start.11 = (bf16[4,2,64,256]{3,2,1,0:T(8,128)(2,1)S(1)}, bf16[4,2,64,256]{3,2,1,0:T(8,128)(2,1)S(1)}, u32[]{:S(2)}, u32[]{:S(2)}) collective-permute-start(bf16[4,2,64,256]{3,2,1,0:T(8,128)(2,1)S(1)} %collective-permute-done.8.refs_5_), channel_id=1, source_target_pairs={{4,0},{8,4},{12,8},{16,12},{20,16},{24,20},{28,24},{0,28},{5,1},{9... | collective-permute-start | bytes 786440 | tf_op jit(solution)/shard_map/ppermute | solution.py:253
  53.6 9.6 %collective-permute-start.13 = (bf16[4,2,64,256]{3,2,1,0:T(8,128)(2,1)S(1)}, bf16[4,2,64,256]{3,2,1,0:T(8,128)(2,1)S(1)}, u32[]{:S(2)}, u32[]{:S(2)}) collective-permute-start(bf16[4,2,64,256]{3,2,1,0:T(8,128)(2,1)S(1)} %collective-permute-done.10.refs_8_), channel_id=1, source_target_pairs={{0,4},{4,8},{8,12},{12,16},{16,20},{20,24},{24,28},{28,0},{1,5},{5... | collective-permute-start | bytes 786440 | tf_op jit(solution)/shard_map/ppermute | solution.py:251
  57.7 11.1 %collective-permute-start.12 = (bf16[4,2,64,256]{3,2,1,0:T(8,128)(2,1)}, bf16[4,2,64,256]{3,2,1,0:T(8,128)(2,1)S(1)}, u32[]{:S(2)}, u32[]{:S(2)}) collective-permute-start(bf16[4,2,64,256]{3,2,1,0:T(8,128)(2,1)} %collective-permute-done.3.refs_2_), channel_id=1, source_target_pairs={{0,4},{4,8},{8,12},{12,16},{16,20},{20,24},{24,28},{28,0},{1,5},{5... | collective-permute-start | bytes 786440 | tf_op jit(solution)/shard_map/ppermute | solution.py:251
  57.9 11.1 %collective-permute-start.14 = (bf16[4,2,64,256]{3,2,1,0:T(8,128)(2,1)}, bf16[4,2,64,256]{3,2,1,0:T(8,128)(2,1)S(1)}, u32[]{:S(2)}, u32[]{:S(2)}) collective-permute-start(bf16[4,2,64,256]{3,2,1,0:T(8,128)(2,1)} %collective-permute-done.6.refs_6_), channel_id=1, source_target_pairs={{4,0},{8,4},{12,8},{16,12},{20,16},{24,20},{28,24},{0,28},{5,1},{9... | collective-permute-start | bytes 786440 | tf_op jit(solution)/shard_map/ppermute | solution.py:253
  63.2 0.7 copy-start.4
  63.9 10.9 %collective-permute-start.18 = (bf16[4,2,64,256]{3,2,1,0:T(8,128)(2,1)S(1)}, bf16[4,2,64,256]{3,2,1,0:T(8,128)(2,1)S(1)}, u32[]{:S(2)}, u32[]{:S(2)}) collective-permute-start(bf16[4,2,64,256]{3,2,1,0:T(8,128)(2,1)S(1)} %get-tuple-element.22.refs_1_), channel_id=1, source_target_pairs={{4,0},{8,4},{12,8},{16,12},{20,16},{24,20},{28,24},{0,28},{5,1},{9... | collective-permute-start | bytes 786440 | tf_op jit(solution)/shard_map/ppermute | solution.py:253
  63.9 10.9 %collective-permute-start.15 = (bf16[4,2,64,256]{3,2,1,0:T(8,128)(2,1)S(1)}, bf16[4,2,64,256]{3,2,1,0:T(8,128)(2,1)S(1)}, u32[]{:S(2)}, u32[]{:S(2)}) collective-permute-start(bf16[4,2,64,256]{3,2,1,0:T(8,128)(2,1)S(1)} %get-tuple-element.21.refs_0_), channel_id=1, source_target_pairs={{0,4},{4,8},{8,12},{12,16},{16,20},{20,24},{24,28},{28,0},{1,5},{5... | collective-permute-start | bytes 786440 | tf_op jit(solution)/shard_map/ppermute | solution.py:251
  65.3 0.7 copy-start.2
  66.1 21.6 %collective-permute-start.21 = (bf16[4,2,64,256]{3,2,1,0:T(8,128)(2,1)S(1)}, bf16[4,2,64,256]{3,2,1,0:T(8,128)(2,1)S(1)}, u32[]{:S(2)}, u32[]{:S(2)}) collective-permute-start(bf16[4,2,64,256]{3,2,1,0:T(8,128)(2,1)S(1)} %get-tuple-element.21.refs_0_), channel_id=1, source_target_pairs={{4,0},{8,4},{12,8},{16,12},{20,16},{24,20},{28,24},{0,28},{5,1},{9... | collective-permute-start | bytes 786440 | tf_op jit(solution)/shard_map/ppermute | solution.py:253
  68.8 18.9 %collective-permute-start.23 = (bf16[4,2,64,256]{3,2,1,0:T(8,128)(2,1)S(1)}, bf16[4,2,64,256]{3,2,1,0:T(8,128)(2,1)S(1)}, u32[]{:S(2)}, u32[]{:S(2)}) collective-permute-start(bf16[4,2,64,256]{3,2,1,0:T(8,128)(2,1)S(1)} %get-tuple-element.22.refs_1_), channel_id=1, source_target_pairs={{0,4},{4,8},{8,12},{12,16},{16,20},{20,24},{24,28},{28,0},{1,5},{5... | collective-permute-start | bytes 786440 | tf_op jit(solution)/shard_map/ppermute | solution.py:251
  69.1 1.0 copy-start.3
  70.0 0.9 copy-start.5
  74.7 18.1 %copy-start.9 = (f32[8]{0:T(128)S(1)}, f32[8]{0:T(128)}, u32[]{:S(2)}) copy-start(f32[8]{0:T(128)} %constant.34.clone) | copy-start | bytes 100
  74.8 15.4 %collective-permute-start.16 = (bf16[4,2,64,256]{3,2,1,0:T(8,128)(2,1)S(1)}, bf16[4,2,64,256]{3,2,1,0:T(8,128)(2,1)}, u32[]{:S(2)}, u32[]{:S(2)}) collective-permute-start(bf16[4,2,64,256]{3,2,1,0:T(8,128)(2,1)S(1)} %collective-permute-done.15.refs_2_), channel_id=1, source_target_pairs={{0,4},{4,8},{8,12},{12,16},{16,20},{20,24},{24,28},{28,0},{1,5},{5... | collective-permute-start | bytes 786440 | tf_op jit(solution)/shard_map/ppermute | solution.py:251
  74.9 15.3 %collective-permute-start.19 = (bf16[4,2,64,256]{3,2,1,0:T(8,128)(2,1)S(1)}, bf16[4,2,64,256]{3,2,1,0:T(8,128)(2,1)}, u32[]{:S(2)}, u32[]{:S(2)}) collective-permute-start(bf16[4,2,64,256]{3,2,1,0:T(8,128)(2,1)S(1)} %collective-permute-done.18.refs_7_), channel_id=1, source_target_pairs={{4,0},{8,4},{12,8},{16,12},{20,16},{24,20},{28,24},{0,28},{5,1},{9... | collective-permute-start | bytes 786440 | tf_op jit(solution)/shard_map/ppermute | solution.py:253
  77.5 40.5 %all-to-all-start.1 = ((bf16[32,2,64,256]{3,2,1,0:T(8,128)(2,1)}), bf16[32,2,64,256]{3,2,1,0:T(8,128)(2,1)}, u32[]{:S(2)}, u32[]{:S(2)}) async-start(bf16[32,2,64,256]{3,2,1,0:T(8,128)(2,1)} %bitcast.4), calls=%async_computation.1 | async-start | bytes 4194304 | tf_op jit(solution)/shard_map/all_to_all | solution.py:269
  87.7 7.8 %collective-permute-start.22 = (bf16[4,2,64,256]{3,2,1,0:T(8,128)(2,1)S(1)}, bf16[4,2,64,256]{3,2,1,0:T(8,128)(2,1)}, u32[]{:S(2)}, u32[]{:S(2)}) collective-permute-start(bf16[4,2,64,256]{3,2,1,0:T(8,128)(2,1)S(1)} %collective-permute-done.21.refs_3_), channel_id=1, source_target_pairs={{4,0},{8,4},{12,8},{16,12},{20,16},{24,20},{28,24},{0,28},{5,1},{9... | collective-permute-start | bytes 786440 | tf_op jit(solution)/shard_map/ppermute | solution.py:253
  89.4 8.9 %collective-permute-start.24 = (bf16[4,2,64,256]{3,2,1,0:T(8,128)(2,1)S(1)}, bf16[4,2,64,256]{3,2,1,0:T(8,128)(2,1)}, u32[]{:S(2)}, u32[]{:S(2)}) collective-permute-start(bf16[4,2,64,256]{3,2,1,0:T(8,128)(2,1)S(1)} %collective-permute-done.23.refs_6_), channel_id=1, source_target_pairs={{0,4},{4,8},{8,12},{12,16},{16,20},{20,24},{24,28},{28,0},{1,5},{5... | collective-permute-start | bytes 786440 | tf_op jit(solution)/shard_map/ppermute | solution.py:251
  89.4 0.7 copy-start
  90.1 13.5 %collective-permute-start.17 = (bf16[4,2,64,256]{3,2,1,0:T(8,128)(2,1)}, bf16[4,2,64,256]{3,2,1,0:T(8,128)(2,1)S(1)}, u32[]{:S(2)}, u32[]{:S(2)}) collective-permute-start(bf16[4,2,64,256]{3,2,1,0:T(8,128)(2,1)} %collective-permute-done.16.refs_4_), channel_id=1, source_target_pairs={{0,4},{4,8},{8,12},{12,16},{16,20},{20,24},{24,28},{28,0},{1,5},{5... | collective-permute-start | bytes 786440 | tf_op jit(solution)/shard_map/ppermute | solution.py:251
  90.2 13.4 %collective-permute-start.20 = (bf16[4,2,64,256]{3,2,1,0:T(8,128)(2,1)}, bf16[4,2,64,256]{3,2,1,0:T(8,128)(2,1)S(1)}, u32[]{:S(2)}, u32[]{:S(2)}) collective-permute-start(bf16[4,2,64,256]{3,2,1,0:T(8,128)(2,1)} %collective-permute-done.19.refs_9_), channel_id=1, source_target_pairs={{4,0},{8,4},{12,8},{16,12},{20,16},{24,20},{28,24},{0,28},{5,1},{9... | collective-permute-start | bytes 786440 | tf_op jit(solution)/shard_map/ppermute | solution.py:253
  95.4 11.2 %collective-permute-start.25 = (bf16[4,2,64,256]{3,2,1,0:T(8,128)(2,1)}, bf16[4,2,64,256]{3,2,1,0:T(8,128)(2,1)S(1)}, u32[]{:S(2)}, u32[]{:S(2)}) collective-permute-start(bf16[4,2,64,256]{3,2,1,0:T(8,128)(2,1)} %collective-permute-done.22.refs_5_), channel_id=1, source_target_pairs={{4,0},{8,4},{12,8},{16,12},{20,16},{24,20},{28,24},{0,28},{5,1},{9... | collective-permute-start | bytes 786440 | tf_op jit(solution)/shard_map/ppermute | solution.py:253
  98.3 10.9 %collective-permute-start.27 = (bf16[4,2,64,256]{3,2,1,0:T(8,128)(2,1)}, bf16[4,2,64,256]{3,2,1,0:T(8,128)(2,1)S(1)}, u32[]{:S(2)}, u32[]{:S(2)}) collective-permute-start(bf16[4,2,64,256]{3,2,1,0:T(8,128)(2,1)} %collective-permute-done.24.refs_8_), channel_id=1, source_target_pairs={{0,4},{4,8},{8,12},{12,16},{16,20},{20,24},{24,28},{28,0},{1,5},{5... | collective-permute-start | bytes 786440 | tf_op jit(solution)/shard_map/ppermute | solution.py:251
  98.3 1.0 copy-start.1
  103.6 11.2 %collective-permute-start.26 = (bf16[4,2,64,256]{3,2,1,0:T(8,128)(2,1)S(1)}, bf16[4,2,64,256]{3,2,1,0:T(8,128)(2,1)S(1)}, u32[]{:S(2)}, u32[]{:S(2)}) collective-permute-start(bf16[4,2,64,256]{3,2,1,0:T(8,128)(2,1)S(1)} %collective-permute-done.17.refs_2_), channel_id=1, source_target_pairs={{0,4},{4,8},{8,12},{12,16},{16,20},{20,24},{24,28},{28,0},{1,5},{5... | collective-permute-start | bytes 786440 | tf_op jit(solution)/shard_map/ppermute | solution.py:251
  103.6 11.2 %collective-permute-start.28 = (bf16[4,2,64,256]{3,2,1,0:T(8,128)(2,1)S(1)}, bf16[4,2,64,256]{3,2,1,0:T(8,128)(2,1)S(1)}, u32[]{:S(2)}, u32[]{:S(2)}) collective-permute-start(bf16[4,2,64,256]{3,2,1,0:T(8,128)(2,1)S(1)} %collective-permute-done.20.refs_6_), channel_id=1, source_target_pairs={{4,0},{8,4},{12,8},{16,12},{20,16},{24,20},{28,24},{0,28},{5,1},{9... | collective-permute-start | bytes 786440 | tf_op jit(solution)/shard_map/ppermute | solution.py:253
  118.0 36.7 %copy-start.6 = (bf16[128,128]{1,0:T(8,128)(2,1)S(1)}, bf16[128,128]{1,0:T(8,128)(2,1)}, u32[]{:S(2)}) copy-start(bf16[128,128]{1,0:T(8,128)(2,1)} %constant.36.clone.t_ref) | copy-start | bytes 98308
